TPU v7x, 32 devices: a whole 2x2x4 slice. The times are simulated.
32 devices in a mesh: space: 4 (over z), band: 8 (over y, x, core).
Axes of the slice: x: 2, y: 2, z: 4, core: 2. Of those that a mesh axis runs over, the one named last changes fastest.
Arguments:
- wavefunctions: bfloat16 [256, 5120], P('band', 'space'), may hold values from -6 to 6
- cell_hamiltonian: bfloat16 [36, 216, 216], P('space'), may hold values from -1 to 2.25, as said below
- connectivity: int32 [36, 216], P('space'), may hold values from 0 to 1535, as said below
- face_nodes: int32 [1024], P('space'), may hold values from 0 to 1279, as said below
- basis_values: bfloat16 [216, 343], replicated, may hold values from -0.4375 to 0.4375
- quad_weights: float32 [36, 343], P('space'), may hold values from 0.1 to 1
- core_density: float32 [36, 343], P('space'), may hold values from 0.05 to 2
- occupancy: float32 [256], P('band'), may hold values from 0.1 to 1
- ritz_values: float32 [256], P('band'), may hold values from -1 to 6
Outputs:
- residual: float32 [256, 5120], P('band', 'space')
- potential: float32 [36, 343], P('space')
Inputs may be any that keep to these rules, and one draw needn't show every extreme that they name: `connectivity`: block s of 9 rows belongs to domain s and names each cell's 216 distinct nodes in that domain's extended numbering: values below 256 are its ghost columns, 256 + n is its owned node n. A domain's cells come in 1 layer of 9 rows; only the first layer names ghost columns and only the last layer names nodes listed in face_nodes. Every ghost column and every owned node is named by some cell. `face_nodes`: block s of 256 entries lists distinct owned nodes of domain s, in the order in which domain s + 1 numbers its ghost columns. `cell_hamiltonian`: each cell's matrix is symmetric.
All inputs are finite; a program needn't handle non-finite values.
Results may differ from a plain program's by a relative error of at most 0.0024.
Values may be sent and summed in bfloat16 or wider, within the bound.
No kernel may reach another device: no remote copies, remote signals or barrier semaphores. Data moves between devices by JAX's collectives and lax.ppermute only.
A program may use at most 64 MiB of HBM per device.

v0:
```python
import math

import jax
import jax.numpy as jnp
from jax import lax
from jax.sharding import PartitionSpec as P

spectrum_center = 5.0
spectrum_half = 5.5


def padded_2(block, sides, width):
    for axis, dim in sides:
        count = lax.axis_size(axis)
        forward = [(i, i + 1) for i in range(count - 1)]
        backward = [(target, source) for source, target in forward]
        low = lax.ppermute(
            lax.slice_in_dim(block, block.shape[dim] - width, None, axis=dim), axis, forward
        )
        high = lax.ppermute(lax.slice_in_dim(block, 0, width, axis=dim), axis, backward)
        block = jnp.concatenate([low, block, high], axis=dim)
    return block


def shifted(block, axis, distance):
    devices = range(lax.axis_size(axis))
    route = [(i - distance, i) for i in devices if i - distance in devices]
    return lax.ppermute(block, axis, route)


def exchange_correlation(density):
    radius = jnp.cbrt(0.75 / math.pi / density)
    exchange_part = -jnp.cbrt(3.0 / math.pi * density)
    shifted_radius = radius + 7.8
    correlation_part = -0.44 / shifted_radius - 0.44 * radius / (
        3.0 * shifted_radius * shifted_radius
    )
    return exchange_part + correlation_part


def shards(
    wavefunctions,
    cell_hamiltonian,
    connectivity,
    face_nodes,
    basis_values,
    quad_weights,
    core_density,
    occupancy,
    ritz_values,
):
    wave_count, owned_count = wavefunctions.shape
    face_count = face_nodes.shape[0]
    cell_count, node_count = connectivity.shape
    flat_links = connectivity.reshape(-1)
    band_total = wave_count * lax.axis_size("band")
    domain_mask = (lax.axis_index("space") > 0).astype(jnp.float32)

    def gather_cells(extended):
        return jnp.take(extended, flat_links, axis=1).reshape(wave_count, cell_count, node_count)

    def hamiltonian_part(cell_values):
        return jnp.einsum(
            "wcb,cab->wca", cell_values, cell_hamiltonian, preferred_element_type=jnp.float32
        )

    def scatter_cells(contributions):
        initial = jnp.zeros((wave_count, face_count + owned_count), jnp.float32)
        return initial.at[:, flat_links].add(contributions.reshape(wave_count, -1))

    starting = wavefunctions.astype(jnp.float32)

    def mirror_cells(values, ghost_values):
        return gather_cells(jnp.concatenate([ghost_values, values], axis=1).astype(jnp.bfloat16))

    def assemble_both(contributions):
        accumulated = scatter_cells(contributions)
        ghost_part = accumulated[:, :face_count]
        owned_part = accumulated[:, face_count:]
        outgoing = jnp.concatenate([ghost_part, owned_part[:, face_nodes]], axis=1)
        padded = padded_2(outgoing, (("space", 1),), face_count)
        owned_total = owned_part.at[:, face_nodes].add(padded[:, -face_count:])
        ghost_total = padded[:, :face_count] + ghost_part
        return (owned_total, ghost_total)

    start_ghost = shifted(wavefunctions[:, face_nodes], "space", 1).astype(jnp.float32)
    applied, applied_ghost = assemble_both(hamiltonian_part(mirror_cells(starting, start_ghost)))
    term_one = (applied - spectrum_center * starting) * (1.0 / spectrum_half)
    ghost_one = domain_mask * (
        (applied_ghost - spectrum_center * start_ghost) * (1.0 / spectrum_half)
    )
    applied, applied_ghost = assemble_both(hamiltonian_part(mirror_cells(term_one, ghost_one)))
    term_two = (applied - spectrum_center * term_one) * (2.0 / spectrum_half) - starting
    ghost_two = domain_mask * (
        (applied_ghost - spectrum_center * ghost_one) * (2.0 / spectrum_half) - start_ghost
    )
    applied, applied_ghost = assemble_both(hamiltonian_part(mirror_cells(term_two, ghost_two)))
    term_three = (applied - spectrum_center * term_two) * (2.0 / spectrum_half) - term_one
    ghost_three = domain_mask * (
        (applied_ghost - spectrum_center * ghost_two) * (2.0 / spectrum_half) - ghost_one
    )
    final_cells = mirror_cells(term_three, ghost_three)
    products = hamiltonian_part(final_cells)
    values_at = jnp.einsum(
        "wca,aq->wcq", final_cells, basis_values, preferred_element_type=jnp.float32
    )
    band_sum = jnp.sum(occupancy[:, None, None] * (values_at * values_at), axis=0)
    totals = lax.psum(band_sum, "band")
    potential = exchange_correlation(core_density + 2.0 / band_total * totals)
    weighted = (values_at * (quad_weights * potential)).astype(jnp.bfloat16)
    projected = jnp.einsum(
        "wcq,aq->wca", weighted, basis_values, preferred_element_type=jnp.float32
    )
    accumulated = scatter_cells(products + projected)
    returned = shifted(accumulated[:, :face_count], "space", -1)
    residual = (
        accumulated[:, face_count:].at[:, face_nodes].add(returned)
        - ritz_values[:, None] * term_three
    )
    return (residual, potential)


def solution(mesh):
    in_specs = (
        P("band", "space"),
        P("space", None, None),
        P("space", None),
        P("space"),
        P(),
        P("space", None),
        P("space", None),
        P("band"),
        P("band"),
    )
    out_specs = (P("band", "space"), P("space", None))
    return jax.shard_map(shards, mesh=mesh, in_specs=in_specs, out_specs=out_specs, check_vma=False)
```

profile of v0, /device:TPU:0, one launch (start us, length us, event | category | flops | bytes accessed | tf_op | source)
XLA Modules:
  0.0 164.7 jit_solution(13013059298248085005)
XLA Ops:
  0.6 0.8 compare_select_fusion.2
  1.4 1.1 copy.81
  2.5 0.9 gather_fusion
  3.5 4.9 %collective-permute-start = (bf16[32,256]{1,0:T(8,128)(2,1)S(1)}, bf16[32,256]{1,0:T(8,128)(2,1)S(1)}, u32[]{:S(2)}, u32[]{:S(2)}) collective-permute-start(bf16[32,256]{1,0:T(8,128)(2,1)S(1)} %bitcast.66), channel_id=1, source_target_pairs={{0,8},{8,16},{16,24},{1,9},{9,17},{17,25},{2,10},{10,18},{18,26},{... | collective-permute-start | bytes 49160 | tf_op jit(solution)/shard_map/ppermute | solution.py:28
  8.7 1.2 collective-permute-done
  10.1 6.3 %gather_fusion.4 = bf16[1944,32]{1,0:T(8,128)(2,1)S(1)} fusion(bf16[32,1536]{0,1:T(8,128)(2,1)S(1)} %pad_maximum_fusion, s32[2048]{0:T(1024)S(1)} %pad_clamp_fusion), kind=kCustom, calls=%fused_computation.clone | custom fusion | bytes 256608 | tf_op jit(solution)/shard_map/jit(_take)/gather | solution.py:60
  16.7 0.4 convolution_bitcast_fusion.3
  17.5 1.3 copy.87
  18.8 12.0 %scatter_custom_fusion = f32[32,1536]{0,1:T(8,128)S(1)} fusion(s32[1944]{0:T(1024)S(1)} %bitcast.67, f32[1944,32]{1,0:T(8,128)} %copy.87, f32[]{:T(128)} %constant.24.clone.1), kind=kCustom, calls=%fused_computation.43 | custom fusion | flops 62208 | bytes 197120 | tf_op jit(solution)/shard_map/scatter-add | solution.py:69
  31.0 1.3 collective-permute-start.2
  32.3 0.7 gather_fusion.1
  33.1 4.8 %collective-permute-start.1 = (f32[32,256]{1,0:T(8,128)S(1)}, f32[32,256]{1,0:T(8,128)S(1)}, u32[]{:S(2)}, u32[]{:S(2)}) collective-permute-start(f32[32,256]{1,0:T(8,128)S(1)} %bitcast.60), channel_id=1, source_target_pairs={{0,8},{8,16},{16,24},{1,9},{9,17},{17,25},{2,10},{10,18},{18,26},{... | collective-permute-start | bytes 98312 | tf_op jit(solution)/shard_map/ppermute | solution.py:17
  38.1 2.2 %scatter_fusion = f32[32,1280]{0,1:T(8,128)S(1)} fusion(f32[32,1280]{0,1:T(8,128)S(1)} %slice.48, s32[256]{0:T(256)S(1)} %compare_select_fusion.2, f32[256,32]{1,0:T(8,128)S(1)} %copy.90), kind=kCustom, calls=%fused_computation.9 | custom fusion | flops 8192 | bytes 99328 | tf_op jit(solution)/shard_map/scatter-add | solution.py:82
  40.3 0.6 fusion.26
  41.3 6.3 %gather_fusion.5 = bf16[1944,32]{1,0:T(8,128)(2,1)S(1)} fusion(bf16[32,1536]{0,1:T(8,128)(2,1)S(1)} %pad_maximum_fusion.1, s32[2048]{0:T(1024)S(1)} %pad_clamp_fusion), kind=kCustom, calls=%fused_computation.1.clone | custom fusion | bytes 256608 | tf_op jit(solution)/shard_map/jit(_take)/gather | solution.py:60
  47.9 0.4 convolution_bitcast_fusion.2
  48.7 1.3 copy.95
  50.0 12.0 %scatter_custom_fusion.2 = f32[32,1536]{0,1:T(8,128)S(1)} fusion(s32[1944]{0:T(1024)S(1)} %bitcast.68, f32[1944,32]{1,0:T(8,128)} %copy.95, f32[]{:T(128)} %constant.24.clone.1), kind=kCustom, calls=%fused_computation.41 | custom fusion | flops 62208 | bytes 197120 | tf_op jit(solution)/shard_map/scatter-add | solution.py:69
  62.2 1.3 collective-permute-start.4
  63.5 0.9 gather_fusion.2
  64.5 4.6 %collective-permute-start.3 = (f32[32,256]{1,0:T(8,128)S(1)}, f32[32,256]{1,0:T(8,128)S(1)}, u32[]{:S(2)}, u32[]{:S(2)}) collective-permute-start(f32[32,256]{1,0:T(8,128)S(1)} %bitcast.63), channel_id=1, source_target_pairs={{0,8},{8,16},{16,24},{1,9},{9,17},{17,25},{2,10},{10,18},{18,26},{... | collective-permute-start | bytes 98312 | tf_op jit(solution)/shard_map/ppermute | solution.py:17
  69.2 0.6 copy-done.19
  69.7 2.4 %scatter_fusion.1 = f32[32,1280]{0,1:T(8,128)S(1)} fusion(f32[32,1280]{0,1:T(8,128)S(1)} %slice.50, s32[256]{0:T(256)S(1)} %copy-done.19, f32[256,32]{1,0:T(8,128)S(1)} %copy.98), kind=kCustom, calls=%fused_computation.11 | custom fusion | flops 8192 | bytes 99328 | tf_op jit(solution)/shard_map/scatter-add | solution.py:82
  72.2 0.5 copy-done.15
  73.1 0.6 copy-done.12
  73.7 6.3 %gather_fusion.6 = bf16[1944,32]{1,0:T(8,128)(2,1)S(1)} fusion(bf16[32,1536]{0,1:T(8,128)(2,1)S(1)} %pad_maximum_fusion.2, s32[2048]{0:T(1024)S(1)} %copy-done.12), kind=kCustom, calls=%fused_computation.2.clone | custom fusion | bytes 256608 | tf_op jit(solution)/shard_map/jit(_take)/gather | solution.py:60
  81.2 1.3 copy.102
  82.5 12.0 %scatter_custom_fusion.4 = f32[32,1536]{0,1:T(8,128)S(1)} fusion(s32[1944]{0:T(1024)} %bitcast.69, f32[1944,32]{1,0:T(8,128)} %copy.102, f32[]{:T(128)} %constant.24.clone.1), kind=kCustom, calls=%fused_computation.39 | custom fusion | flops 62208 | bytes 197120 | tf_op jit(solution)/shard_map/scatter-add | solution.py:69
  94.5 0.8 copy.119
  95.4 1.3 collective-permute-start.6
  96.7 1.1 slice.52
  97.8 0.9 gather_fusion.3
  98.8 4.6 %collective-permute-start.5 = (f32[32,256]{1,0:T(8,128)S(1)}, f32[32,256]{1,0:T(8,128)S(1)}, u32[]{:S(2)}, u32[]{:S(2)}) collective-permute-start(f32[32,256]{1,0:T(8,128)S(1)} %bitcast.62), channel_id=1, source_target_pairs={{0,8},{8,16},{16,24},{1,9},{9,17},{17,25},{2,10},{10,18},{18,26},{... | collective-permute-start | bytes 98312 | tf_op jit(solution)/shard_map/ppermute | solution.py:17
  103.4 0.6 copy-done.20
  104.0 2.2 %scatter_fusion.2 = f32[32,1280]{0,1:T(8,128)S(1)} fusion(f32[32,1280]{0,1:T(8,128)S(1)} %slice.52, s32[256]{0:T(256)S(1)} %copy-done.20, f32[256,32]{1,0:T(8,128)S(1)} %copy.105), kind=kCustom, calls=%fused_computation.13 | custom fusion | flops 8192 | bytes 99328 | tf_op jit(solution)/shard_map/scatter-add | solution.py:82
  106.2 1.2 fusion.25
  107.7 1.1 pad_maximum_fusion.3
  108.8 6.3 %gather_fusion.7 = bf16[1944,32]{1,0:T(8,128)(2,1)S(1)} fusion(bf16[32,1536]{0,1:T(8,128)(2,1)S(1)} %pad_maximum_fusion.3, s32[2048]{0:T(1024)S(1)} %copy-done.13), kind=kCustom, calls=%fused_computation.3.clone | custom fusion | bytes 256608 | tf_op jit(solution)/shard_map/jit(_take)/gather | solution.py:60
  115.9 0.5 copy-done.3
  116.7 22.6 %psum.7 = f32[9,343]{1,0:T(8,128)S(1)} all-reduce(f32[9,343]{1,0:T(8,128)S(1)} %get-tuple-element.19), channel_id=1, replica_groups=mesh['space'=4,'band'=8] {'band'}, use_global_device_ids=true, to_apply=%region_7.9 | all-reduce | flops 3087 | bytes 24696 | tf_op jit(solution)/shard_map/psum | solution.py:108
  139.3 0.7 fusion.23
  140.6 1.3 copy.110
  141.9 12.0 %scatter_custom_fusion.6 = f32[32,1536]{0,1:T(8,128)S(1)} fusion(s32[1944]{0:T(1024)} %bitcast.70, f32[1944,32]{1,0:T(8,128)} %copy.110, f32[]{:T(128)} %constant.24.clone.1), kind=kCustom, calls=%fused_computation.37 | custom fusion | flops 62208 | bytes 197120 | tf_op jit(solution)/shard_map/scatter-add | solution.py:69
  154.0 1.3 collective-permute-start.7
  155.4 5.5 %collective-permute-done.7 = f32[32,256]{0,1:T(8,128)S(1)} collective-permute-done((f32[32,256]{0,1:T(8,128)S(1)}, f32[32,256]{0,1:T(8,128)S(1)}, u32[]{:S(2)}, u32[]{:S(2)}) %collective-permute-start.7) | collective-permute-done | bytes 32800 | tf_op jit(solution)/shard_map/ppermute | solution.py:28
  160.9 2.2 %scatter_custom_fusion.7 = f32[32,1280]{0,1:T(8,128)S(1)} fusion(f32[32,1280]{0,1:T(8,128)S(1)} %slice.54, s32[256]{0:T(256)S(1)} %copy-done.20, f32[32,256]{0,1:T(8,128)S(1)} %collective-permute-done.7), kind=kCustom, calls=%fused_computation.50 | custom fusion | flops 8192 | bytes 294912 | tf_op jit(solution)/shard_map/scatter-add | solution.py:117
  163.1 0.6 copy-done.26
  163.8 0.9 copy.111
  (105 shorter events, 6.7 us)
Async XLA Ops:
  0.6 16.1 %copy-start = (bf16[9,216,216]{2,1,0:T(8,128)(2,1)S(1)}, bf16[9,216,216]{2,1,0:T(8,128)(2,1)}, u32[]{:S(2)}) copy-start(bf16[9,216,216]{2,1,0:T(8,128)(2,1)} %param.12) | copy-start | bytes 2519428
  1.4 36.7 %copy-start.18 = (s32[256]{0:T(256)}, s32[256]{0:T(256)S(1)}, u32[]{:S(2)}) copy-start(s32[256]{0:T(256)S(1)} %compare_select_fusion.2) | copy-start | bytes 3076
  1.4 30.9 %copy-start.23 = (s32[1024]{0:T(1024)}, s32[1024]{0:T(1024)S(1)}, u32[]{:S(2)}) copy-start(s32[1024]{0:T(1024)S(1)} %pad_clamp_fusion.1) | copy-start | bytes 12292
  3.4 5.0 %copy-start.17 = (s32[9,216]{1,0:T(8,128)S(1)}, s32[9,216]{1,0:T(8,128)}, u32[]{:S(2)}) copy-start(s32[9,216]{1,0:T(8,128)} %param.13) | copy-start | bytes 23332
  3.5 6.4 %collective-permute-start = (bf16[32,256]{1,0:T(8,128)(2,1)S(1)}, bf16[32,256]{1,0:T(8,128)(2,1)S(1)}, u32[]{:S(2)}, u32[]{:S(2)}) collective-permute-start(bf16[32,256]{1,0:T(8,128)(2,1)S(1)} %bitcast.66), channel_id=1, source_target_pairs={{0,8},{8,16},{16,24},{1,9},{9,17},{17,25},{2,10},{10,18},{18,26},{... | collective-permute-start | bytes 49160 | tf_op jit(solution)/shard_map/ppermute | solution.py:28
  8.7 41.4 %copy-start.24 = (s32[1944,1]{0,1:T(1,128)}, s32[1944,1]{0,1:T(1,128)S(1)}, u32[]{:S(2)}) copy-start(s32[1944,1]{0,1:T(1,128)S(1)} %compare_select_fusion) | copy-start | bytes 23332
  8.7 32.6 %copy-start.11 = (s32[2048]{0:T(1024)}, s32[2048]{0:T(1024)S(1)}, u32[]{:S(2)}) copy-start(s32[2048]{0:T(1024)S(1)} %pad_clamp_fusion) | copy-start | bytes 24580
  9.8 30.5 %copy-start.8 = (bf16[32,256]{1,0:T(8,128)(2,1)}, bf16[32,256]{1,0:T(8,128)(2,1)S(1)}, u32[]{:S(2)}) copy-start(bf16[32,256]{1,0:T(8,128)(2,1)S(1)} %collective-permute-done) | copy-start | bytes 49156
  31.0 7.0 %collective-permute-start.2 = (f32[32,256]{1,0:T(8,128)S(1)}, f32[32,256]{1,0:T(8,128)S(1)}, u32[]{:S(2)}, u32[]{:S(2)}) collective-permute-start(f32[32,256]{1,0:T(8,128)S(1)} %copy.117), channel_id=1, source_target_pairs={{8,0},{16,8},{24,16},{9,1},{17,9},{25,17},{10,2},{18,10},{26,18},{... | collective-permute-start | bytes 98312 | tf_op jit(solution)/shard_map/ppermute | solution.py:20
  33.1 7.2 %collective-permute-start.1 = (f32[32,256]{1,0:T(8,128)S(1)}, f32[32,256]{1,0:T(8,128)S(1)}, u32[]{:S(2)}, u32[]{:S(2)}) collective-permute-start(f32[32,256]{1,0:T(8,128)S(1)} %bitcast.60), channel_id=1, source_target_pairs={{0,8},{8,16},{16,24},{1,9},{9,17},{17,25},{2,10},{10,18},{18,26},{... | collective-permute-start | bytes 98312 | tf_op jit(solution)/shard_map/ppermute | solution.py:17
  62.2 9.9 %copy-start.4 = (f32[32,256]{1,0:T(8,128)}, f32[32,256]{1,0:T(8,128)S(1)}, u32[]{:S(2)}) copy-start(f32[32,256]{1,0:T(8,128)S(1)} %copy.118) | copy-start | bytes 98308
  62.2 6.8 %collective-permute-start.4 = (f32[32,256]{1,0:T(8,128)S(1)}, f32[32,256]{1,0:T(8,128)S(1)}, u32[]{:S(2)}, u32[]{:S(2)}) collective-permute-start(f32[32,256]{1,0:T(8,128)S(1)} %copy.118), channel_id=1, source_target_pairs={{8,0},{16,8},{24,16},{9,1},{17,9},{25,17},{10,2},{18,10},{26,18},{... | collective-permute-start | bytes 98312 | tf_op jit(solution)/shard_map/ppermute | solution.py:20
  64.5 7.6 %collective-permute-start.3 = (f32[32,256]{1,0:T(8,128)S(1)}, f32[32,256]{1,0:T(8,128)S(1)}, u32[]{:S(2)}, u32[]{:S(2)}) collective-permute-start(f32[32,256]{1,0:T(8,128)S(1)} %bitcast.63), channel_id=1, source_target_pairs={{0,8},{8,16},{16,24},{1,9},{9,17},{17,25},{2,10},{10,18},{18,26},{... | collective-permute-start | bytes 98312 | tf_op jit(solution)/shard_map/ppermute | solution.py:17
  69.0 0.7 copy-start.19
  69.7 2.4 %copy-start.6 = (f32[32,256]{1,0:T(8,128)S(1)}, f32[32,256]{1,0:T(8,128)}, u32[]{:S(2)}) copy-start(f32[32,256]{1,0:T(8,128)} %get-tuple-element.18) | copy-start | bytes 98308
  69.7 2.4 %copy-start.9 = (bf16[32,256]{1,0:T(8,128)(2,1)S(1)}, bf16[32,256]{1,0:T(8,128)(2,1)}, u32[]{:S(2)}) copy-start(bf16[32,256]{1,0:T(8,128)(2,1)} %copy-done.8) | copy-start | bytes 49156
  72.1 0.6 copy-start.15
  73.0 0.7 copy-start.12
  94.5 0.9 copy-start.1
  95.4 7.9 %collective-permute-start.6 = (f32[32,256]{1,0:T(8,128)}, f32[32,256]{1,0:T(8,128)S(1)}, u32[]{:S(2)}, u32[]{:S(2)}) collective-permute-start(f32[32,256]{1,0:T(8,128)} %copy.119), channel_id=1, source_target_pairs={{8,0},{16,8},{24,16},{9,1},{17,9},{25,17},{10,2},{18,10},{26,18},{... | collective-permute-start | bytes 98312 | tf_op jit(solution)/shard_map/ppermute | solution.py:20
  98.8 8.7 %collective-permute-start.5 = (f32[32,256]{1,0:T(8,128)S(1)}, f32[32,256]{1,0:T(8,128)S(1)}, u32[]{:S(2)}, u32[]{:S(2)}) collective-permute-start(f32[32,256]{1,0:T(8,128)S(1)} %bitcast.62), channel_id=1, source_target_pairs={{0,8},{8,16},{16,24},{1,9},{9,17},{17,25},{2,10},{10,18},{18,26},{... | collective-permute-start | bytes 98312 | tf_op jit(solution)/shard_map/ppermute | solution.py:17
  103.3 0.7 copy-start.20
  106.2 1.3 copy-start.5
  106.2 1.3 copy-start.7
  106.2 1.3 copy-start.10
  106.2 1.3 copy-start.14
  106.2 1.3 copy-start.16
  107.7 1.1 copy-start.13
  115.4 0.9 copy-start.3
  115.4 0.9 copy-start.25
  116.7 22.6 %copy-start.21 = (f32[9,343]{1,0:T(8,128)S(1)}, f32[9,343]{1,0:T(8,128)}, u32[]{:S(2)}) copy-start(f32[9,343]{1,0:T(8,128)} %param.16) | copy-start | bytes 37048
  116.7 22.6 %copy-start.22 = (f32[9,343]{1,0:T(8,128)S(1)}, f32[9,343]{1,0:T(8,128)}, u32[]{:S(2)}) copy-start(f32[9,343]{1,0:T(8,128)} %param.17) | copy-start | bytes 37048
  154.0 6.9 %collective-permute-start.7 = (f32[32,256]{0,1:T(8,128)S(1)}, f32[32,256]{0,1:T(8,128)S(1)}, u32[]{:S(2)}, u32[]{:S(2)}) collective-permute-start(f32[32,256]{0,1:T(8,128)S(1)} %slice.55), channel_id=1, source_target_pairs={{8,0},{16,8},{24,16},{9,1},{17,9},{25,17},{10,2},{18,10},{26,18},{... | collective-permute-start | bytes 98312 | tf_op jit(solution)/shard_map/ppermute | solution.py:28
  155.4 7.7 %copy-start.2 = (f32[32,1280]{0,1:T(8,128)S(1)}, f32[32,1280]{0,1:T(8,128)}, u32[]{:S(2)}) copy-start(f32[32,1280]{0,1:T(8,128)} %get-tuple-element.16) | copy-start | bytes 491524
  163.1 0.7 copy-start.26
where the time goes:
time: 165 us
  other arithmetic  63.5 us (38%)
  local copies, waits for them, and re-layouts  44.2 us (27%)
  starting transfers between devices  24 us (15%)
  blocking collectives  22.6 us (14%)
  waiting for transfers between devices  6.67 us (4%)
  matrix products  2.32 us (1%)
    scatter-add x4, other arithmetic, scatter_cells(): return initial.at[:, flat_links].add(contributions.reshape(wave_count, -1))  48.2 us
    gather x4, local copies, waits for them, and re-layouts, gather_cells(): jnp.take(extended, flat_links, axis=1)  25.2 us
    psum x1, blocking collectives, shards(): totals = lax.psum(band_sum, 'band')  22.6 us
    ppermute x3, starting transfers between devices, padded_2(): lax.ppermute(lax.slice_in_dim(block, block.shape[dim] - width, None, axis...  13.9 us
    scatter-add x3, other arithmetic, assemble_both(): owned_total = owned_part.at[:, face_nodes].add(padded[:, -face_count:])  6.73 us
    ppermute x2, waiting for transfers between devices, shifted(): return lax.ppermute(block, axis, route)  6.66 us
    unnamed x59, local copies, waits for them, and re-layouts  6.46 us
    ppermute x2, starting transfers between devices, shifted(): return lax.ppermute(block, axis, route)  6.23 us
  transfers between devices with their start and end apart: 8, of which 2 were waited for; matrix products, arithmetic and copies ran while one was open for 7% of the time, Pallas kernels for 0%

commit v1 on v0

v1 whole, which is shorter than its diff:
```python
import functools
import math

import jax
import jax.numpy as jnp
from jax import lax
from jax.experimental import pallas as pl
from jax.experimental.pallas import tpu as pltpu
from jax.sharding import PartitionSpec as P

spectrum_center = 5.0
spectrum_half = 5.5

VMEM = pl.BlockSpec(memory_space=pltpu.VMEM)
SMEM = pl.BlockSpec(memory_space=pltpu.SMEM)
bf16 = jnp.bfloat16
f32 = jnp.float32


def dot(left, right):
    return jnp.dot(left, right, preferred_element_type=f32)


def dot_rows(left, right):
    return lax.dot_general(left, right, (((1,), (1,)), ((), ())), preferred_element_type=f32)


def halves(x):
    high = x.astype(bf16)
    low = (x - high.astype(f32)).astype(bf16)
    return jnp.concatenate([high, low], axis=0)


def joined(x):
    rows = x.shape[0] // 2
    return x[:rows] + x[rows:]


def column(row):
    n = row.shape[1]
    eye = lax.broadcasted_iota(jnp.int32, (n, n), 0) == lax.broadcasted_iota(jnp.int32, (n, n), 1)
    return jnp.sum(jnp.where(eye, row, jnp.zeros_like(row)), axis=1, keepdims=True)


def one_hot(hit):
    return jnp.where(hit, 1.0, 0.0).astype(bf16)


def call(kernel, outs, *args, flops=1 << 28, smem=0):
    return pl.pallas_call(
        kernel,
        out_shape=[pltpu.VMEM(shape, dtype) for shape, dtype in outs],
        in_specs=[SMEM] * smem + [VMEM] * (len(args) - smem),
        out_specs=[VMEM] * len(outs),
        compiler_params=pltpu.CompilerParams(vmem_limit_bytes=20 << 20),
        cost_estimate=pl.CostEstimate(flops=flops, bytes_accessed=1 << 20, transcendentals=0),
    )(*args)


def pick_kernel(w_ref, face_ref, table_ref, out_ref):
    owned = w_ref.shape[1]
    count = face_ref.shape[1]
    table = one_hot(lax.broadcasted_iota(jnp.int32, (owned, count), 0) == face_ref[...])
    table_ref[...] = table
    out_ref[...] = dot(w_ref[...], table).astype(bf16)


def tables_kernel(
    w_ref, links_ref, face_ref, face_table_ref, own_ref, edge_ref, inner_ref, values_ref, state_ref
):
    owned, slots = own_ref.shape
    count = face_ref.shape[1]
    links = jnp.broadcast_to(links_ref[...], (8, slots))
    strip = 16

    def own_rows(i, carry):
        start = pl.multiple_of(i * strip, strip)
        index = lax.broadcasted_iota(jnp.int32, (strip, slots), 0) + (start + count)
        own_ref[pl.ds(start, strip), :] = one_hot(index == jnp.concatenate([links, links], axis=0))
        return carry

    lax.fori_loop(0, owned // strip, own_rows, 0, unroll=4)
    ghost_index = lax.broadcasted_iota(jnp.int32, (count, 1), 0)
    face_index = column(face_ref[...].astype(f32)).astype(jnp.int32) + count
    for part, index in enumerate((ghost_index, face_index)):
        for start in range(0, count, strip):
            rows = jnp.broadcast_to(index[start : start + strip], (strip, slots))
            edge_ref[pl.ds(part * count + start, strip), :] = one_hot(
                rows == jnp.concatenate([links, links], axis=0)
            )
    named = dot_rows(jnp.ones((8, count), bf16), face_table_ref[...])
    inner = 1.0 - named
    inner_ref[...] = inner
    w = w_ref[...]
    values_ref[...] = dot(w, own_ref[...]).astype(bf16)
    state_ref[...] = w.astype(f32) * inner[:1]


def cell_products(values, matrix_ref, out_ref):
    cells, nodes, _ = matrix_ref.shape
    pitch = values.shape[1] // cells
    out_ref[...] = jnp.zeros_like(out_ref)
    for cell in range(cells):
        start = cell * pitch
        out_ref[:, start : start + nodes] = dot(values[:, start : start + nodes], matrix_ref[cell])


def send_sums(values, matrix_ref, edge_ref, parts_ref, ghost_ref, face_ref, product_ref):
    cell_products(values, matrix_ref, product_ref)
    parts = halves(product_ref[...])
    parts_ref[...] = parts
    sums = joined(dot_rows(parts, edge_ref[...]))
    count = ghost_ref.shape[1]
    ghost_ref[...] = sums[:, :count]
    face_ref[...] = sums[:, count:]


def first_kernel(
    flags_ref, values_ref, got_ref, matrix_ref, edge_ref,
    parts_ref, ghost_ref, face_ref, state_ref, product_ref,
):
    got = got_ref[...].astype(f32)
    got = jnp.where(flags_ref[0] > 0, got, jnp.zeros_like(got))
    state_ref[...] = got
    count = got.shape[1]
    values = values_ref[...].astype(f32) + dot(got.astype(bf16), edge_ref[:count, :])
    send_sums(values.astype(bf16), matrix_ref, edge_ref, parts_ref, ghost_ref, face_ref, product_ref)


def advance(scale, applied, state, before):
    new = (applied - spectrum_center * state) * scale
    return new if before is None else new - before


def edge_step(scale, flags_ref, got_ghost, got_face, sum_ghost, sum_face, ghost, face, before):
    keep_ghost, keep_face = flags_ref[0] > 0, flags_ref[1] > 0
    arrived = got_face[...]
    applied_face = sum_face[...] + jnp.where(keep_face, arrived, jnp.zeros_like(arrived))
    new_face = advance(scale, applied_face, face[...], before and before[1][...])
    new_ghost = advance(
        scale, sum_ghost[...] + got_ghost[...], ghost[...], before and before[0][...]
    )
    new_ghost = jnp.where(keep_ghost, new_ghost, jnp.zeros_like(new_ghost))
    return new_ghost, new_face


def next_values(new_ghost, new_face, values_ref, edge_ref):
    edge = jnp.concatenate([new_ghost.astype(bf16), new_face.astype(bf16)], axis=1)
    return (values_ref[...].astype(f32) + dot(edge, edge_ref[...])).astype(bf16)


def edge_kernel(scale, with_before, flags_ref, got_ghost, got_face, sum_ghost, sum_face, ghost, face, *rest):
    before, rest = (rest[:2], rest[2:]) if with_before else (None, rest)
    values_ref, matrix_ref, edge_ref, parts_ref, out_ghost, out_face, new_ghost, new_face, product_ref = rest
    ghost_value, face_value = edge_step(
        scale, flags_ref, got_ghost, got_face, sum_ghost, sum_face, ghost, face, before
    )
    new_ghost[...] = ghost_value
    new_face[...] = face_value
    values = next_values(ghost_value, face_value, values_ref, edge_ref)
    send_sums(values, matrix_ref, edge_ref, parts_ref, out_ghost, out_face, product_ref)


def inner_kernel(scale, with_before, parts_ref, state_ref, *rest):
    before = rest[0][...] if with_before else None
    own_ref, inner_ref, new_ref, values_ref = rest[1:] if with_before else rest
    applied = joined(dot_rows(parts_ref[...], own_ref[...]))
    new = advance(scale, applied, state_ref[...], before) * inner_ref[:1]
    new_ref[...] = new
    values_ref[...] = dot(new.astype(bf16), own_ref[...]).astype(bf16)


def density_kernel(
    flags_ref, got_ghost, got_face, sum_ghost, sum_face, ghost, face, before_ghost, before_face,
    values_ref, edge_ref, basis_ref, occupancy_ref,
    new_face, final_ref, at_ref, band_ref, *, scale, cells,
):
    ghost_value, face_value = edge_step(
        scale, flags_ref, got_ghost, got_face, sum_ghost, sum_face, ghost, face,
        (before_ghost, before_face),
    )
    new_face[...] = face_value
    values = next_values(ghost_value, face_value, values_ref, edge_ref)
    final_ref[...] = values
    nodes = basis_ref.shape[0]
    waves, slots = values.shape
    pitch = slots // cells
    stacked = jnp.concatenate(
        [values[:, cell * pitch : (cell + 1) * pitch] for cell in range(cells)], axis=0
    )
    at = dot(stacked[:, :nodes], basis_ref[...])
    at_ref[...] = at
    weights = column(occupancy_ref[...])
    for cell in range(cells):
        block = at[cell * waves : (cell + 1) * waves]
        band_ref[cell : cell + 1, :] = jnp.sum(weights * (block * block), axis=0, keepdims=True)


def products_kernel(values_ref, matrix_ref, product_ref):
    cell_products(values_ref[...], matrix_ref, product_ref)


def cube_root(x):
    return jnp.exp(jnp.log(x) * (1.0 / 3.0))


def exchange_correlation(density):
    radius = cube_root(0.75 / math.pi / density)
    exchange_part = -cube_root(3.0 / math.pi * density)
    shifted_radius = radius + 7.8
    correlation_part = -0.44 / shifted_radius - 0.44 * radius / (
        3.0 * shifted_radius * shifted_radius
    )
    return exchange_part + correlation_part


def potential_kernel(total_ref, *rest, factor):
    more, (core_ref, quad_ref, at_ref, basis_ref, product_ref, edge_ref,
           potential_ref, parts_ref, ghost_ref, term_ref) = rest[:-10], rest[-10:]
    total = total_ref[...]
    if more:
        total = (total + more[0][...]) + (more[1][...] + more[2][...])
    potential = exchange_correlation(core_ref[...] + factor * total)
    potential_ref[...] = potential
    scaled = quad_ref[...] * potential
    cells = scaled.shape[0]
    waves, slots = product_ref.shape
    pitch = slots // cells
    nodes = basis_ref.shape[0]
    weighted = jnp.concatenate(
        [
            (at_ref[cell * waves : (cell + 1) * waves, :] * scaled[cell : cell + 1]).astype(bf16)
            for cell in range(cells)
        ],
        axis=0,
    )
    projected = dot_rows(weighted, basis_ref[...])
    term_ref[...] = product_ref[...]
    for cell in range(cells):
        start = cell * pitch
        term_ref[:, start : start + nodes] += projected[cell * waves : (cell + 1) * waves]
    parts = halves(term_ref[...])
    parts_ref[...] = parts
    count = ghost_ref.shape[1]
    ghost_ref[...] = joined(dot_rows(parts, edge_ref[:count, :]))


def residual_kernel(parts_ref, state_ref, face_ref, ritz_ref, own_ref, face_table_ref, out_ref):
    ritz = column(ritz_ref[...])
    faces = joined(dot_rows(halves(ritz * face_ref[...]), face_table_ref[...]))
    out_ref[...] = (
        joined(dot_rows(parts_ref[...], own_ref[...])) - ritz * state_ref[...] - faces
    )


def finish_kernel(flags_ref, got_ref, partial_ref, face_table_ref, out_ref):
    got = got_ref[...]
    got = jnp.where(flags_ref[1] > 0, got, jnp.zeros_like(got))
    out_ref[...] = partial_ref[...] + joined(dot_rows(halves(got), face_table_ref[...]))


def around(x, axis, distance):
    count = lax.axis_size(axis)
    return lax.ppermute(x, axis, [(i, (i + distance) % count) for i in range(count)])


def swapped(x, axis, mask):
    return lax.ppermute(x, axis, [(i, i ^ mask) for i in range(lax.axis_size(axis))])


def band_parts(x, axis):
    count = lax.axis_size(axis)
    if count & (count - 1):
        return [lax.psum(x, axis)]
    bit = 1
    if count > 1:
        x = x + swapped(x, axis, bit)
        bit = 2
    parts = [x]
    while bit < count:
        x = parts[0] if len(parts) == 1 else (parts[0] + parts[1]) + (parts[2] + parts[3])
        if 2 * bit < count:
            parts = [x] + [swapped(x, axis, mask) for mask in (bit, 2 * bit, 3 * bit)]
            bit *= 4
        else:
            parts = [x + swapped(x, axis, bit)]
            bit *= 2
    return parts


def shards(
    wavefunctions,
    cell_hamiltonian,
    connectivity,
    face_nodes,
    basis_values,
    quad_weights,
    core_density,
    occupancy,
    ritz_values,
):
    waves, owned = wavefunctions.shape
    count = face_nodes.shape[0]
    cells, nodes = connectivity.shape
    points = basis_values.shape[1]
    pitch = -(-nodes // 128) * 128
    slots = cells * pitch
    band_total = waves * lax.axis_size("band")
    domain = lax.axis_index("space")
    flags = jnp.stack([domain > 0, domain < lax.axis_size("space") - 1]).astype(jnp.int32)
    links = jnp.pad(connectivity, ((0, 0), (0, pitch - nodes)), constant_values=-1)
    links = links.reshape(1, slots)
    faces = face_nodes.reshape(1, count)

    edge_out = [((waves, count), f32)] * 2
    parts_out = ((2 * waves, slots), bf16)
    product_out = ((waves, slots), f32)
    values_out = ((waves, slots), bf16)
    state_out = ((waves, owned), f32)

    face_table, start_face = call(
        pick_kernel, [((owned, count), bf16), ((waves, count), bf16)], wavefunctions, faces
    )
    start_ghost = around(start_face, "space", 1)
    own, edge, inner, values, state = call(
        tables_kernel,
        [((owned, slots), bf16), ((2 * count, slots), bf16), ((8, owned), f32), values_out, state_out],
        wavefunctions, links, faces, face_table,
    )
    parts, sum_ghost, sum_face, ghost, _ = call(
        first_kernel,
        [parts_out, *edge_out, edge_out[0], product_out],
        flags, values, start_ghost, cell_hamiltonian, edge, smem=1,
    )
    face = start_face.astype(f32)
    before_edge, before_state = (), ()
    scale = 1.0 / spectrum_half
    for step in range(3):
        got_ghost = around(sum_face, "space", 1)
        got_face = around(sum_ghost, "space", -1)
        new_state, values = call(
            functools.partial(inner_kernel, scale, step > 0),
            [state_out, values_out],
            parts, state, *before_state, own, inner,
        )
        received = (flags, got_ghost, got_face, sum_ghost, sum_face, ghost, face, *before_edge)
        if step < 2:
            parts, sum_ghost, sum_face, new_ghost, new_face, _ = call(
                functools.partial(edge_kernel, scale, step > 0),
                [parts_out, *edge_out, *edge_out, product_out],
                *received, values, cell_hamiltonian, edge, smem=1,
            )
            before_edge, ghost, face = (ghost, face), new_ghost, new_face
        else:
            face, final, at, band = call(
                functools.partial(density_kernel, scale=scale, cells=cells),
                [edge_out[0], values_out, ((cells * waves, points), f32), ((cells, points), f32)],
                *received, values, edge, basis_values, occupancy.reshape(1, waves), smem=1,
            )
        before_state, state = (state,), new_state
        scale = 2.0 / spectrum_half
    (products,) = call(products_kernel, [product_out], final, cell_hamiltonian)
    totals = band_parts(band, "band")
    potential, parts, sum_ghost, _ = call(
        functools.partial(potential_kernel, factor=2.0 / band_total),
        [((cells, points), f32), parts_out, edge_out[0], product_out],
        *totals, core_density, quad_weights, at, basis_values, products, edge,
    )
    returned = around(sum_ghost, "space", -1)
    (partial,) = call(
        residual_kernel, [state_out],
        parts, state, face, ritz_values.reshape(1, waves), own, face_table,
    )
    (residual,) = call(finish_kernel, [state_out], flags, returned, partial, face_table, smem=1)
    return (residual, potential)


def solution(mesh):
    in_specs = (
        P("band", "space"),
        P("space", None, None),
        P("space", None),
        P("space"),
        P(),
        P("space", None),
        P("space", None),
        P("band"),
        P("band"),
    )
    out_specs = (P("band", "space"), P("space", None))
    return jax.shard_map(shards, mesh=mesh, in_specs=in_specs, out_specs=out_specs, check_vma=False)
```

time: 165 us -> 57.6 us (0.35)
  other arithmetic: 63.5 us -> 0.09 us
  local copies, waits for them, and re-layouts: 44.2 us -> 6.37 us
  Pallas kernels: 0 us -> 25.2 us
  blocking collectives: 22.6 us -> 0 us
  starting transfers between devices: 24 us -> 20.6 us
  waiting for transfers between devices: 6.67 us -> 4.2 us
  matrix products: 2.32 us -> 0 us
    scatter-add x8 -> x0, other arithmetic: 57.1 us -> none  [the longest x4 48.2 us: scatter_cells(): return initial.at[:, flat_links].add(contributions.reshape(wave_count, -1))]
    gather x12 -> x0, local copies, waits for them, and re-layouts: 28.7 us -> none  [the longest x4 25.2 us: gather_cells(): jnp.take(extended, flat_links, axis=1)]
    pallas_call x0 -> x13, Pallas kernels: none -> 25.2 us  [call(): pl.pallas_call(kernel, out_shape=[pltpu.VMEM(shape, dtype) for shape, dty...]
    psum x1 -> x0, blocking collectives: 22.6 us -> none  [shards(): totals = lax.psum(band_sum, 'band')]
    reshape x10 -> x0, local copies, waits for them, and re-layouts: 6.17 us -> none  [the longest x8 6 us: scatter_cells(): return initial.at[:, flat_links].add(contributions.reshape(wave_count, -1))]
    ppermute x8 -> x12, starting transfers between devices: 24 us -> 20.6 us  [the longest x8 17.1 us: around(): lax.ppermute(x, axis, [(i, (i + distance) % count) for i in range(count)])]
    ppermute x8 -> x12, waiting for transfers between devices: 6.67 us -> 4.2 us  [the longest x4 4.17 us: swapped(): lax.ppermute(x, axis, [(i, i ^ mask) for i in range(lax.axis_size(axis))])]
    dot_general x6 -> x0, matrix products: 2.32 us -> none  [the longest x4 1.72 us: hamiltonian_part(): jnp.einsum('wcb,cab->wca', cell_values, cell_hamiltonian, preferred_eleme...]
  transfers between devices with their start and end apart: 8 -> 12, of which waited for: 2 -> 4; matrix products, arithmetic and copies ran while one was open for 7% -> 2% of each run, Pallas kernels for 0% -> 25%
where the time goes in v1:
time: 57.6 us; the launch traced here: 57.3 us
  Pallas kernels  25.2 us (44%)
  starting transfers between devices  20.6 us (36%)
  local copies, waits for them, and re-layouts  6.37 us (11%)
  waiting for transfers between devices  4.2 us (7%)
  between operations  0.82 us (1%)
    pallas_call x13, Pallas kernels, call(): pl.pallas_call(kernel, out_shape=[pltpu.VMEM(shape, dtype) for shape, dty...  25.2 us
    ppermute x8, starting transfers between devices, around(): lax.ppermute(x, axis, [(i, (i + distance) % count) for i in range(count)])  17.1 us
    unnamed x26, local copies, waits for them, and re-layouts  6.37 us
    ppermute x4, waiting for transfers between devices, swapped(): lax.ppermute(x, axis, [(i, i ^ mask) for i in range(lax.axis_size(axis))])  4.17 us
    ppermute x4, starting transfers between devices, swapped(): lax.ppermute(x, axis, [(i, i ^ mask) for i in range(lax.axis_size(axis))])  3.56 us
  transfers between devices with their start and end apart: 12, of which 4 were waited for; matrix products, arithmetic and copies ran while one was open for 2% of the time, Pallas kernels for 25%

profile of v1, /device:TPU:0, one launch (start us, length us, event | category | flops | bytes accessed | tf_op | source)
XLA Modules:
  0.0 57.3 jit_solution(12092012171973445251)
XLA Ops:
  0.6 0.0 copy-start.7
  0.6 0.9 %copy-done.7 = bf16[32,1280]{1,0:T(8,128)(2,1)S(1)} copy-done((bf16[32,1280]{1,0:T(8,128)(2,1)S(1)}, bf16[32,1280]{1,0:T(8,128)(2,1)}, u32[]{:S(2)}) %copy-start.7) | copy-done | bytes 81944
  1.5 0.7 %copy-done.9 = s32[256]{0:T(256)S(1)} copy-done((s32[256]{0:T(256)S(1)}, s32[256]{0:T(256)}, u32[]{:S(2)}) %copy-start.9) | copy-done | bytes 1048
  2.2 0.2 shard_map.104
  2.4 3.1 %collective-permute-start = (bf16[32,256]{1,0:T(8,128)(2,1)S(1)}, bf16[32,256]{1,0:T(8,128)(2,1)S(1)}, u32[]{:S(2)}, u32[]{:S(2)}) collective-permute-start(bf16[32,256]{1,0:T(8,128)(2,1)S(1)} %get-tuple-element.38), channel_id=1, source_target_pairs={{0,8},{8,16},{16,24},{24,0},{1,9},{9,17},{17,25},{25,1},{2,10},{10... | collective-permute-start | bytes 49160 | tf_op jit(solution)/shard_map/ppermute | solution.py:264
  5.5 0.7 %pad_bitcast_fusion = s32[1,1,9,256]{3,2,1,0:T(8,128)S(1)} fusion(s32[9,216]{1,0:T(8,128)} %param.11), kind=kLoop, calls=%fused_computation | loop fusion | bytes 16992
  6.3 0.1 add_convert_fusion.flags_ref
  6.3 0.9 %copy-done.8 = bf16[32,1280]{1,0:T(8,128)(2,1)S(1)} copy-done((bf16[32,1280]{1,0:T(8,128)(2,1)S(1)}, bf16[32,1280]{1,0:T(8,128)(2,1)}, u32[]{:S(2)}) %copy-start.8) | copy-done | bytes 81944
  7.2 0.7 %copy-done.10 = s32[256]{0:T(256)S(1)} copy-done((s32[256]{0:T(256)S(1)}, s32[256]{0:T(256)}, u32[]{:S(2)}) %copy-start.10) | copy-done | bytes 1048
  7.9 2.8 %shard_map.105 = (bf16[1280,2304]{1,0:T(8,128)(2,1)S(1)}, bf16[512,2304]{1,0:T(8,128)(2,1)S(1)}, f32[8,1280]{1,0:T(8,128)S(1)}, bf16[32,2304]{1,0:T(8,128)(2,1)S(1)}, f32[32,1280]{1,0:T(8,128)S(1)}) custom-call(bf16[32,1280]{1,0:T(8,128)(2,1)S(1)} %copy-done.8, s32[1,2304]{1,0:T(1,128)S(1)} %bitcast.9, s32[1,256]{1,0:T(1,128)S(1)} %bitcast.13, ...), custom_call_target="tpu_custom_call" | custom-call | flops 268435456 | bytes 1048576 | tf_op jit(solution)/shard_map/pallas_call | solution.py:50
  10.7 0.0 collective-permute-done.got_ref
  10.7 0.0 copy-start
  10.7 1.2 %copy-done = bf16[9,216,216]{2,1,0:T(8,128)(2,1)S(1)} copy-done((bf16[9,216,216]{2,1,0:T(8,128)(2,1)S(1)}, bf16[9,216,216]{2,1,0:T(8,128)(2,1)}, u32[]{:S(2)}) %copy-start) | copy-done | bytes 839832
  11.9 2.3 %shard_map.106 = (bf16[64,2304]{1,0:T(8,128)(2,1)S(1)}, f32[32,256]{1,0:T(8,128)S(1)}, f32[32,256]{1,0:T(8,128)S(1)}, f32[32,256]{1,0:T(8,128)S(1)}, f32[32,2304]{1,0:T(8,128)}) custom-call(s32[2]{0:T(128)S(1)} %add_convert_fusion.flags_ref, bf16[32,2304]{1,0:T(8,128)(2,1)S(1)} %get-tuple-element.37.values_ref, ...), custom_call_target="tpu_custom_call" | custom-call | flops 268435456 | bytes 1048576 | tf_op jit(solution)/shard_map/pallas_call | solution.py:50
  14.2 1.6 %collective-permute-start.1 = (f32[32,256]{1,0:T(8,128)S(1)}, f32[32,256]{1,0:T(8,128)S(1)}, u32[]{:S(2)}, u32[]{:S(2)}) collective-permute-start(f32[32,256]{1,0:T(8,128)S(1)} %get-tuple-element.40.sum_face), channel_id=1, source_target_pairs={{0,8},{8,16},{16,24},{24,0},{1,9},{9,17},{17,25},{25,1},{2,10},{10... | collective-permute-start | bytes 98312 | tf_op jit(solution)/shard_map/ppermute | solution.py:264
  15.8 2.2 %collective-permute-start.2 = (f32[32,256]{1,0:T(8,128)S(1)}, f32[32,256]{1,0:T(8,128)S(1)}, u32[]{:S(2)}, u32[]{:S(2)}) collective-permute-start(f32[32,256]{1,0:T(8,128)S(1)} %get-tuple-element.41.sum_ghost), channel_id=1, source_target_pairs={{0,24},{8,0},{16,8},{24,16},{1,25},{9,1},{17,9},{25,17},{2,26},{10... | collective-permute-start | bytes 98312 | tf_op jit(solution)/shard_map/ppermute | solution.py:264
  18.0 3.1 %shard_map.107 = (f32[32,1280]{1,0:T(8,128)S(1)}, bf16[32,2304]{1,0:T(8,128)(2,1)S(1)}) custom-call(bf16[64,2304]{1,0:T(8,128)(2,1)S(1)} %get-tuple-element.43.parts_ref, f32[32,1280]{1,0:T(8,128)S(1)} %get-tuple-element.44.state_ref.rest_0_, bf16[1280,2304]{1,0:T(8,128)(2,1)S(1)} %get-tuple-element.45.rest_0_.rest_1_.own_ref, ...), custom_call_target="tpu_custom_call" | custom-call | flops 268435456 | bytes 1048576 | tf_op jit(solution)/shard_map/pallas_call | solution.py:50
  21.1 0.0 collective-permute-done.1.got_ghost
  21.1 0.0 collective-permute-done.2.got_face
  21.2 2.4 %shard_map.108 = (bf16[64,2304]{1,0:T(8,128)(2,1)S(1)}, f32[32,256]{1,0:T(8,128)S(1)}, f32[32,256]{1,0:T(8,128)S(1)}, f32[32,256]{1,0:T(8,128)S(1)}, f32[32,256]{1,0:T(8,128)S(1)}, /*index=5*/f32[32,2304]{1,0:T(8,128)}) custom-call(s32[2]{0:T(128)S(1)} %add_convert_fusion.flags_ref, f32[32,256]{1,0:T(8,128)S(1)} %collective-permute-done.1.got_ghost, ...), custom_call_target="tpu_custom_call" | custom-call | flops 268435456 | bytes 1048576 | tf_op jit(solution)/shard_map/pallas_call | solution.py:50
  23.6 0.1 collective-permute-start.3
  23.7 3.7 %collective-permute-start.4 = (f32[32,256]{1,0:T(8,128)S(1)}, f32[32,256]{1,0:T(8,128)S(1)}, u32[]{:S(2)}, u32[]{:S(2)}) collective-permute-start(f32[32,256]{1,0:T(8,128)S(1)} %get-tuple-element.49.sum_ghost), channel_id=1, source_target_pairs={{0,24},{8,0},{16,8},{24,16},{1,25},{9,1},{17,9},{25,17},{2,26},{10... | collective-permute-start | bytes 98312 | tf_op jit(solution)/shard_map/ppermute | solution.py:264
  27.4 3.1 %shard_map.109 = (f32[32,1280]{1,0:T(8,128)S(1)}, bf16[32,2304]{1,0:T(8,128)(2,1)S(1)}) custom-call(bf16[64,2304]{1,0:T(8,128)(2,1)S(1)} %get-tuple-element.52.parts_ref, f32[32,1280]{1,0:T(8,128)S(1)} %get-tuple-element.53.state_ref.rest_0_, f32[32,1280]{1,0:T(8,128)S(1)} %get-tuple-element.44.state_ref.rest_0_, ...), custom_call_target="tpu_custom_call" | custom-call | flops 268435456 | bytes 1048576 | tf_op jit(solution)/shard_map/pallas_call | solution.py:50
  30.6 0.0 copy-start.5
  30.6 0.0 collective-permute-done.3.got_ghost
  30.6 0.0 collective-permute-done.4.got_face
  30.6 2.4 %shard_map.110 = (bf16[64,2304]{1,0:T(8,128)(2,1)S(1)}, f32[32,256]{1,0:T(8,128)S(1)}, f32[32,256]{1,0:T(8,128)S(1)}, f32[32,256]{1,0:T(8,128)S(1)}, f32[32,256]{1,0:T(8,128)S(1)}, /*index=5*/f32[32,2304]{1,0:T(8,128)}) custom-call(s32[2]{0:T(128)S(1)} %add_convert_fusion.flags_ref, f32[32,256]{1,0:T(8,128)S(1)} %collective-permute-done.3.got_ghost, ...), custom_call_target="tpu_custom_call" | custom-call | flops 268435456 | bytes 1048576 | tf_op jit(solution)/shard_map/pallas_call | solution.py:50
  33.0 0.0 collective-permute-start.5
  33.1 3.8 %collective-permute-start.6 = (f32[32,256]{1,0:T(8,128)S(1)}, f32[32,256]{1,0:T(8,128)S(1)}, u32[]{:S(2)}, u32[]{:S(2)}) collective-permute-start(f32[32,256]{1,0:T(8,128)S(1)} %get-tuple-element.56.sum_ghost), channel_id=1, source_target_pairs={{0,24},{8,0},{16,8},{24,16},{1,25},{9,1},{17,9},{25,17},{2,26},{10... | collective-permute-start | bytes 98312 | tf_op jit(solution)/shard_map/ppermute | solution.py:264
  36.9 3.1 %shard_map.111 = (f32[32,1280]{1,0:T(8,128)S(1)}, bf16[32,2304]{1,0:T(8,128)(2,1)S(1)}) custom-call(bf16[64,2304]{1,0:T(8,128)(2,1)S(1)} %get-tuple-element.59.parts_ref, f32[32,1280]{1,0:T(8,128)S(1)} %get-tuple-element.60.state_ref, f32[32,1280]{1,0:T(8,128)S(1)} %get-tuple-element.53.state_ref.rest_0_, ...), custom_call_target="tpu_custom_call" | custom-call | flops 268435456 | bytes 1048576 | tf_op jit(solution)/shard_map/pallas_call | solution.py:50
  40.0 0.0 collective-permute-done.6.got_face
  40.1 1.2 %shard_map.112 = (f32[32,256]{1,0:T(8,128)S(1)}, bf16[32,2304]{1,0:T(8,128)(2,1)S(1)}, f32[288,343]{1,0:T(8,128)S(1)}, f32[9,343]{1,0:T(8,128)S(1)}) custom-call(s32[2]{0:T(128)S(1)} %add_convert_fusion.flags_ref, f32[32,256]{1,0:T(8,128)S(1)} %collective-permute-done.5.got_ghost, f32[32,256]{1,0:T(8,128)S(1)} %collective-permute-done.6.got_face, ...), custom_call_target="tpu_custom_call" | custom-call | flops 268435456 | bytes 1048576 | tf_op jit(solution)/shard_map/pallas_call | solution.py:50
  41.3 0.1 collective-permute-start.7
  41.3 1.2 %collective-permute-done.7 = f32[9,343]{1,0:T(8,128)S(1)} collective-permute-done((f32[9,343]{1,0:T(8,128)S(1)}, f32[9,343]{1,0:T(8,128)S(1)}, u32[]{:S(2)}, u32[]{:S(2)}) %collective-permute-start.7) | collective-permute-done | bytes 12380 | tf_op jit(solution)/shard_map/ppermute | solution.py:268
  42.5 2.5 %collective-permute-start.10 = (f32[9,343]{1,0:T(8,128)S(1)}, f32[9,343]{1,0:T(8,128)S(1)}, u32[]{:S(2)}, u32[]{:S(2)}) collective-permute-start(f32[9,343]{1,0:T(8,128)S(1)} %add.5.total_ref), channel_id=1, source_target_pairs={{0,6},{1,7},{2,4},{3,5},{4,2},{5,3},{6,0},{7,1},{8,14},{9,15},{10,... | collective-permute-start | bytes 37052 | tf_op jit(solution)/shard_map/ppermute | solution.py:268
  45.0 0.5 collective-permute-start.9
  45.5 0.5 collective-permute-start.8
  46.0 0.3 shard_map.113.rest_7_
  46.3 0.9 %collective-permute-done.10.rest_2_ = f32[9,343]{1,0:T(8,128)S(1)} collective-permute-done((f32[9,343]{1,0:T(8,128)S(1)}, f32[9,343]{1,0:T(8,128)S(1)}, u32[]{:S(2)}, u32[]{:S(2)}) %collective-permute-start.10) | collective-permute-done | bytes 12380 | tf_op jit(solution)/shard_map/ppermute | solution.py:268
  47.2 1.6 %collective-permute-done.9.rest_1_ = f32[9,343]{1,0:T(8,128)S(1)} collective-permute-done((f32[9,343]{1,0:T(8,128)S(1)}, f32[9,343]{1,0:T(8,128)S(1)}, u32[]{:S(2)}, u32[]{:S(2)}) %collective-permute-start.9) | collective-permute-done | bytes 12380 | tf_op jit(solution)/shard_map/ppermute | solution.py:268
  48.8 0.5 collective-permute-done.8.rest_0_
  49.3 1.3 %shard_map.114 = (f32[9,343]{1,0:T(8,128)S(1)}, bf16[64,2304]{1,0:T(8,128)(2,1)S(1)}, f32[32,256]{1,0:T(8,128)S(1)}, f32[32,2304]{1,0:T(8,128)}) custom-call(f32[9,343]{1,0:T(8,128)S(1)} %add.5.total_ref, f32[9,343]{1,0:T(8,128)S(1)} %collective-permute-done.8.rest_0_, f32[9,343]{1,0:T(8,128)S(1)} %collective-permute-done.9.rest_1_, ...), custom_call_target="tpu_custom_call" | custom-call | flops 268435456 | bytes 1048576 | tf_op jit(solution)/shard_map/pallas_call | solution.py:50
  50.6 2.5 %collective-permute-start.11 = (f32[32,256]{1,0:T(8,128)S(1)}, f32[32,256]{1,0:T(8,128)S(1)}, u32[]{:S(2)}, u32[]{:S(2)}) collective-permute-start(f32[32,256]{1,0:T(8,128)S(1)} %get-tuple-element.65), channel_id=1, source_target_pairs={{0,24},{8,0},{16,8},{24,16},{1,25},{9,1},{17,9},{25,17},{2,26},{10... | collective-permute-start | bytes 98312 | tf_op jit(solution)/shard_map/ppermute | solution.py:264
  53.1 0.6 %copy.13 = f32[9,343]{1,0:T(8,128)} copy(f32[9,343]{1,0:T(8,128)S(1)} %get-tuple-element.71) | data formatting | bytes 24696
  53.8 1.9 %shard_map.115.partial_ref = f32[32,1280]{1,0:T(8,128)S(1)} custom-call(bf16[64,2304]{1,0:T(8,128)(2,1)S(1)} %get-tuple-element.66.parts_ref, f32[32,1280]{1,0:T(8,128)S(1)} %get-tuple-element.67.state_ref, f32[32,256]{1,0:T(8,128)S(1)} %get-tuple-element.68.face_ref, f32[1,32]{1,0:T(1,128)S(1)} %bitcast.11, ...), custom_call_target="tpu_custom_call" | custom-call | flops 268435456 | bytes 1048576 | tf_op jit(solution)/shard_map/pallas_call | solution.py:50
  55.7 0.0 collective-permute-done.11.got_ref
  55.7 0.9 %shard_map.116 = f32[32,1280]{1,0:T(8,128)S(1)} custom-call(s32[2]{0:T(128)S(1)} %add_convert_fusion.flags_ref, f32[32,256]{1,0:T(8,128)S(1)} %collective-permute-done.11.got_ref, f32[32,1280]{1,0:T(8,128)S(1)} %shard_map.115.partial_ref, bf16[1280,256]{1,0:T(8,128)(2,1)S(1)} %get-tuple-element.36.face_table_ref), custom_call_target="tpu_custom_call" | custom-call | flops 268435456 | bytes 1048576 | tf_op jit(solution)/shard_map/pallas_call | solution.py:50
  56.6 0.7 %copy.12 = f32[32,1280]{1,0:T(8,128)} copy(f32[32,1280]{1,0:T(8,128)S(1)} %shard_map.116) | data formatting | bytes 327680
  (18 shorter events, 0.0 us)
Async XLA Ops:
  0.6 0.9 %copy-start.7 = (bf16[32,1280]{1,0:T(8,128)(2,1)S(1)}, bf16[32,1280]{1,0:T(8,128)(2,1)}, u32[]{:S(2)}) copy-start(bf16[32,1280]{1,0:T(8,128)(2,1)} %w_ref.3) | copy-start | bytes 245764
  1.5 0.7 %copy-start.9 = (s32[256]{0:T(256)S(1)}, s32[256]{0:T(256)}, u32[]{:S(2)}) copy-start(s32[256]{0:T(256)} %param.12) | copy-start | bytes 3076
  2.2 18.9 %copy-start.1 = (bf16[9,216,216]{2,1,0:T(8,128)(2,1)S(1)}, bf16[9,216,216]{2,1,0:T(8,128)(2,1)}, u32[]{:S(2)}) copy-start(bf16[9,216,216]{2,1,0:T(8,128)(2,1)} %matrix_ref.3) | copy-start | bytes 2519428
  2.4 8.2 %collective-permute-start = (bf16[32,256]{1,0:T(8,128)(2,1)S(1)}, bf16[32,256]{1,0:T(8,128)(2,1)S(1)}, u32[]{:S(2)}, u32[]{:S(2)}) collective-permute-start(bf16[32,256]{1,0:T(8,128)(2,1)S(1)} %get-tuple-element.38), channel_id=1, source_target_pairs={{0,8},{8,16},{16,24},{24,0},{1,9},{9,17},{17,25},{25,1},{2,10},{10... | collective-permute-start | bytes 49160 | tf_op jit(solution)/shard_map/ppermute | solution.py:264
  6.3 0.9 %copy-start.8 = (bf16[32,1280]{1,0:T(8,128)(2,1)S(1)}, bf16[32,1280]{1,0:T(8,128)(2,1)}, u32[]{:S(2)}) copy-start(bf16[32,1280]{1,0:T(8,128)(2,1)} %w_ref.3) | copy-start | bytes 245764
  7.2 0.7 %copy-start.10 = (s32[256]{0:T(256)S(1)}, s32[256]{0:T(256)}, u32[]{:S(2)}) copy-start(s32[256]{0:T(256)} %param.12) | copy-start | bytes 3076
  10.7 1.2 %copy-start = (bf16[9,216,216]{2,1,0:T(8,128)(2,1)S(1)}, bf16[9,216,216]{2,1,0:T(8,128)(2,1)}, u32[]{:S(2)}) copy-start(bf16[9,216,216]{2,1,0:T(8,128)(2,1)} %matrix_ref.3) | copy-start | bytes 2519428
  14.2 6.9 %collective-permute-start.1 = (f32[32,256]{1,0:T(8,128)S(1)}, f32[32,256]{1,0:T(8,128)S(1)}, u32[]{:S(2)}, u32[]{:S(2)}) collective-permute-start(f32[32,256]{1,0:T(8,128)S(1)} %get-tuple-element.40.sum_face), channel_id=1, source_target_pairs={{0,8},{8,16},{16,24},{24,0},{1,9},{9,17},{17,25},{25,1},{2,10},{10... | collective-permute-start | bytes 98312 | tf_op jit(solution)/shard_map/ppermute | solution.py:264
  15.8 5.4 %collective-permute-start.2 = (f32[32,256]{1,0:T(8,128)S(1)}, f32[32,256]{1,0:T(8,128)S(1)}, u32[]{:S(2)}, u32[]{:S(2)}) collective-permute-start(f32[32,256]{1,0:T(8,128)S(1)} %get-tuple-element.41.sum_ghost), channel_id=1, source_target_pairs={{0,24},{8,0},{16,8},{24,16},{1,25},{9,1},{17,9},{25,17},{2,26},{10... | collective-permute-start | bytes 98312 | tf_op jit(solution)/shard_map/ppermute | solution.py:264
  23.6 7.0 %collective-permute-start.3 = (f32[32,256]{1,0:T(8,128)S(1)}, f32[32,256]{1,0:T(8,128)S(1)}, u32[]{:S(2)}, u32[]{:S(2)}) collective-permute-start(f32[32,256]{1,0:T(8,128)S(1)} %get-tuple-element.48.sum_face), channel_id=1, source_target_pairs={{0,8},{8,16},{16,24},{24,0},{1,9},{9,17},{17,25},{25,1},{2,10},{10... | collective-permute-start | bytes 98312 | tf_op jit(solution)/shard_map/ppermute | solution.py:264
  23.7 6.9 %collective-permute-start.4 = (f32[32,256]{1,0:T(8,128)S(1)}, f32[32,256]{1,0:T(8,128)S(1)}, u32[]{:S(2)}, u32[]{:S(2)}) collective-permute-start(f32[32,256]{1,0:T(8,128)S(1)} %get-tuple-element.49.sum_ghost), channel_id=1, source_target_pairs={{0,24},{8,0},{16,8},{24,16},{1,25},{9,1},{17,9},{25,17},{2,26},{10... | collective-permute-start | bytes 98312 | tf_op jit(solution)/shard_map/ppermute | solution.py:264
  30.6 9.5 %copy-start.2 = (bf16[216,343]{1,0:T(8,128)(2,1)S(1)}, bf16[216,343]{1,0:T(8,128)(2,1)}, u32[]{:S(2)}) copy-start(bf16[216,343]{1,0:T(8,128)(2,1)} %rest_6_.1) | copy-start | bytes 444532
  30.6 9.5 %copy-start.5 = (f32[32]{0:T(128)S(1)}, f32[32]{0:T(128)}, u32[]{:S(2)}) copy-start(f32[32]{0:T(128)} %param.16) | copy-start | bytes 388
  33.0 16.3 %copy-start.3 = (f32[9,343]{1,0:T(8,128)S(1)}, f32[9,343]{1,0:T(8,128)}, u32[]{:S(2)}) copy-start(f32[9,343]{1,0:T(8,128)} %rest_3_.3) | copy-start | bytes 37048
  33.0 16.3 %copy-start.4 = (f32[9,343]{1,0:T(8,128)S(1)}, f32[9,343]{1,0:T(8,128)}, u32[]{:S(2)}) copy-start(f32[9,343]{1,0:T(8,128)} %rest_4_.1) | copy-start | bytes 37048
  33.0 7.0 %collective-permute-start.5 = (f32[32,256]{1,0:T(8,128)S(1)}, f32[32,256]{1,0:T(8,128)S(1)}, u32[]{:S(2)}, u32[]{:S(2)}) collective-permute-start(f32[32,256]{1,0:T(8,128)S(1)} %get-tuple-element.55.sum_face), channel_id=1, source_target_pairs={{0,8},{8,16},{16,24},{24,0},{1,9},{9,17},{17,25},{25,1},{2,10},{10... | collective-permute-start | bytes 98312 | tf_op jit(solution)/shard_map/ppermute | solution.py:264
  33.1 7.0 %collective-permute-start.6 = (f32[32,256]{1,0:T(8,128)S(1)}, f32[32,256]{1,0:T(8,128)S(1)}, u32[]{:S(2)}, u32[]{:S(2)}) collective-permute-start(f32[32,256]{1,0:T(8,128)S(1)} %get-tuple-element.56.sum_ghost), channel_id=1, source_target_pairs={{0,24},{8,0},{16,8},{24,16},{1,25},{9,1},{17,9},{25,17},{2,26},{10... | collective-permute-start | bytes 98312 | tf_op jit(solution)/shard_map/ppermute | solution.py:264
  36.9 16.9 %copy-start.6 = (f32[32]{0:T(128)S(1)}, f32[32]{0:T(128)}, u32[]{:S(2)}) copy-start(f32[32]{0:T(128)} %param.17) | copy-start | bytes 388
  41.3 1.3 %collective-permute-start.7 = (f32[9,343]{1,0:T(8,128)S(1)}, f32[9,343]{1,0:T(8,128)S(1)}, u32[]{:S(2)}, u32[]{:S(2)}) collective-permute-start(f32[9,343]{1,0:T(8,128)S(1)} %get-tuple-element.62), channel_id=1, source_target_pairs={{0,1},{1,0},{2,3},{3,2},{4,5},{5,4},{6,7},{7,6},{8,9},{9,8},{10,11... | collective-permute-start | bytes 37052 | tf_op jit(solution)/shard_map/ppermute | solution.py:268
  42.5 4.7 %collective-permute-start.10 = (f32[9,343]{1,0:T(8,128)S(1)}, f32[9,343]{1,0:T(8,128)S(1)}, u32[]{:S(2)}, u32[]{:S(2)}) collective-permute-start(f32[9,343]{1,0:T(8,128)S(1)} %add.5.total_ref), channel_id=1, source_target_pairs={{0,6},{1,7},{2,4},{3,5},{4,2},{5,3},{6,0},{7,1},{8,14},{9,15},{10,... | collective-permute-start | bytes 37052 | tf_op jit(solution)/shard_map/ppermute | solution.py:268
  45.0 3.8 %collective-permute-start.9 = (f32[9,343]{1,0:T(8,128)S(1)}, f32[9,343]{1,0:T(8,128)S(1)}, u32[]{:S(2)}, u32[]{:S(2)}) collective-permute-start(f32[9,343]{1,0:T(8,128)S(1)} %add.5.total_ref), channel_id=1, source_target_pairs={{0,4},{1,5},{2,6},{3,7},{4,0},{5,1},{6,2},{7,3},{8,12},{9,13},{10,... | collective-permute-start | bytes 37052 | tf_op jit(solution)/shard_map/ppermute | solution.py:268
  45.5 3.8 %collective-permute-start.8 = (f32[9,343]{1,0:T(8,128)S(1)}, f32[9,343]{1,0:T(8,128)S(1)}, u32[]{:S(2)}, u32[]{:S(2)}) collective-permute-start(f32[9,343]{1,0:T(8,128)S(1)} %add.5.total_ref), channel_id=1, source_target_pairs={{0,2},{1,3},{2,0},{3,1},{4,6},{5,7},{6,4},{7,5},{8,10},{9,11},{10,... | collective-permute-start | bytes 37052 | tf_op jit(solution)/shard_map/ppermute | solution.py:268
  50.6 5.1 %collective-permute-start.11 = (f32[32,256]{1,0:T(8,128)S(1)}, f32[32,256]{1,0:T(8,128)S(1)}, u32[]{:S(2)}, u32[]{:S(2)}) collective-permute-start(f32[32,256]{1,0:T(8,128)S(1)} %get-tuple-element.65), channel_id=1, source_target_pairs={{0,24},{8,0},{16,8},{24,16},{1,25},{9,1},{17,9},{25,17},{2,26},{10... | collective-permute-start | bytes 98312 | tf_op jit(solution)/shard_map/ppermute | solution.py:264

commit v2 on v1

--- a/solution.py
+++ b/solution.py
@@ -13,6 +13,7 @@
 
 VMEM = pl.BlockSpec(memory_space=pltpu.VMEM)
 SMEM = pl.BlockSpec(memory_space=pltpu.SMEM)
+OUTSIDE = pl.BlockSpec(memory_space=pl.ANY)
 bf16 = jnp.bfloat16
 f32 = jnp.float32
 
@@ -46,85 +47,143 @@
     return jnp.where(hit, 1.0, 0.0).astype(bf16)
 
 
-def call(kernel, outs, *args, flops=1 << 28, smem=0):
+def call(kernel, outs, *args, flops=1 << 28, smem=0, held=0, sent=0, scratch=()):
+    count = len(args) - smem - held
+    kept = len(outs) - sent
     return pl.pallas_call(
         kernel,
-        out_shape=[pltpu.VMEM(shape, dtype) for shape, dtype in outs],
-        in_specs=[SMEM] * smem + [VMEM] * (len(args) - smem),
-        out_specs=[VMEM] * len(outs),
+        out_shape=[pltpu.VMEM(*out) for out in outs[:kept]]
+        + [jax.ShapeDtypeStruct(*out) for out in outs[kept:]],
+        in_specs=[SMEM] * smem + [OUTSIDE] * held + [VMEM] * count,
+        out_specs=[VMEM] * kept + [OUTSIDE] * sent,
+        scratch_shapes=list(scratch),
         compiler_params=pltpu.CompilerParams(vmem_limit_bytes=20 << 20),
         cost_estimate=pl.CostEstimate(flops=flops, bytes_accessed=1 << 20, transcendentals=0),
     )(*args)
 
 
-def pick_kernel(w_ref, face_ref, table_ref, out_ref):
+def pick_kernel(w_in, face_in, links_in, matrix_in, w_ref, face_ref, links_ref, matrix_ref, table_ref, out_ref, sems):
+    pairs = ((w_in, w_ref), (face_in, face_ref), (links_in, links_ref), (matrix_in, matrix_ref))
+    copies = [
+        pltpu.make_async_copy(source, target, sems.at[i]) for i, (source, target) in enumerate(pairs)
+    ]
+    for copy in copies:
+        copy.start()
     owned = w_ref.shape[1]
     count = face_ref.shape[1]
+    copies[1].wait()
     table = one_hot(lax.broadcasted_iota(jnp.int32, (owned, count), 0) == face_ref[...])
     table_ref[...] = table
+    copies[0].wait()
     out_ref[...] = dot(w_ref[...], table).astype(bf16)
+    copies[2].wait()
+    copies[3].wait()
+
+
+def short_one_hot(left, right):
+    return jnp.where(left == right, jnp.ones(left.shape, bf16), jnp.zeros(left.shape, bf16))
+
+
+def across(block, width):
+    return jnp.concatenate([block] * (width // block.shape[1]), axis=1)
 
 
 def tables_kernel(
-    w_ref, links_ref, face_ref, face_table_ref, own_ref, edge_ref, inner_ref, values_ref, state_ref
+    w_ref, face_ref, links_ref, matrix_ref, face_table_ref,
+    own_ref, edge_ref, from_own_ref, from_edge_ref, padded_ref, inner_ref, values_ref, state_ref,
+    row_ref, turn_ref, wide_ref,
 ):
     owned, slots = own_ref.shape
     count = face_ref.shape[1]
-    links = jnp.broadcast_to(links_ref[...], (8, slots))
-    strip = 16
+    cells, nodes = links_ref.shape
+    pitch = slots // cells
+    strip, lanes = 16, 128
+    short = jnp.int16
+
+    row_ref[...] = jnp.full(row_ref.shape, -1, jnp.int32)
+    turn_ref[...] = jnp.full(turn_ref.shape, -1.0, f32)
+    for cell in range(cells):
+        line = links_ref[cell : cell + 1, :]
+        row_ref[:, cell * pitch : cell * pitch + nodes] = jnp.broadcast_to(line, (strip, nodes))
+        turn_ref[cell : cell + 1, :nodes] = line.astype(f32)
+    links = row_ref[...].astype(short)
 
     def own_rows(i, carry):
         start = pl.multiple_of(i * strip, strip)
-        index = lax.broadcasted_iota(jnp.int32, (strip, slots), 0) + (start + count)
-        own_ref[pl.ds(start, strip), :] = one_hot(index == jnp.concatenate([links, links], axis=0))
+        index = lax.broadcasted_iota(jnp.int32, (strip, lanes), 0) + (start + count)
+        own_ref[pl.ds(start, strip), :] = short_one_hot(across(index.astype(short), slots), links)
         return carry
 
     lax.fori_loop(0, owned // strip, own_rows, 0, unroll=4)
+    w = w_ref[...]
+    values_ref[...] = dot(w, own_ref[...]).astype(bf16)
+
     ghost_index = lax.broadcasted_iota(jnp.int32, (count, 1), 0)
     face_index = column(face_ref[...].astype(f32)).astype(jnp.int32) + count
     for part, index in enumerate((ghost_index, face_index)):
         for start in range(0, count, strip):
-            rows = jnp.broadcast_to(index[start : start + strip], (strip, slots))
-            edge_ref[pl.ds(part * count + start, strip), :] = one_hot(
-                rows == jnp.concatenate([links, links], axis=0)
+            block = jnp.broadcast_to(index[start : start + strip], (strip, lanes)).astype(short)
+            edge_ref[part * count + start : part * count + start + strip, :] = short_one_hot(
+                across(block, slots), links
             )
+
+    edge_row = jnp.concatenate(
+        [
+            lax.broadcasted_iota(jnp.int32, (strip, count), 1),
+            jnp.broadcast_to(face_ref[...], (strip, count)) + count,
+        ],
+        axis=1,
+    ).astype(short)
+    own_row = (lax.broadcasted_iota(jnp.int32, (strip, owned), 1) + count).astype(short)
+    turned = jnp.transpose(turn_ref[...])
+    for cell in range(cells):
+        for start in range(0, pitch, strip):
+            block = jnp.broadcast_to(turned[start : start + strip, cell : cell + 1], (strip, lanes))
+            block = block.astype(jnp.int32).astype(short)
+            rows = slice(cell * pitch + start, cell * pitch + start + strip)
+            from_edge_ref[rows, :] = short_one_hot(across(block, 2 * count), edge_row)
+            from_own_ref[rows, :] = short_one_hot(across(block, owned), own_row)
+
+    wide_ref[...] = jnp.zeros_like(wide_ref)
+    for cell in range(cells):
+        wide_ref[cell % 2, :nodes, :nodes] = matrix_ref[cell].astype(f32)
+        padded_ref[cell] = wide_ref[cell % 2].astype(bf16)
+
     named = dot_rows(jnp.ones((8, count), bf16), face_table_ref[...])
     inner = 1.0 - named
     inner_ref[...] = inner
-    w = w_ref[...]
-    values_ref[...] = dot(w, own_ref[...]).astype(bf16)
     state_ref[...] = w.astype(f32) * inner[:1]
 
 
-def cell_products(values, matrix_ref, out_ref):
-    cells, nodes, _ = matrix_ref.shape
-    pitch = values.shape[1] // cells
-    out_ref[...] = jnp.zeros_like(out_ref)
-    for cell in range(cells):
-        start = cell * pitch
-        out_ref[:, start : start + nodes] = dot(values[:, start : start + nodes], matrix_ref[cell])
-
-
-def send_sums(values, matrix_ref, edge_ref, parts_ref, ghost_ref, face_ref, product_ref):
-    cell_products(values, matrix_ref, product_ref)
-    parts = halves(product_ref[...])
-    parts_ref[...] = parts
-    sums = joined(dot_rows(parts, edge_ref[...]))
+def cell_block(values, matrix_ref, cell):
+    pitch = matrix_ref.shape[1]
+    return dot(values[:, cell * pitch : (cell + 1) * pitch], matrix_ref[cell])
+
+
+def put_parts(parts_ref, cell, pitch, block):
+    parts_ref[:, cell * pitch : (cell + 1) * pitch] = halves(block)
+
+
+def send_sums(values, matrix_ref, from_edge_ref, parts_ref, ghost_ref, face_ref):
+    cells, pitch, _ = matrix_ref.shape
+    for cell in range(cells):
+        put_parts(parts_ref, cell, pitch, cell_block(values, matrix_ref, cell))
+    sums = joined(dot(parts_ref[...], from_edge_ref[...]))
     count = ghost_ref.shape[1]
     ghost_ref[...] = sums[:, :count]
     face_ref[...] = sums[:, count:]
 
 
 def first_kernel(
-    flags_ref, values_ref, got_ref, matrix_ref, edge_ref,
-    parts_ref, ghost_ref, face_ref, state_ref, product_ref,
+    flags_ref, values_ref, got_ref, matrix_ref, edge_ref, from_edge_ref,
+    parts_ref, ghost_ref, face_ref, state_ref,
 ):
     got = got_ref[...].astype(f32)
     got = jnp.where(flags_ref[0] > 0, got, jnp.zeros_like(got))
     state_ref[...] = got
     count = got.shape[1]
     values = values_ref[...].astype(f32) + dot(got.astype(bf16), edge_ref[:count, :])
-    send_sums(values.astype(bf16), matrix_ref, edge_ref, parts_ref, ghost_ref, face_ref, product_ref)
+    send_sums(values.astype(bf16), matrix_ref, from_edge_ref, parts_ref, ghost_ref, face_ref)
 
 
 def advance(scale, applied, state, before):
@@ -151,20 +210,20 @@
 
 def edge_kernel(scale, with_before, flags_ref, got_ghost, got_face, sum_ghost, sum_face, ghost, face, *rest):
     before, rest = (rest[:2], rest[2:]) if with_before else (None, rest)
-    values_ref, matrix_ref, edge_ref, parts_ref, out_ghost, out_face, new_ghost, new_face, product_ref = rest
+    values_ref, matrix_ref, edge_ref, from_edge_ref, parts_ref, out_ghost, out_face, new_ghost, new_face = rest
     ghost_value, face_value = edge_step(
         scale, flags_ref, got_ghost, got_face, sum_ghost, sum_face, ghost, face, before
     )
     new_ghost[...] = ghost_value
     new_face[...] = face_value
     values = next_values(ghost_value, face_value, values_ref, edge_ref)
-    send_sums(values, matrix_ref, edge_ref, parts_ref, out_ghost, out_face, product_ref)
+    send_sums(values, matrix_ref, from_edge_ref, parts_ref, out_ghost, out_face)
 
 
 def inner_kernel(scale, with_before, parts_ref, state_ref, *rest):
     before = rest[0][...] if with_before else None
-    own_ref, inner_ref, new_ref, values_ref = rest[1:] if with_before else rest
-    applied = joined(dot_rows(parts_ref[...], own_ref[...]))
+    own_ref, from_own_ref, inner_ref, new_ref, values_ref = rest[1:] if with_before else rest
+    applied = joined(dot(parts_ref[...], from_own_ref[...]))
     new = advance(scale, applied, state_ref[...], before) * inner_ref[:1]
     new_ref[...] = new
     values_ref[...] = dot(new.astype(bf16), own_ref[...]).astype(bf16)
@@ -196,8 +255,19 @@
         band_ref[cell : cell + 1, :] = jnp.sum(weights * (block * block), axis=0, keepdims=True)
 
 
-def products_kernel(values_ref, matrix_ref, product_ref):
-    cell_products(values_ref[...], matrix_ref, product_ref)
+def products_kernel(
+    values_ref, matrix_ref, basis_ref, face_ref, product_ref, wide_basis_ref, to_face_ref, wide_ref
+):
+    cells, pitch, _ = matrix_ref.shape
+    values = values_ref[...]
+    for cell in range(cells):
+        product_ref[:, cell * pitch : (cell + 1) * pitch] = cell_block(values, matrix_ref, cell)
+    nodes = basis_ref.shape[0]
+    wide_ref[...] = jnp.zeros_like(wide_ref)
+    wide_ref[:nodes, :] = basis_ref[...].astype(f32)
+    wide_basis_ref[...] = wide_ref[...].astype(bf16)
+    index = column(face_ref[...].astype(f32)).astype(jnp.int32)
+    to_face_ref[...] = one_hot(lax.broadcasted_iota(jnp.int32, to_face_ref.shape, 1) == index)
 
 
 def cube_root(x):
@@ -215,8 +285,8 @@
 
 
 def potential_kernel(total_ref, *rest, factor):
-    more, (core_ref, quad_ref, at_ref, basis_ref, product_ref, edge_ref,
-           potential_ref, parts_ref, ghost_ref, term_ref) = rest[:-10], rest[-10:]
+    more, (core_ref, quad_ref, at_ref, basis_ref, product_ref, from_edge_ref,
+           potential_ref, parts_ref, ghost_ref) = rest[:-9], rest[-9:]
     total = total_ref[...]
     if more:
         total = (total + more[0][...]) + (more[1][...] + more[2][...])
@@ -226,7 +296,6 @@
     cells = scaled.shape[0]
     waves, slots = product_ref.shape
     pitch = slots // cells
-    nodes = basis_ref.shape[0]
     weighted = jnp.concatenate(
         [
             (at_ref[cell * waves : (cell + 1) * waves, :] * scaled[cell : cell + 1]).astype(bf16)
@@ -235,28 +304,32 @@
         axis=0,
     )
     projected = dot_rows(weighted, basis_ref[...])
-    term_ref[...] = product_ref[...]
-    for cell in range(cells):
-        start = cell * pitch
-        term_ref[:, start : start + nodes] += projected[cell * waves : (cell + 1) * waves]
-    parts = halves(term_ref[...])
-    parts_ref[...] = parts
+    for cell in range(cells):
+        block = product_ref[:, cell * pitch : (cell + 1) * pitch]
+        put_parts(parts_ref, cell, pitch, block + projected[cell * waves : (cell + 1) * waves])
     count = ghost_ref.shape[1]
-    ghost_ref[...] = joined(dot_rows(parts, edge_ref[:count, :]))
-
-
-def residual_kernel(parts_ref, state_ref, face_ref, ritz_ref, own_ref, face_table_ref, out_ref):
+    ghost_ref[...] = joined(dot(parts_ref[...], from_edge_ref[:, :count]))
+
+
+def residual_kernel(
+    parts_ref, state_ref, face_ref, ritz_ref, from_own_ref, to_face_ref, potential_ref,
+    out_ref, potential_out, sem,
+):
+    copy = pltpu.make_async_copy(potential_ref, potential_out, sem)
+    copy.start()
     ritz = column(ritz_ref[...])
-    faces = joined(dot_rows(halves(ritz * face_ref[...]), face_table_ref[...]))
-    out_ref[...] = (
-        joined(dot_rows(parts_ref[...], own_ref[...])) - ritz * state_ref[...] - faces
-    )
-
-
-def finish_kernel(flags_ref, got_ref, partial_ref, face_table_ref, out_ref):
+    faces = joined(dot(halves(ritz * face_ref[...]), to_face_ref[...]))
+    out_ref[...] = joined(dot(parts_ref[...], from_own_ref[...])) - ritz * state_ref[...] - faces
+    copy.wait()
+
+
+def finish_kernel(flags_ref, got_ref, partial_ref, to_face_ref, out_ref, hold_ref, sem):
     got = got_ref[...]
     got = jnp.where(flags_ref[1] > 0, got, jnp.zeros_like(got))
-    out_ref[...] = partial_ref[...] + joined(dot_rows(halves(got), face_table_ref[...]))
+    hold_ref[...] = partial_ref[...] + joined(dot(halves(got), to_face_ref[...]))
+    copy = pltpu.make_async_copy(hold_ref, out_ref, sem)
+    copy.start()
+    copy.wait()
 
 
 def around(x, axis, distance):
@@ -308,29 +381,48 @@
     band_total = waves * lax.axis_size("band")
     domain = lax.axis_index("space")
     flags = jnp.stack([domain > 0, domain < lax.axis_size("space") - 1]).astype(jnp.int32)
-    links = jnp.pad(connectivity, ((0, 0), (0, pitch - nodes)), constant_values=-1)
-    links = links.reshape(1, slots)
-    faces = face_nodes.reshape(1, count)
-
     edge_out = [((waves, count), f32)] * 2
     parts_out = ((2 * waves, slots), bf16)
-    product_out = ((waves, slots), f32)
     values_out = ((waves, slots), bf16)
     state_out = ((waves, owned), f32)
 
-    face_table, start_face = call(
-        pick_kernel, [((owned, count), bf16), ((waves, count), bf16)], wavefunctions, faces
+    w, faces, links, matrix, face_table, start_face = call(
+        pick_kernel,
+        [
+            (wavefunctions.shape, bf16),
+            ((1, count), jnp.int32),
+            (connectivity.shape, jnp.int32),
+            (cell_hamiltonian.shape, bf16),
+            ((owned, count), bf16),
+            ((waves, count), bf16),
+        ],
+        wavefunctions, face_nodes.reshape(1, count), connectivity, cell_hamiltonian,
+        held=4, scratch=[pltpu.SemaphoreType.DMA((4,))],
     )
     start_ghost = around(start_face, "space", 1)
-    own, edge, inner, values, state = call(
+    own, edge, from_own, from_edge, padded, inner, values, state = call(
         tables_kernel,
-        [((owned, slots), bf16), ((2 * count, slots), bf16), ((8, owned), f32), values_out, state_out],
-        wavefunctions, links, faces, face_table,
-    )
-    parts, sum_ghost, sum_face, ghost, _ = call(
+        [
+            ((owned, slots), bf16),
+            ((2 * count, slots), bf16),
+            ((slots, owned), bf16),
+            ((slots, 2 * count), bf16),
+            ((cells, pitch, pitch), bf16),
+            ((8, owned), f32),
+            values_out,
+            state_out,
+        ],
+        w, faces, links, matrix, face_table,
+        scratch=[
+            pltpu.VMEM((16, slots), jnp.int32),
+            pltpu.VMEM((-(-cells // 128) * 128, pitch), f32),
+            pltpu.VMEM((2, pitch, pitch), f32),
+        ],
+    )
+    parts, sum_ghost, sum_face, ghost = call(
         first_kernel,
-        [parts_out, *edge_out, edge_out[0], product_out],
-        flags, values, start_ghost, cell_hamiltonian, edge, smem=1,
+        [parts_out, *edge_out, edge_out[0]],
+        flags, values, start_ghost, padded, edge, from_edge, smem=1,
     )
     face = start_face.astype(f32)
     before_edge, before_state = (), ()
@@ -341,14 +433,14 @@
         new_state, values = call(
             functools.partial(inner_kernel, scale, step > 0),
             [state_out, values_out],
-            parts, state, *before_state, own, inner,
+            parts, state, *before_state, own, from_own, inner,
         )
         received = (flags, got_ghost, got_face, sum_ghost, sum_face, ghost, face, *before_edge)
         if step < 2:
-            parts, sum_ghost, sum_face, new_ghost, new_face, _ = call(
+            parts, sum_ghost, sum_face, new_ghost, new_face = call(
                 functools.partial(edge_kernel, scale, step > 0),
-                [parts_out, *edge_out, *edge_out, product_out],
-                *received, values, cell_hamiltonian, edge, smem=1,
+                [parts_out, *edge_out, *edge_out],
+                *received, values, padded, edge, from_edge, smem=1,
             )
             before_edge, ghost, face = (ghost, face), new_ghost, new_face
         else:
@@ -359,19 +451,28 @@
             )
         before_state, state = (state,), new_state
         scale = 2.0 / spectrum_half
-    (products,) = call(products_kernel, [product_out], final, cell_hamiltonian)
+    products, wide_basis, to_face = call(
+        products_kernel,
+        [((waves, slots), f32), ((pitch, points), bf16), ((count, owned), bf16)],
+        final, padded, basis_values, faces, scratch=[pltpu.VMEM((pitch, points), f32)],
+    )
     totals = band_parts(band, "band")
-    potential, parts, sum_ghost, _ = call(
+    potential, parts, sum_ghost = call(
         functools.partial(potential_kernel, factor=2.0 / band_total),
-        [((cells, points), f32), parts_out, edge_out[0], product_out],
-        *totals, core_density, quad_weights, at, basis_values, products, edge,
+        [((cells, points), f32), parts_out, edge_out[0]],
+        *totals, core_density, quad_weights, at, wide_basis, products, from_edge,
     )
     returned = around(sum_ghost, "space", -1)
-    (partial,) = call(
-        residual_kernel, [state_out],
-        parts, state, face, ritz_values.reshape(1, waves), own, face_table,
-    )
-    (residual,) = call(finish_kernel, [state_out], flags, returned, partial, face_table, smem=1)
+    partial, potential = call(
+        residual_kernel,
+        [state_out, ((cells, points), f32)],
+        parts, state, face, ritz_values.reshape(1, waves), from_own, to_face, potential,
+        sent=1, scratch=[pltpu.SemaphoreType.DMA],
+    )
+    (residual,) = call(
+        finish_kernel, [state_out], flags, returned, partial, to_face,
+        smem=1, sent=1, scratch=[pltpu.VMEM(*state_out), pltpu.SemaphoreType.DMA],
+    )
     return (residual, potential)
 
 

time: 57.6 us -> 51.8 us (0.90)
  Pallas kernels: 25.2 us -> 20.4 us
  local copies, waits for them, and re-layouts: 6.37 us -> 3.51 us
  starting transfers between devices: 20.6 us -> 21.8 us
  waiting for transfers between devices: 4.2 us -> 4.94 us
    pallas_call x13, Pallas kernels: 25.2 us -> 20.4 us  [call(): pl.pallas_call(kernel, out_shape=[pltpu.VMEM(*out) for out in outs[:kept]...]
    unnamed x26 -> x18, local copies, waits for them, and re-layouts: 6.37 us -> 3.51 us
    ppermute x8, starting transfers between devices: 17.1 us -> 18.2 us  [around(): lax.ppermute(x, axis, [(i, (i + distance) % count) for i in range(count)])]
  transfers between devices with their start and end apart: 12 -> 12, of which waited for: 4 -> 6; matrix products, arithmetic and copies ran while one was open for 2% -> 0% of each run, Pallas kernels for 25% -> 22%
where the time goes in v2:
time: 51.8 us; the launch traced here: 51.5 us
  starting transfers between devices  21.8 us (42%)
  Pallas kernels  20.4 us (39%)
  waiting for transfers between devices  4.94 us (10%)
  local copies, waits for them, and re-layouts  3.51 us (7%)
  between operations  0.77 us (1%)
    pallas_call x13, Pallas kernels, call(): pl.pallas_call(kernel, out_shape=[pltpu.VMEM(*out) for out in outs[:kept]...  20.4 us
    ppermute x8, starting transfers between devices, around(): lax.ppermute(x, axis, [(i, (i + distance) % count) for i in range(count)])  18.2 us
    ppermute x4, waiting for transfers between devices, swapped(): lax.ppermute(x, axis, [(i, i ^ mask) for i in range(lax.axis_size(axis))])  4.34 us
    ppermute x4, starting transfers between devices, swapped(): lax.ppermute(x, axis, [(i, i ^ mask) for i in range(lax.axis_size(axis))])  3.56 us
    unnamed x18, local copies, waits for them, and re-layouts  3.51 us
  transfers between devices with their start and end apart: 12, of which 6 were waited for; matrix products, arithmetic and copies ran while one was open for 0% of the time, Pallas kernels for 22%

profile of v2, /device:TPU:0, one launch (start us, length us, event | category | flops | bytes accessed | tf_op | source)
XLA Modules:
  0.0 51.5 jit_solution(8896211985954190161)
XLA Ops:
  0.6 0.0 copy-start
  0.6 1.2 %copy-done = bf16[9,216,216]{2,1,0:T(8,128)(2,1)S(1)} copy-done((bf16[9,216,216]{2,1,0:T(8,128)(2,1)S(1)}, bf16[9,216,216]{2,1,0:T(8,128)(2,1)}, u32[]{:S(2)}) %copy-start) | copy-done | bytes 839832
  1.8 0.9 %copy-done.2 = bf16[32,1280]{1,0:T(8,128)(2,1)S(1)} copy-done((bf16[32,1280]{1,0:T(8,128)(2,1)S(1)}, bf16[32,1280]{1,0:T(8,128)(2,1)}, u32[]{:S(2)}) %copy-start.2) | copy-done | bytes 81944
  2.7 0.7 %copy-done.5 = s32[9,216]{1,0:T(8,128)S(1)} copy-done((s32[9,216]{1,0:T(8,128)S(1)}, s32[9,216]{1,0:T(8,128)}, u32[]{:S(2)}) %copy-start.5) | copy-done | bytes 7800
  3.4 0.7 %copy-done.6 = s32[256]{0:T(256)S(1)} copy-done((s32[256]{0:T(256)S(1)}, s32[256]{0:T(256)}, u32[]{:S(2)}) %copy-start.6) | copy-done | bytes 1048
  4.1 0.9 %shard_map.104 = (bf16[32,1280]{1,0:T(8,128)(2,1)S(1)}, s32[1,256]{1,0:T(1,128)S(1)}, s32[9,216]{1,0:T(8,128)S(1)}, bf16[9,216,216]{2,1,0:T(8,128)(2,1)S(1)}, bf...) custom-call(bf16[32,1280]{1,0:T(8,128)(2,1)S(1)} %copy-done.2, s32[1,256]{1,0:T(1,128)S(1)} %bitcast.5, ...), custom_call_target="tpu_custom_call" | custom-call | flops 268435456 | bytes 1048576 | tf_op jit(solution)/shard_map/pallas_call | solution.py:53
  5.0 3.1 %collective-permute-start = (bf16[32,256]{1,0:T(8,128)(2,1)S(1)}, bf16[32,256]{1,0:T(8,128)(2,1)S(1)}, u32[]{:S(2)}, u32[]{:S(2)}) collective-permute-start(bf16[32,256]{1,0:T(8,128)(2,1)S(1)} %get-tuple-element.54), channel_id=1, source_target_pairs={{0,8},{8,16},{16,24},{24,0},{1,9},{9,17},{17,25},{25,1},{2,10},{10... | collective-permute-start | bytes 49160 | tf_op jit(solution)/shard_map/ppermute | solution.py:337
  8.1 0.1 add_convert_fusion.flags_ref
  8.2 3.2 %shard_map.105 = (bf16[1280,2304]{1,0:T(8,128)(2,1)S(1)}, bf16[512,2304]{1,0:T(8,128)(2,1)S(1)}, bf16[2304,1280]{1,0:T(8,128)(2,1)S(1)}, bf16[2304,512]{1,0:T(8,...) custom-call(bf16[32,1280]{1,0:T(8,128)(2,1)S(1)} %get-tuple-element., ...), custom_call_target="tpu_custom_call" | custom-call | flops 268435456 | bytes 1048576 | tf_op jit(solution)/shard_map/pallas_call | solution.py:53
  11.4 0.5 collective-permute-done.got_ref
  11.9 1.5 %shard_map.106 = (bf16[64,2304]{1,0:T(8,128)(2,1)S(1)}, f32[32,256]{1,0:T(8,128)S(1)}, f32[32,256]{1,0:T(8,128)S(1)}, f32[32,256]{1,0:T(8,128)S(1)}) custom-call(s32[2]{0:T(128)S(1)} %add_convert_fusion.flags_ref, bf16[32,2304]{1,0:T(8,128)(2,1)S(1)} %get-tuple-element.53.values_ref, bf16[32,256]{1,0:T(8,128)(2,1)S(1)} %collective-permute-done.got_ref, ...), custom_call_target="tpu_custom_call" | custom-call | flops 268435456 | bytes 1048576 | tf_op jit(solution)/shard_map/pallas_call | solution.py:53
  13.3 1.1 %collective-permute-start.1 = (f32[32,256]{1,0:T(8,128)S(1)}, f32[32,256]{1,0:T(8,128)S(1)}, u32[]{:S(2)}, u32[]{:S(2)}) collective-permute-start(f32[32,256]{1,0:T(8,128)S(1)} %get-tuple-element.58.sum_face), channel_id=1, source_target_pairs={{0,8},{8,16},{16,24},{24,0},{1,9},{9,17},{17,25},{25,1},{2,10},{10... | collective-permute-start | bytes 98312 | tf_op jit(solution)/shard_map/ppermute | solution.py:337
  14.4 2.7 %collective-permute-start.2 = (f32[32,256]{1,0:T(8,128)S(1)}, f32[32,256]{1,0:T(8,128)S(1)}, u32[]{:S(2)}, u32[]{:S(2)}) collective-permute-start(f32[32,256]{1,0:T(8,128)S(1)} %get-tuple-element.59.sum_ghost), channel_id=1, source_target_pairs={{0,24},{8,0},{16,8},{24,16},{1,25},{9,1},{17,9},{25,17},{2,26},{10... | collective-permute-start | bytes 98312 | tf_op jit(solution)/shard_map/ppermute | solution.py:337
  17.2 2.1 %shard_map.107 = (f32[32,1280]{1,0:T(8,128)S(1)}, bf16[32,2304]{1,0:T(8,128)(2,1)S(1)}) custom-call(bf16[64,2304]{1,0:T(8,128)(2,1)S(1)} %get-tuple-element.61.parts_ref, f32[32,1280]{1,0:T(8,128)S(1)} %get-tuple-element.62.state_ref.rest_0_, bf16[1280,2304]{1,0:T(8,128)(2,1)S(1)} %get-tuple-element.63.rest_0_.rest_1_, ...), custom_call_target="tpu_custom_call" | custom-call | flops 268435456 | bytes 1048576 | tf_op jit(solution)/shard_map/pallas_call | solution.py:53
  19.3 0.0 collective-permute-done.1.got_ghost
  19.3 0.0 collective-permute-done.2.got_face
  19.3 1.7 %shard_map.108 = (bf16[64,2304]{1,0:T(8,128)(2,1)S(1)}, f32[32,256]{1,0:T(8,128)S(1)}, f32[32,256]{1,0:T(8,128)S(1)}, f32[32,256]{1,0:T(8,128)S(1)}, f32[32,256]{1,0:T(8,128)S(1)}) custom-call(s32[2]{0:T(128)S(1)} %add_convert_fusion.flags_ref, f32[32,256]{1,0:T(8,128)S(1)} %collective-permute-done.1.got_ghost, ...), custom_call_target="tpu_custom_call" | custom-call | flops 268435456 | bytes 1048576 | tf_op jit(solution)/shard_map/pallas_call | solution.py:53
  21.0 0.7 %collective-permute-start.3 = (f32[32,256]{1,0:T(8,128)S(1)}, f32[32,256]{1,0:T(8,128)S(1)}, u32[]{:S(2)}, u32[]{:S(2)}) collective-permute-start(f32[32,256]{1,0:T(8,128)S(1)} %get-tuple-element.67.sum_face), channel_id=1, source_target_pairs={{0,8},{8,16},{16,24},{24,0},{1,9},{9,17},{17,25},{25,1},{2,10},{10... | collective-permute-start | bytes 98312 | tf_op jit(solution)/shard_map/ppermute | solution.py:337
  21.7 3.1 %collective-permute-start.4 = (f32[32,256]{1,0:T(8,128)S(1)}, f32[32,256]{1,0:T(8,128)S(1)}, u32[]{:S(2)}, u32[]{:S(2)}) collective-permute-start(f32[32,256]{1,0:T(8,128)S(1)} %get-tuple-element.68.sum_ghost), channel_id=1, source_target_pairs={{0,24},{8,0},{16,8},{24,16},{1,25},{9,1},{17,9},{25,17},{2,26},{10... | collective-permute-start | bytes 98312 | tf_op jit(solution)/shard_map/ppermute | solution.py:337
  24.9 2.1 %shard_map.109 = (f32[32,1280]{1,0:T(8,128)S(1)}, bf16[32,2304]{1,0:T(8,128)(2,1)S(1)}) custom-call(bf16[64,2304]{1,0:T(8,128)(2,1)S(1)} %get-tuple-element.71.parts_ref, f32[32,1280]{1,0:T(8,128)S(1)} %get-tuple-element.72.state_ref.rest_0_, f32[32,1280]{1,0:T(8,128)S(1)} %get-tuple-element.62.state_ref.rest_0_, ...), custom_call_target="tpu_custom_call" | custom-call | flops 268435456 | bytes 1048576 | tf_op jit(solution)/shard_map/pallas_call | solution.py:53
  27.0 0.0 collective-permute-done.3.got_ghost
  27.0 0.0 collective-permute-done.4.got_face
  27.0 1.7 %shard_map.110 = (bf16[64,2304]{1,0:T(8,128)(2,1)S(1)}, f32[32,256]{1,0:T(8,128)S(1)}, f32[32,256]{1,0:T(8,128)S(1)}, f32[32,256]{1,0:T(8,128)S(1)}, f32[32,256]{1,0:T(8,128)S(1)}) custom-call(s32[2]{0:T(128)S(1)} %add_convert_fusion.flags_ref, f32[32,256]{1,0:T(8,128)S(1)} %collective-permute-done.3.got_ghost, ...), custom_call_target="tpu_custom_call" | custom-call | flops 268435456 | bytes 1048576 | tf_op jit(solution)/shard_map/pallas_call | solution.py:53
  28.7 0.7 %collective-permute-start.5 = (f32[32,256]{1,0:T(8,128)S(1)}, f32[32,256]{1,0:T(8,128)S(1)}, u32[]{:S(2)}, u32[]{:S(2)}) collective-permute-start(f32[32,256]{1,0:T(8,128)S(1)} %get-tuple-element.74.sum_face), channel_id=1, source_target_pairs={{0,8},{8,16},{16,24},{24,0},{1,9},{9,17},{17,25},{25,1},{2,10},{10... | collective-permute-start | bytes 98312 | tf_op jit(solution)/shard_map/ppermute | solution.py:337
  29.4 3.2 %collective-permute-start.6 = (f32[32,256]{1,0:T(8,128)S(1)}, f32[32,256]{1,0:T(8,128)S(1)}, u32[]{:S(2)}, u32[]{:S(2)}) collective-permute-start(f32[32,256]{1,0:T(8,128)S(1)} %get-tuple-element.75.sum_ghost), channel_id=1, source_target_pairs={{0,24},{8,0},{16,8},{24,16},{1,25},{9,1},{17,9},{25,17},{2,26},{10... | collective-permute-start | bytes 98312 | tf_op jit(solution)/shard_map/ppermute | solution.py:337
  32.6 2.1 %shard_map.111 = (f32[32,1280]{1,0:T(8,128)S(1)}, bf16[32,2304]{1,0:T(8,128)(2,1)S(1)}) custom-call(bf16[64,2304]{1,0:T(8,128)(2,1)S(1)} %get-tuple-element.78.parts_ref, f32[32,1280]{1,0:T(8,128)S(1)} %get-tuple-element.79.state_ref, f32[32,1280]{1,0:T(8,128)S(1)} %get-tuple-element.72.state_ref.rest_0_, ...), custom_call_target="tpu_custom_call" | custom-call | flops 268435456 | bytes 1048576 | tf_op jit(solution)/shard_map/pallas_call | solution.py:53
  34.7 0.0 copy-start.4
  34.7 0.0 collective-permute-done.5.got_ghost
  34.7 0.0 collective-permute-done.6.got_face
  34.8 0.0 copy-done.1
  34.8 0.0 copy-done.7
  34.8 1.2 %shard_map.112 = (f32[32,256]{1,0:T(8,128)S(1)}, bf16[32,2304]{1,0:T(8,128)(2,1)S(1)}, f32[288,343]{1,0:T(8,128)S(1)}, f32[9,343]{1,0:T(8,128)S(1)}) custom-call(s32[2]{0:T(128)S(1)} %add_convert_fusion.flags_ref, f32[32,256]{1,0:T(8,128)S(1)} %collective-permute-done.5.got_ghost, f32[32,256]{1,0:T(8,128)S(1)} %collective-permute-done.6.got_face, ...), custom_call_target="tpu_custom_call" | custom-call | flops 268435456 | bytes 1048576 | tf_op jit(solution)/shard_map/pallas_call | solution.py:53
  36.0 0.1 collective-permute-start.7
  36.1 1.2 %collective-permute-done.7 = f32[9,343]{1,0:T(8,128)S(1)} collective-permute-done((f32[9,343]{1,0:T(8,128)S(1)}, f32[9,343]{1,0:T(8,128)S(1)}, u32[]{:S(2)}, u32[]{:S(2)}) %collective-permute-start.7) | collective-permute-done | bytes 12380 | tf_op jit(solution)/shard_map/ppermute | solution.py:341
  37.2 2.7 %collective-permute-start.10 = (f32[9,343]{1,0:T(8,128)S(1)}, f32[9,343]{1,0:T(8,128)S(1)}, u32[]{:S(2)}, u32[]{:S(2)}) collective-permute-start(f32[9,343]{1,0:T(8,128)S(1)} %add.3.total_ref), channel_id=1, source_target_pairs={{0,6},{1,7},{2,4},{3,5},{4,2},{5,3},{6,0},{7,1},{8,14},{9,15},{10,... | collective-permute-start | bytes 37052 | tf_op jit(solution)/shard_map/ppermute | solution.py:341
  39.9 0.5 %collective-permute-start.8 = (f32[9,343]{1,0:T(8,128)S(1)}, f32[9,343]{1,0:T(8,128)S(1)}, u32[]{:S(2)}, u32[]{:S(2)}) collective-permute-start(f32[9,343]{1,0:T(8,128)S(1)} %add.3.total_ref), channel_id=1, source_target_pairs={{0,2},{1,3},{2,0},{3,1},{4,6},{5,7},{6,4},{7,5},{8,10},{9,11},{10,... | collective-permute-start | bytes 37052 | tf_op jit(solution)/shard_map/ppermute | solution.py:341
  40.4 0.3 collective-permute-start.9
  40.7 0.4 shard_map.113
  41.1 0.9 %collective-permute-done.10.rest_2_ = f32[9,343]{1,0:T(8,128)S(1)} collective-permute-done((f32[9,343]{1,0:T(8,128)S(1)}, f32[9,343]{1,0:T(8,128)S(1)}, u32[]{:S(2)}, u32[]{:S(2)}) %collective-permute-start.10) | collective-permute-done | bytes 12380 | tf_op jit(solution)/shard_map/ppermute | solution.py:341
  42.0 1.8 %collective-permute-done.8.rest_0_ = f32[9,343]{1,0:T(8,128)S(1)} collective-permute-done((f32[9,343]{1,0:T(8,128)S(1)}, f32[9,343]{1,0:T(8,128)S(1)}, u32[]{:S(2)}, u32[]{:S(2)}) %collective-permute-start.8) | collective-permute-done | bytes 12380 | tf_op jit(solution)/shard_map/ppermute | solution.py:341
  43.7 0.5 %collective-permute-done.9.rest_1_ = f32[9,343]{1,0:T(8,128)S(1)} collective-permute-done((f32[9,343]{1,0:T(8,128)S(1)}, f32[9,343]{1,0:T(8,128)S(1)}, u32[]{:S(2)}, u32[]{:S(2)}) %collective-permute-start.9) | collective-permute-done | bytes 12380 | tf_op jit(solution)/shard_map/ppermute | solution.py:341
  44.3 0.0 copy-done.3
  44.3 0.0 copy-done.4
  44.3 0.6 %shard_map.114 = (f32[9,343]{1,0:T(8,128)S(1)}, bf16[64,2304]{1,0:T(8,128)(2,1)S(1)}, f32[32,256]{1,0:T(8,128)S(1)}) custom-call(f32[9,343]{1,0:T(8,128)S(1)} %add.3.total_ref, f32[9,343]{1,0:T(8,128)S(1)} %collective-permute-done.8.rest_0_, f32[9,343]{1,0:T(8,128)S(1)} %collective-permute-done.9.rest_1_, f32[9,343]{1,0:T(8,128)S(1)} %collective-permute-done.10.rest_2_, ...), custom_call_target="tpu_custom_call" | custom-call | flops 268435456 | bytes 1048576 | tf_op jit(solution)/shard_map/pallas_call | solution.py:53
  44.9 3.5 %collective-permute-start.11 = (f32[32,256]{1,0:T(8,128)S(1)}, f32[32,256]{1,0:T(8,128)S(1)}, u32[]{:S(2)}, u32[]{:S(2)}) collective-permute-start(f32[32,256]{1,0:T(8,128)S(1)} %get-tuple-element.86), channel_id=1, source_target_pairs={{0,24},{8,0},{16,8},{24,16},{1,25},{9,1},{17,9},{25,17},{2,26},{10... | collective-permute-start | bytes 98312 | tf_op jit(solution)/shard_map/ppermute | solution.py:337
  48.4 1.5 %shard_map.115 = (f32[32,1280]{1,0:T(8,128)S(1)}, f32[9,343]{1,0:T(8,128)}) custom-call(bf16[64,2304]{1,0:T(8,128)(2,1)S(1)} %get-tuple-element.87.parts_ref, f32[32,1280]{1,0:T(8,128)S(1)} %get-tuple-element.88.state_ref, f32[32,256]{1,0:T(8,128)S(1)} %get-tuple-element.89.face_ref, f32[1,32]{1,0:T(1,128)S(1)} %bitcast.7, ...), custom_call_target="tpu_custom_call" | custom-call | flops 268435456 | bytes 1048576 | tf_op jit(solution)/shard_map/pallas_call | solution.py:53
  50.0 0.1 collective-permute-done.11.got_ref
  50.0 1.5 %shard_map.116 = f32[32,1280]{1,0:T(8,128)} custom-call(s32[2]{0:T(128)S(1)} %add_convert_fusion.flags_ref, f32[32,256]{1,0:T(8,128)S(1)} %collective-permute-done.11.got_ref, f32[32,1280]{1,0:T(8,128)S(1)} %get-tuple-element.92.partial_ref, bf16[256,1280]{1,0:T(8,128)(2,1)S(1)} %get-tuple-element.90.to_face_ref), custom_call_target="tpu_custom_call" | custom-call | flops 268435456 | bytes 1048576 | tf_op jit(solution)/shard_map/pallas_call | solution.py:53
  (10 shorter events, 0.0 us)
Async XLA Ops:
  0.6 1.2 %copy-start = (bf16[9,216,216]{2,1,0:T(8,128)(2,1)S(1)}, bf16[9,216,216]{2,1,0:T(8,128)(2,1)}, u32[]{:S(2)}) copy-start(bf16[9,216,216]{2,1,0:T(8,128)(2,1)} %matrix_in.1) | copy-start | bytes 2519428
  1.8 0.9 %copy-start.2 = (bf16[32,1280]{1,0:T(8,128)(2,1)S(1)}, bf16[32,1280]{1,0:T(8,128)(2,1)}, u32[]{:S(2)}) copy-start(bf16[32,1280]{1,0:T(8,128)(2,1)} %w_in.1) | copy-start | bytes 245764
  2.7 0.7 %copy-start.5 = (s32[9,216]{1,0:T(8,128)S(1)}, s32[9,216]{1,0:T(8,128)}, u32[]{:S(2)}) copy-start(s32[9,216]{1,0:T(8,128)} %links_in.1) | copy-start | bytes 23332
  3.4 0.7 %copy-start.6 = (s32[256]{0:T(256)S(1)}, s32[256]{0:T(256)}, u32[]{:S(2)}) copy-start(s32[256]{0:T(256)} %param.12) | copy-start | bytes 3076
  5.0 6.8 %collective-permute-start = (bf16[32,256]{1,0:T(8,128)(2,1)S(1)}, bf16[32,256]{1,0:T(8,128)(2,1)S(1)}, u32[]{:S(2)}, u32[]{:S(2)}) collective-permute-start(bf16[32,256]{1,0:T(8,128)(2,1)S(1)} %get-tuple-element.54), channel_id=1, source_target_pairs={{0,8},{8,16},{16,24},{24,0},{1,9},{9,17},{17,25},{25,1},{2,10},{10... | collective-permute-start | bytes 49160 | tf_op jit(solution)/shard_map/ppermute | solution.py:337
  13.3 5.9 %collective-permute-start.1 = (f32[32,256]{1,0:T(8,128)S(1)}, f32[32,256]{1,0:T(8,128)S(1)}, u32[]{:S(2)}, u32[]{:S(2)}) collective-permute-start(f32[32,256]{1,0:T(8,128)S(1)} %get-tuple-element.58.sum_face), channel_id=1, source_target_pairs={{0,8},{8,16},{16,24},{24,0},{1,9},{9,17},{17,25},{25,1},{2,10},{10... | collective-permute-start | bytes 98312 | tf_op jit(solution)/shard_map/ppermute | solution.py:337
  14.4 4.8 %collective-permute-start.2 = (f32[32,256]{1,0:T(8,128)S(1)}, f32[32,256]{1,0:T(8,128)S(1)}, u32[]{:S(2)}, u32[]{:S(2)}) collective-permute-start(f32[32,256]{1,0:T(8,128)S(1)} %get-tuple-element.59.sum_ghost), channel_id=1, source_target_pairs={{0,24},{8,0},{16,8},{24,16},{1,25},{9,1},{17,9},{25,17},{2,26},{10... | collective-permute-start | bytes 98312 | tf_op jit(solution)/shard_map/ppermute | solution.py:337
  21.0 6.0 %collective-permute-start.3 = (f32[32,256]{1,0:T(8,128)S(1)}, f32[32,256]{1,0:T(8,128)S(1)}, u32[]{:S(2)}, u32[]{:S(2)}) collective-permute-start(f32[32,256]{1,0:T(8,128)S(1)} %get-tuple-element.67.sum_face), channel_id=1, source_target_pairs={{0,8},{8,16},{16,24},{24,0},{1,9},{9,17},{17,25},{25,1},{2,10},{10... | collective-permute-start | bytes 98312 | tf_op jit(solution)/shard_map/ppermute | solution.py:337
  21.7 5.3 %collective-permute-start.4 = (f32[32,256]{1,0:T(8,128)S(1)}, f32[32,256]{1,0:T(8,128)S(1)}, u32[]{:S(2)}, u32[]{:S(2)}) collective-permute-start(f32[32,256]{1,0:T(8,128)S(1)} %get-tuple-element.68.sum_ghost), channel_id=1, source_target_pairs={{0,24},{8,0},{16,8},{24,16},{1,25},{9,1},{17,9},{25,17},{2,26},{10... | collective-permute-start | bytes 98312 | tf_op jit(solution)/shard_map/ppermute | solution.py:337
  28.7 6.0 %collective-permute-start.5 = (f32[32,256]{1,0:T(8,128)S(1)}, f32[32,256]{1,0:T(8,128)S(1)}, u32[]{:S(2)}, u32[]{:S(2)}) collective-permute-start(f32[32,256]{1,0:T(8,128)S(1)} %get-tuple-element.74.sum_face), channel_id=1, source_target_pairs={{0,8},{8,16},{16,24},{24,0},{1,9},{9,17},{17,25},{25,1},{2,10},{10... | collective-permute-start | bytes 98312 | tf_op jit(solution)/shard_map/ppermute | solution.py:337
  29.4 5.3 %collective-permute-start.6 = (f32[32,256]{1,0:T(8,128)S(1)}, f32[32,256]{1,0:T(8,128)S(1)}, u32[]{:S(2)}, u32[]{:S(2)}) collective-permute-start(f32[32,256]{1,0:T(8,128)S(1)} %get-tuple-element.75.sum_ghost), channel_id=1, source_target_pairs={{0,24},{8,0},{16,8},{24,16},{1,25},{9,1},{17,9},{25,17},{2,26},{10... | collective-permute-start | bytes 98312 | tf_op jit(solution)/shard_map/ppermute | solution.py:337
  32.6 2.2 %copy-start.1 = (bf16[216,343]{1,0:T(8,128)(2,1)S(1)}, bf16[216,343]{1,0:T(8,128)(2,1)}, u32[]{:S(2)}) copy-start(bf16[216,343]{1,0:T(8,128)(2,1)} %basis_ref.3) | copy-start | bytes 444532
  32.6 2.2 %copy-start.7 = (f32[32]{0:T(128)S(1)}, f32[32]{0:T(128)}, u32[]{:S(2)}) copy-start(f32[32]{0:T(128)} %param.16) | copy-start | bytes 388
  34.7 9.6 %copy-start.3 = (f32[9,343]{1,0:T(8,128)S(1)}, f32[9,343]{1,0:T(8,128)}, u32[]{:S(2)}) copy-start(f32[9,343]{1,0:T(8,128)} %rest_3_.1) | copy-start | bytes 37048
  34.7 9.6 %copy-start.4 = (f32[9,343]{1,0:T(8,128)S(1)}, f32[9,343]{1,0:T(8,128)}, u32[]{:S(2)}) copy-start(f32[9,343]{1,0:T(8,128)} %rest_4_.1) | copy-start | bytes 37048
  36.0 1.3 %collective-permute-start.7 = (f32[9,343]{1,0:T(8,128)S(1)}, f32[9,343]{1,0:T(8,128)S(1)}, u32[]{:S(2)}, u32[]{:S(2)}) collective-permute-start(f32[9,343]{1,0:T(8,128)S(1)} %get-tuple-element.81), channel_id=1, source_target_pairs={{0,1},{1,0},{2,3},{3,2},{4,5},{5,4},{6,7},{7,6},{8,9},{9,8},{10,11... | collective-permute-start | bytes 37052 | tf_op jit(solution)/shard_map/ppermute | solution.py:341
  37.2 4.7 %collective-permute-start.10 = (f32[9,343]{1,0:T(8,128)S(1)}, f32[9,343]{1,0:T(8,128)S(1)}, u32[]{:S(2)}, u32[]{:S(2)}) collective-permute-start(f32[9,343]{1,0:T(8,128)S(1)} %add.3.total_ref), channel_id=1, source_target_pairs={{0,6},{1,7},{2,4},{3,5},{4,2},{5,3},{6,0},{7,1},{8,14},{9,15},{10,... | collective-permute-start | bytes 37052 | tf_op jit(solution)/shard_map/ppermute | solution.py:341
  39.9 3.8 %collective-permute-start.8 = (f32[9,343]{1,0:T(8,128)S(1)}, f32[9,343]{1,0:T(8,128)S(1)}, u32[]{:S(2)}, u32[]{:S(2)}) collective-permute-start(f32[9,343]{1,0:T(8,128)S(1)} %add.3.total_ref), channel_id=1, source_target_pairs={{0,2},{1,3},{2,0},{3,1},{4,6},{5,7},{6,4},{7,5},{8,10},{9,11},{10,... | collective-permute-start | bytes 37052 | tf_op jit(solution)/shard_map/ppermute | solution.py:341
  40.4 3.8 %collective-permute-start.9 = (f32[9,343]{1,0:T(8,128)S(1)}, f32[9,343]{1,0:T(8,128)S(1)}, u32[]{:S(2)}, u32[]{:S(2)}) collective-permute-start(f32[9,343]{1,0:T(8,128)S(1)} %add.3.total_ref), channel_id=1, source_target_pairs={{0,4},{1,5},{2,6},{3,7},{4,0},{5,1},{6,2},{7,3},{8,12},{9,13},{10,... | collective-permute-start | bytes 37052 | tf_op jit(solution)/shard_map/ppermute | solution.py:341
  40.7 7.7 %copy-start.8 = (f32[32]{0:T(128)S(1)}, f32[32]{0:T(128)}, u32[]{:S(2)}) copy-start(f32[32]{0:T(128)} %param.17) | copy-start | bytes 388
  44.9 5.1 %collective-permute-start.11 = (f32[32,256]{1,0:T(8,128)S(1)}, f32[32,256]{1,0:T(8,128)S(1)}, u32[]{:S(2)}, u32[]{:S(2)}) collective-permute-start(f32[32,256]{1,0:T(8,128)S(1)} %get-tuple-element.86), channel_id=1, source_target_pairs={{0,24},{8,0},{16,8},{24,16},{1,25},{9,1},{17,9},{25,17},{2,26},{10... | collective-permute-start | bytes 98312 | tf_op jit(solution)/shard_map/ppermute | solution.py:337

commit v3 on v2

--- a/solution.py
+++ b/solution.py
@@ -13,7 +13,7 @@
 
 VMEM = pl.BlockSpec(memory_space=pltpu.VMEM)
 SMEM = pl.BlockSpec(memory_space=pltpu.SMEM)
-OUTSIDE = pl.BlockSpec(memory_space=pl.ANY)
+OUTSIDE = pl.BlockSpec(memory_space=pltpu.HBM)
 bf16 = jnp.bfloat16
 f32 = jnp.float32
 
@@ -47,7 +47,7 @@
     return jnp.where(hit, 1.0, 0.0).astype(bf16)
 
 
-def call(kernel, outs, *args, flops=1 << 28, smem=0, held=0, sent=0, scratch=()):
+def call(kernel, outs, *args, flops=1 << 28, smem=0, held=0, sent=0, scratch=(), room=20):
     count = len(args) - smem - held
     kept = len(outs) - sent
     return pl.pallas_call(
@@ -57,7 +57,7 @@
         in_specs=[SMEM] * smem + [OUTSIDE] * held + [VMEM] * count,
         out_specs=[VMEM] * kept + [OUTSIDE] * sent,
         scratch_shapes=list(scratch),
-        compiler_params=pltpu.CompilerParams(vmem_limit_bytes=20 << 20),
+        compiler_params=pltpu.CompilerParams(vmem_limit_bytes=room << 20),
         cost_estimate=pl.CostEstimate(flops=flops, bytes_accessed=1 << 20, transcendentals=0),
     )(*args)
 
@@ -164,26 +164,32 @@
     parts_ref[:, cell * pitch : (cell + 1) * pitch] = halves(block)
 
 
-def send_sums(values, matrix_ref, from_edge_ref, parts_ref, ghost_ref, face_ref):
+def chosen(flags_ref, first, second):
+    even = flags_ref[2] > 0
+    return jnp.where(even, second, first), jnp.where(even, first, second)
+
+
+def send_sums(flags_ref, values, matrix_ref, from_edge_ref, parts_ref, first_ref, second_ref):
     cells, pitch, _ = matrix_ref.shape
     for cell in range(cells):
         put_parts(parts_ref, cell, pitch, cell_block(values, matrix_ref, cell))
     sums = joined(dot(parts_ref[...], from_edge_ref[...]))
-    count = ghost_ref.shape[1]
-    ghost_ref[...] = sums[:, :count]
-    face_ref[...] = sums[:, count:]
+    count = first_ref.shape[1]
+    first_ref[...], second_ref[...] = chosen(flags_ref, sums[:, :count], sums[:, count:])
 
 
 def first_kernel(
-    flags_ref, values_ref, got_ref, matrix_ref, edge_ref, from_edge_ref,
-    parts_ref, ghost_ref, face_ref, state_ref,
+    flags_ref, values_ref, got_first, got_second, matrix_ref, edge_ref, from_edge_ref,
+    parts_ref, first_ref, second_ref, state_ref,
 ):
-    got = got_ref[...].astype(f32)
+    got, _ = chosen(flags_ref, got_first[...].astype(f32), got_second[...].astype(f32))
     got = jnp.where(flags_ref[0] > 0, got, jnp.zeros_like(got))
     state_ref[...] = got
     count = got.shape[1]
     values = values_ref[...].astype(f32) + dot(got.astype(bf16), edge_ref[:count, :])
-    send_sums(values.astype(bf16), matrix_ref, from_edge_ref, parts_ref, ghost_ref, face_ref)
+    send_sums(
+        flags_ref, values.astype(bf16), matrix_ref, from_edge_ref, parts_ref, first_ref, second_ref
+    )
 
 
 def advance(scale, applied, state, before):
@@ -191,14 +197,13 @@
     return new if before is None else new - before
 
 
-def edge_step(scale, flags_ref, got_ghost, got_face, sum_ghost, sum_face, ghost, face, before):
+def edge_step(scale, flags_ref, got_first, got_second, sum_first, sum_second, ghost, face, before):
     keep_ghost, keep_face = flags_ref[0] > 0, flags_ref[1] > 0
-    arrived = got_face[...]
-    applied_face = sum_face[...] + jnp.where(keep_face, arrived, jnp.zeros_like(arrived))
+    got_ghost, got_face = chosen(flags_ref, got_first[...], got_second[...])
+    sum_ghost, sum_face = chosen(flags_ref, sum_first[...], sum_second[...])
+    applied_face = sum_face + jnp.where(keep_face, got_face, jnp.zeros_like(got_face))
     new_face = advance(scale, applied_face, face[...], before and before[1][...])
-    new_ghost = advance(
-        scale, sum_ghost[...] + got_ghost[...], ghost[...], before and before[0][...]
-    )
+    new_ghost = advance(scale, sum_ghost + got_ghost, ghost[...], before and before[0][...])
     new_ghost = jnp.where(keep_ghost, new_ghost, jnp.zeros_like(new_ghost))
     return new_ghost, new_face
 
@@ -208,16 +213,16 @@
     return (values_ref[...].astype(f32) + dot(edge, edge_ref[...])).astype(bf16)
 
 
-def edge_kernel(scale, with_before, flags_ref, got_ghost, got_face, sum_ghost, sum_face, ghost, face, *rest):
+def edge_kernel(scale, with_before, flags_ref, got_first, got_second, sum_first, sum_second, ghost, face, *rest):
     before, rest = (rest[:2], rest[2:]) if with_before else (None, rest)
-    values_ref, matrix_ref, edge_ref, from_edge_ref, parts_ref, out_ghost, out_face, new_ghost, new_face = rest
+    values_ref, matrix_ref, edge_ref, from_edge_ref, parts_ref, out_first, out_second, new_ghost, new_face = rest
     ghost_value, face_value = edge_step(
-        scale, flags_ref, got_ghost, got_face, sum_ghost, sum_face, ghost, face, before
+        scale, flags_ref, got_first, got_second, sum_first, sum_second, ghost, face, before
     )
     new_ghost[...] = ghost_value
     new_face[...] = face_value
     values = next_values(ghost_value, face_value, values_ref, edge_ref)
-    send_sums(values, matrix_ref, from_edge_ref, parts_ref, out_ghost, out_face)
+    send_sums(flags_ref, values, matrix_ref, from_edge_ref, parts_ref, out_first, out_second)
 
 
 def inner_kernel(scale, with_before, parts_ref, state_ref, *rest):
@@ -230,12 +235,12 @@
 
 
 def density_kernel(
-    flags_ref, got_ghost, got_face, sum_ghost, sum_face, ghost, face, before_ghost, before_face,
+    flags_ref, got_first, got_second, sum_first, sum_second, ghost, face, before_ghost, before_face,
     values_ref, edge_ref, basis_ref, occupancy_ref,
     new_face, final_ref, at_ref, band_ref, *, scale, cells,
 ):
     ghost_value, face_value = edge_step(
-        scale, flags_ref, got_ghost, got_face, sum_ghost, sum_face, ghost, face,
+        scale, flags_ref, got_first, got_second, sum_first, sum_second, ghost, face,
         (before_ghost, before_face),
     )
     new_face[...] = face_value
@@ -323,8 +328,8 @@
     copy.wait()
 
 
-def finish_kernel(flags_ref, got_ref, partial_ref, to_face_ref, out_ref, hold_ref, sem):
-    got = got_ref[...]
+def finish_kernel(flags_ref, got_first, got_second, partial_ref, to_face_ref, out_ref, hold_ref, sem):
+    _, got = chosen(flags_ref, got_first[...], got_second[...])
     got = jnp.where(flags_ref[1] > 0, got, jnp.zeros_like(got))
     hold_ref[...] = partial_ref[...] + joined(dot(halves(got), to_face_ref[...]))
     copy = pltpu.make_async_copy(hold_ref, out_ref, sem)
@@ -332,9 +337,19 @@
     copy.wait()
 
 
-def around(x, axis, distance):
-    count = lax.axis_size(axis)
-    return lax.ppermute(x, axis, [(i, (i + distance) % count) for i in range(count)])
+def paired(x, parity):
+    domains, bands = lax.axis_size("space"), lax.axis_size("band")
+    route = []
+    for domain in range(domains):
+        other = domain + 1 if domain % 2 == parity else domain - 1
+        for band in range(bands):
+            target = (other, band) if 0 <= other < domains else (domain, band ^ 1 if bands % 2 == 0 else band)
+            route.append((domain * bands + band, target[0] * bands + target[1]))
+    return lax.ppermute(x, ("space", "band"), route)
+
+
+def exchanged(first, second):
+    return paired(first, 0), paired(second, 1)
 
 
 def swapped(x, axis, mask):
@@ -353,10 +368,10 @@
     while bit < count:
         x = parts[0] if len(parts) == 1 else (parts[0] + parts[1]) + (parts[2] + parts[3])
         if 2 * bit < count:
-            parts = [x] + [swapped(x, axis, mask) for mask in (bit, 2 * bit, 3 * bit)]
+            parts = [x] + [swapped(x, axis, mask ^ 1) for mask in (bit, 2 * bit, 3 * bit)]
             bit *= 4
         else:
-            parts = [x + swapped(x, axis, bit)]
+            parts = [x + swapped(x, axis, bit ^ 1)]
             bit *= 2
     return parts
 
@@ -380,7 +395,9 @@
     slots = cells * pitch
     band_total = waves * lax.axis_size("band")
     domain = lax.axis_index("space")
-    flags = jnp.stack([domain > 0, domain < lax.axis_size("space") - 1]).astype(jnp.int32)
+    flags = jnp.stack(
+        [domain > 0, domain < lax.axis_size("space") - 1, domain % 2 == 0]
+    ).astype(jnp.int32)
     edge_out = [((waves, count), f32)] * 2
     parts_out = ((2 * waves, slots), bf16)
     values_out = ((waves, slots), bf16)
@@ -397,9 +414,9 @@
             ((waves, count), bf16),
         ],
         wavefunctions, face_nodes.reshape(1, count), connectivity, cell_hamiltonian,
-        held=4, scratch=[pltpu.SemaphoreType.DMA((4,))],
-    )
-    start_ghost = around(start_face, "space", 1)
+        held=4, scratch=[pltpu.SemaphoreType.DMA((4,))], room=56,
+    )
+    start_pair = exchanged(start_face, start_face)
     own, edge, from_own, from_edge, padded, inner, values, state = call(
         tables_kernel,
         [
@@ -419,25 +436,24 @@
             pltpu.VMEM((2, pitch, pitch), f32),
         ],
     )
-    parts, sum_ghost, sum_face, ghost = call(
+    parts, *sums, ghost = call(
         first_kernel,
         [parts_out, *edge_out, edge_out[0]],
-        flags, values, start_ghost, padded, edge, from_edge, smem=1,
+        flags, values, *start_pair, padded, edge, from_edge, smem=1,
     )
     face = start_face.astype(f32)
     before_edge, before_state = (), ()
     scale = 1.0 / spectrum_half
     for step in range(3):
-        got_ghost = around(sum_face, "space", 1)
-        got_face = around(sum_ghost, "space", -1)
+        got = exchanged(*sums)
         new_state, values = call(
             functools.partial(inner_kernel, scale, step > 0),
             [state_out, values_out],
             parts, state, *before_state, own, from_own, inner,
         )
-        received = (flags, got_ghost, got_face, sum_ghost, sum_face, ghost, face, *before_edge)
+        received = (flags, *got, *sums, ghost, face, *before_edge)
         if step < 2:
-            parts, sum_ghost, sum_face, new_ghost, new_face = call(
+            parts, *sums, new_ghost, new_face = call(
                 functools.partial(edge_kernel, scale, step > 0),
                 [parts_out, *edge_out, *edge_out],
                 *received, values, padded, edge, from_edge, smem=1,
@@ -462,7 +478,7 @@
         [((cells, points), f32), parts_out, edge_out[0]],
         *totals, core_density, quad_weights, at, wide_basis, products, from_edge,
     )
-    returned = around(sum_ghost, "space", -1)
+    returned = exchanged(sum_ghost, sum_ghost)
     partial, potential = call(
         residual_kernel,
         [state_out, ((cells, points), f32)],
@@ -470,7 +486,7 @@
         sent=1, scratch=[pltpu.SemaphoreType.DMA],
     )
     (residual,) = call(
-        finish_kernel, [state_out], flags, returned, partial, to_face,
+        finish_kernel, [state_out], flags, *returned, partial, to_face,
         smem=1, sent=1, scratch=[pltpu.VMEM(*state_out), pltpu.SemaphoreType.DMA],
     )
     return (residual, potential)

time: 51.8 us -> 41.5 us (0.80)
  starting transfers between devices: 21.8 us -> 15.6 us
  local copies, waits for them, and re-layouts: 3.51 us -> 0.03 us
  waiting for transfers between devices: 4.94 us -> 3.99 us
    ppermute x8 -> x10, starting transfers between devices: 18.2 us -> 11.9 us  [paired(): return lax.ppermute(x, ('space', 'band'), route)]
    unnamed x18 -> x10, local copies, waits for them, and re-layouts: 3.51 us -> 0.03 us
    ppermute x4, waiting for transfers between devices: 4.34 us -> 3.23 us  [swapped(): lax.ppermute(x, axis, [(i, i ^ mask) for i in range(lax.axis_size(axis))])]
  transfers between devices with their start and end apart: 12 -> 14, of which waited for: 6 -> 4; matrix products, arithmetic and copies ran while one was open for 0% -> 0% of each run, Pallas kernels for 22% -> 28%
where the time goes in v3:
time: 41.5 us; the launch traced here: 41.3 us
  Pallas kernels  20.8 us (50%)
  starting transfers between devices  15.6 us (38%)
  waiting for transfers between devices  3.99 us (10%)
  between operations  0.8 us (2%)
    pallas_call x13, Pallas kernels, call(): pl.pallas_call(kernel, out_shape=[pltpu.VMEM(*out) for out in outs[:kept]...  20.8 us
    ppermute x10, starting transfers between devices, paired(): return lax.ppermute(x, ('space', 'band'), route)  11.9 us
    ppermute x4, starting transfers between devices, swapped(): lax.ppermute(x, axis, [(i, i ^ mask) for i in range(lax.axis_size(axis))])  3.73 us
    ppermute x4, waiting for transfers between devices, swapped(): lax.ppermute(x, axis, [(i, i ^ mask) for i in range(lax.axis_size(axis))])  3.23 us
  transfers between devices with their start and end apart: 14, of which 4 were waited for; matrix products, arithmetic and copies ran while one was open for 0% of the time, Pallas kernels for 28%

profile of v3, /device:TPU:0, one launch (start us, length us, event | category | flops | bytes accessed | tf_op | source)
XLA Modules:
  0.0 41.3 jit_solution(8096110814129237356)
XLA Ops:
  0.6 1.3 %shard_map.104 = (bf16[32,1280]{1,0:T(8,128)(2,1)S(1)}, s32[1,256]{1,0:T(1,128)S(1)}, s32[9,216]{1,0:T(8,128)S(1)}, bf16[9,216,216]{2,1,0:T(8,128)(2,1)S(1)}, bf...) custom-call(bf16[32,1280]{1,0:T(8,128)(2,1)} %w_in.1, s32[1,256]{1,0:T(1,128)} %bitcast.8, s32[9,216]{1,0:T(8,128)} %links_in.1, ...), custom_call_target="tpu_custom_call" | custom-call | flops 268435456 | bytes 1048576 | tf_op jit(solution)/shard_map/pallas_call | solution.py:53
  2.0 3.1 %collective-permute-start = (bf16[32,256]{1,0:T(8,128)(2,1)S(1)}, bf16[32,256]{1,0:T(8,128)(2,1)S(1)}, u32[]{:S(2)}, u32[]{:S(2)}) collective-permute-start(bf16[32,256]{1,0:T(8,128)(2,1)S(1)} %get-tuple-element.54), channel_id=1, source_target_pairs={{0,8},{1,9},{2,10},{3,11},{4,12},{5,13},{6,14},{7,15},{8,0},{9,1},... | collective-permute-start | bytes 49160 | tf_op jit(solution)/shard_map/ppermute | solution.py:348
  5.1 0.0 collective-permute-start.1
  5.1 0.1 add_convert_fusion.flags_ref
  5.1 3.2 %shard_map.105 = (bf16[1280,2304]{1,0:T(8,128)(2,1)S(1)}, bf16[512,2304]{1,0:T(8,128)(2,1)S(1)}, bf16[2304,1280]{1,0:T(8,128)(2,1)S(1)}, bf16[2304,512]{1,0:T(8,...) custom-call(bf16[32,1280]{1,0:T(8,128)(2,1)S(1)} %get-tuple-element., ...), custom_call_target="tpu_custom_call" | custom-call | flops 268435456 | bytes 1048576 | tf_op jit(solution)/shard_map/pallas_call | solution.py:53
  8.3 0.0 collective-permute-done.got_first
  8.3 0.0 collective-permute-done.1.got_second
  8.3 1.5 %shard_map.106 = (bf16[64,2304]{1,0:T(8,128)(2,1)S(1)}, f32[32,256]{1,0:T(8,128)S(1)}, f32[32,256]{1,0:T(8,128)S(1)}, f32[32,256]{1,0:T(8,128)S(1)}) custom-call(s32[3]{0:T(128)S(1)} %add_convert_fusion.flags_ref, bf16[32,2304]{1,0:T(8,128)(2,1)S(1)} %get-tuple-element.53.values_ref, bf16[32,256]{1,0:T(8,128)(2,1)S(1)} %collective-permute-done.got_first, ...), custom_call_target="tpu_custom_call" | custom-call | flops 268435456 | bytes 1048576 | tf_op jit(solution)/shard_map/pallas_call | solution.py:53
  9.8 3.2 %collective-permute-start.2 = (f32[32,256]{1,0:T(8,128)S(1)}, f32[32,256]{1,0:T(8,128)S(1)}, u32[]{:S(2)}, u32[]{:S(2)}) collective-permute-start(f32[32,256]{1,0:T(8,128)S(1)} %get-tuple-element.58.sum_first), channel_id=1, source_target_pairs={{0,8},{1,9},{2,10},{3,11},{4,12},{5,13},{6,14},{7,15},{8,0},{9,1},... | collective-permute-start | bytes 98312 | tf_op jit(solution)/shard_map/ppermute | solution.py:348
  13.0 0.0 collective-permute-start.3
  13.0 2.1 %shard_map.107 = (f32[32,1280]{1,0:T(8,128)S(1)}, bf16[32,2304]{1,0:T(8,128)(2,1)S(1)}) custom-call(bf16[64,2304]{1,0:T(8,128)(2,1)S(1)} %get-tuple-element.61.parts_ref, f32[32,1280]{1,0:T(8,128)S(1)} %get-tuple-element.62.state_ref.rest_0_, bf16[1280,2304]{1,0:T(8,128)(2,1)S(1)} %get-tuple-element.63.rest_0_.rest_1_, ...), custom_call_target="tpu_custom_call" | custom-call | flops 268435456 | bytes 1048576 | tf_op jit(solution)/shard_map/pallas_call | solution.py:53
  15.1 0.0 collective-permute-done.2.got_first
  15.1 0.0 collective-permute-done.3.got_second
  15.1 1.7 %shard_map.108 = (bf16[64,2304]{1,0:T(8,128)(2,1)S(1)}, f32[32,256]{1,0:T(8,128)S(1)}, f32[32,256]{1,0:T(8,128)S(1)}, f32[32,256]{1,0:T(8,128)S(1)}, f32[32,256]{1,0:T(8,128)S(1)}) custom-call(s32[3]{0:T(128)S(1)} %add_convert_fusion.flags_ref, f32[32,256]{1,0:T(8,128)S(1)} %collective-permute-done.2.got_first, ...), custom_call_target="tpu_custom_call" | custom-call | flops 268435456 | bytes 1048576 | tf_op jit(solution)/shard_map/pallas_call | solution.py:53
  16.8 1.9 %collective-permute-start.4 = (f32[32,256]{1,0:T(8,128)S(1)}, f32[32,256]{1,0:T(8,128)S(1)}, u32[]{:S(2)}, u32[]{:S(2)}) collective-permute-start(f32[32,256]{1,0:T(8,128)S(1)} %get-tuple-element.67.sum_first), channel_id=1, source_target_pairs={{0,8},{1,9},{2,10},{3,11},{4,12},{5,13},{6,14},{7,15},{8,0},{9,1},... | collective-permute-start | bytes 98312 | tf_op jit(solution)/shard_map/ppermute | solution.py:348
  18.7 0.0 collective-permute-start.5
  18.7 2.1 %shard_map.109 = (f32[32,1280]{1,0:T(8,128)S(1)}, bf16[32,2304]{1,0:T(8,128)(2,1)S(1)}) custom-call(bf16[64,2304]{1,0:T(8,128)(2,1)S(1)} %get-tuple-element.71.parts_ref, f32[32,1280]{1,0:T(8,128)S(1)} %get-tuple-element.72.state_ref.rest_0_, f32[32,1280]{1,0:T(8,128)S(1)} %get-tuple-element.62.state_ref.rest_0_, ...), custom_call_target="tpu_custom_call" | custom-call | flops 268435456 | bytes 1048576 | tf_op jit(solution)/shard_map/pallas_call | solution.py:53
  20.8 0.0 collective-permute-done.4.got_first
  20.9 0.0 collective-permute-done.5.got_second
  20.9 1.7 %shard_map.110 = (bf16[64,2304]{1,0:T(8,128)(2,1)S(1)}, f32[32,256]{1,0:T(8,128)S(1)}, f32[32,256]{1,0:T(8,128)S(1)}, f32[32,256]{1,0:T(8,128)S(1)}, f32[32,256]{1,0:T(8,128)S(1)}) custom-call(s32[3]{0:T(128)S(1)} %add_convert_fusion.flags_ref, f32[32,256]{1,0:T(8,128)S(1)} %collective-permute-done.4.got_first, ...), custom_call_target="tpu_custom_call" | custom-call | flops 268435456 | bytes 1048576 | tf_op jit(solution)/shard_map/pallas_call | solution.py:53
  22.5 2.0 %collective-permute-start.6 = (f32[32,256]{1,0:T(8,128)S(1)}, f32[32,256]{1,0:T(8,128)S(1)}, u32[]{:S(2)}, u32[]{:S(2)}) collective-permute-start(f32[32,256]{1,0:T(8,128)S(1)} %get-tuple-element.74.sum_first), channel_id=1, source_target_pairs={{0,8},{1,9},{2,10},{3,11},{4,12},{5,13},{6,14},{7,15},{8,0},{9,1},... | collective-permute-start | bytes 98312 | tf_op jit(solution)/shard_map/ppermute | solution.py:348
  24.5 0.0 collective-permute-start.7
  24.5 2.1 %shard_map.111 = (f32[32,1280]{1,0:T(8,128)S(1)}, bf16[32,2304]{1,0:T(8,128)(2,1)S(1)}) custom-call(bf16[64,2304]{1,0:T(8,128)(2,1)S(1)} %get-tuple-element.78.parts_ref, f32[32,1280]{1,0:T(8,128)S(1)} %get-tuple-element.79.state_ref, f32[32,1280]{1,0:T(8,128)S(1)} %get-tuple-element.72.state_ref.rest_0_, ...), custom_call_target="tpu_custom_call" | custom-call | flops 268435456 | bytes 1048576 | tf_op jit(solution)/shard_map/pallas_call | solution.py:53
  26.7 0.0 copy-start.2
  26.7 0.0 collective-permute-done.6.got_first
  26.7 0.0 collective-permute-done.7.got_second
  26.7 0.0 copy-done
  26.7 0.0 copy-done.3
  26.7 1.2 %shard_map.112 = (f32[32,256]{1,0:T(8,128)S(1)}, bf16[32,2304]{1,0:T(8,128)(2,1)S(1)}, f32[288,343]{1,0:T(8,128)S(1)}, f32[9,343]{1,0:T(8,128)S(1)}) custom-call(s32[3]{0:T(128)S(1)} %add_convert_fusion.flags_ref, f32[32,256]{1,0:T(8,128)S(1)} %collective-permute-done.6.got_first, f32[32,256]{1,0:T(8,128)S(1)} %collective-permute-done.7.got_second, ...), custom_call_target="tpu_custom_call" | custom-call | flops 268435456 | bytes 1048576 | tf_op jit(solution)/shard_map/pallas_call | solution.py:53
  27.9 0.6 %collective-permute-start.8 = (f32[9,343]{1,0:T(8,128)S(1)}, f32[9,343]{1,0:T(8,128)S(1)}, u32[]{:S(2)}, u32[]{:S(2)}) collective-permute-start(f32[9,343]{1,0:T(8,128)S(1)} %get-tuple-element.81), channel_id=1, source_target_pairs={{0,1},{1,0},{2,3},{3,2},{4,5},{5,4},{6,7},{7,6},{8,9},{9,8},{10,11... | collective-permute-start | bytes 37052 | tf_op jit(solution)/shard_map/ppermute | solution.py:356
  28.5 0.8 %collective-permute-done.8 = f32[9,343]{1,0:T(8,128)S(1)} collective-permute-done((f32[9,343]{1,0:T(8,128)S(1)}, f32[9,343]{1,0:T(8,128)S(1)}, u32[]{:S(2)}, u32[]{:S(2)}) %collective-permute-start.8) | collective-permute-done | bytes 12380 | tf_op jit(solution)/shard_map/ppermute | solution.py:356
  29.4 1.5 %collective-permute-start.10 = (f32[9,343]{1,0:T(8,128)S(1)}, f32[9,343]{1,0:T(8,128)S(1)}, u32[]{:S(2)}, u32[]{:S(2)}) collective-permute-start(f32[9,343]{1,0:T(8,128)S(1)} %add.8.total_ref), channel_id=1, source_target_pairs={{0,5},{1,4},{2,7},{3,6},{4,1},{5,0},{6,3},{7,2},{8,13},{9,12},{10,... | collective-permute-start | bytes 37052 | tf_op jit(solution)/shard_map/ppermute | solution.py:356
  30.8 1.2 %collective-permute-start.11 = (f32[9,343]{1,0:T(8,128)S(1)}, f32[9,343]{1,0:T(8,128)S(1)}, u32[]{:S(2)}, u32[]{:S(2)}) collective-permute-start(f32[9,343]{1,0:T(8,128)S(1)} %add.8.total_ref), channel_id=1, source_target_pairs={{0,7},{1,6},{2,5},{3,4},{4,3},{5,2},{6,1},{7,0},{8,15},{9,14},{10,... | collective-permute-start | bytes 37052 | tf_op jit(solution)/shard_map/ppermute | solution.py:356
  32.0 0.5 %collective-permute-start.9 = (f32[9,343]{1,0:T(8,128)S(1)}, f32[9,343]{1,0:T(8,128)S(1)}, u32[]{:S(2)}, u32[]{:S(2)}) collective-permute-start(f32[9,343]{1,0:T(8,128)S(1)} %add.8.total_ref), channel_id=1, source_target_pairs={{0,3},{1,2},{2,1},{3,0},{4,7},{5,6},{6,5},{7,4},{8,11},{9,10},{10,... | collective-permute-start | bytes 37052 | tf_op jit(solution)/shard_map/ppermute | solution.py:356
  32.5 0.4 shard_map.113
  32.9 0.0 collective-permute-done.10.rest_1_
  32.9 2.1 %collective-permute-done.11.rest_2_ = f32[9,343]{1,0:T(8,128)S(1)} collective-permute-done((f32[9,343]{1,0:T(8,128)S(1)}, f32[9,343]{1,0:T(8,128)S(1)}, u32[]{:S(2)}, u32[]{:S(2)}) %collective-permute-start.11) | collective-permute-done | bytes 12380 | tf_op jit(solution)/shard_map/ppermute | solution.py:356
  35.0 0.3 collective-permute-done.9.rest_0_
  35.3 0.0 copy-done.1
  35.3 0.0 copy-done.2
  35.3 0.6 %shard_map.114 = (f32[9,343]{1,0:T(8,128)S(1)}, bf16[64,2304]{1,0:T(8,128)(2,1)S(1)}, f32[32,256]{1,0:T(8,128)S(1)}) custom-call(f32[9,343]{1,0:T(8,128)S(1)} %add.8.total_ref, f32[9,343]{1,0:T(8,128)S(1)} %collective-permute-done.9.rest_0_, f32[9,343]{1,0:T(8,128)S(1)} %collective-permute-done.10.rest_1_, f32[9,343]{1,0:T(8,128)S(1)} %collective-permute-done.11.rest_2_, ...), custom_call_target="tpu_custom_call" | custom-call | flops 268435456 | bytes 1048576 | tf_op jit(solution)/shard_map/pallas_call | solution.py:53
  35.9 1.7 %collective-permute-start.12 = (f32[32,256]{1,0:T(8,128)S(1)}, f32[32,256]{1,0:T(8,128)S(1)}, u32[]{:S(2)}, u32[]{:S(2)}) collective-permute-start(f32[32,256]{1,0:T(8,128)S(1)} %get-tuple-element.86), channel_id=1, source_target_pairs={{0,8},{1,9},{2,10},{3,11},{4,12},{5,13},{6,14},{7,15},{8,0},{9,1},... | collective-permute-start | bytes 98312 | tf_op jit(solution)/shard_map/ppermute | solution.py:348
  37.6 0.0 collective-permute-start.13
  37.6 0.0 copy-done.4
  37.6 1.5 %shard_map.115 = (f32[32,1280]{1,0:T(8,128)S(1)}, f32[9,343]{1,0:T(8,128)}) custom-call(bf16[64,2304]{1,0:T(8,128)(2,1)S(1)} %get-tuple-element.87.parts_ref, f32[32,1280]{1,0:T(8,128)S(1)} %get-tuple-element.88.state_ref, f32[32,256]{1,0:T(8,128)S(1)} %get-tuple-element.89.face_ref, f32[1,32]{1,0:T(1,128)S(1)} %bitcast.7, ...), custom_call_target="tpu_custom_call" | custom-call | flops 268435456 | bytes 1048576 | tf_op jit(solution)/shard_map/pallas_call | solution.py:53
  39.1 0.7 %collective-permute-done.12.got_first = f32[32,256]{1,0:T(8,128)S(1)} collective-permute-done((f32[32,256]{1,0:T(8,128)S(1)}, f32[32,256]{1,0:T(8,128)S(1)}, u32[]{:S(2)}, u32[]{:S(2)}) %collective-permute-start.12) | collective-permute-done | bytes 32800 | tf_op jit(solution)/shard_map/ppermute | solution.py:348
  39.9 0.0 collective-permute-done.13.got_second
  39.9 1.5 %shard_map.116 = f32[32,1280]{1,0:T(8,128)} custom-call(s32[3]{0:T(128)S(1)} %add_convert_fusion.flags_ref, f32[32,256]{1,0:T(8,128)S(1)} %collective-permute-done.12.got_first, f32[32,256]{1,0:T(8,128)S(1)} %collective-permute-done.13.got_second, f32[32,1280]{1,0:T(8,128)S(1)} %get-tuple-element.92.partial_ref, ...), custom_call_target="tpu_custom_call" | custom-call | flops 268435456 | bytes 1048576 | tf_op jit(solution)/shard_map/pallas_call | solution.py:53
  (6 shorter events, 0.0 us)
Async XLA Ops:
  2.0 6.3 %collective-permute-start = (bf16[32,256]{1,0:T(8,128)(2,1)S(1)}, bf16[32,256]{1,0:T(8,128)(2,1)S(1)}, u32[]{:S(2)}, u32[]{:S(2)}) collective-permute-start(bf16[32,256]{1,0:T(8,128)(2,1)S(1)} %get-tuple-element.54), channel_id=1, source_target_pairs={{0,8},{1,9},{2,10},{3,11},{4,12},{5,13},{6,14},{7,15},{8,0},{9,1},... | collective-permute-start | bytes 49160 | tf_op jit(solution)/shard_map/ppermute | solution.py:348
  5.1 3.3 %collective-permute-start.1 = (bf16[32,256]{1,0:T(8,128)(2,1)S(1)}, bf16[32,256]{1,0:T(8,128)(2,1)S(1)}, u32[]{:S(2)}, u32[]{:S(2)}) collective-permute-start(bf16[32,256]{1,0:T(8,128)(2,1)S(1)} %get-tuple-element.54), channel_id=1, source_target_pairs={{0,1},{1,0},{2,3},{3,2},{4,5},{5,4},{6,7},{7,6},{8,16},{9,17},{10,... | collective-permute-start | bytes 49160 | tf_op jit(solution)/shard_map/ppermute | solution.py:348
  9.8 5.3 %collective-permute-start.2 = (f32[32,256]{1,0:T(8,128)S(1)}, f32[32,256]{1,0:T(8,128)S(1)}, u32[]{:S(2)}, u32[]{:S(2)}) collective-permute-start(f32[32,256]{1,0:T(8,128)S(1)} %get-tuple-element.58.sum_first), channel_id=1, source_target_pairs={{0,8},{1,9},{2,10},{3,11},{4,12},{5,13},{6,14},{7,15},{8,0},{9,1},... | collective-permute-start | bytes 98312 | tf_op jit(solution)/shard_map/ppermute | solution.py:348
  13.0 2.1 %collective-permute-start.3 = (f32[32,256]{1,0:T(8,128)S(1)}, f32[32,256]{1,0:T(8,128)S(1)}, u32[]{:S(2)}, u32[]{:S(2)}) collective-permute-start(f32[32,256]{1,0:T(8,128)S(1)} %get-tuple-element.59.sum_second), channel_id=1, source_target_pairs={{0,1},{1,0},{2,3},{3,2},{4,5},{5,4},{6,7},{7,6},{8,16},{9,17},{10,... | collective-permute-start | bytes 98312 | tf_op jit(solution)/shard_map/ppermute | solution.py:348
  16.8 4.1 %collective-permute-start.4 = (f32[32,256]{1,0:T(8,128)S(1)}, f32[32,256]{1,0:T(8,128)S(1)}, u32[]{:S(2)}, u32[]{:S(2)}) collective-permute-start(f32[32,256]{1,0:T(8,128)S(1)} %get-tuple-element.67.sum_first), channel_id=1, source_target_pairs={{0,8},{1,9},{2,10},{3,11},{4,12},{5,13},{6,14},{7,15},{8,0},{9,1},... | collective-permute-start | bytes 98312 | tf_op jit(solution)/shard_map/ppermute | solution.py:348
  18.7 2.1 %collective-permute-start.5 = (f32[32,256]{1,0:T(8,128)S(1)}, f32[32,256]{1,0:T(8,128)S(1)}, u32[]{:S(2)}, u32[]{:S(2)}) collective-permute-start(f32[32,256]{1,0:T(8,128)S(1)} %get-tuple-element.68.sum_second), channel_id=1, source_target_pairs={{0,1},{1,0},{2,3},{3,2},{4,5},{5,4},{6,7},{7,6},{8,16},{9,17},{10,... | collective-permute-start | bytes 98312 | tf_op jit(solution)/shard_map/ppermute | solution.py:348
  22.5 4.1 %collective-permute-start.6 = (f32[32,256]{1,0:T(8,128)S(1)}, f32[32,256]{1,0:T(8,128)S(1)}, u32[]{:S(2)}, u32[]{:S(2)}) collective-permute-start(f32[32,256]{1,0:T(8,128)S(1)} %get-tuple-element.74.sum_first), channel_id=1, source_target_pairs={{0,8},{1,9},{2,10},{3,11},{4,12},{5,13},{6,14},{7,15},{8,0},{9,1},... | collective-permute-start | bytes 98312 | tf_op jit(solution)/shard_map/ppermute | solution.py:348
  24.5 2.2 %collective-permute-start.7 = (f32[32,256]{1,0:T(8,128)S(1)}, f32[32,256]{1,0:T(8,128)S(1)}, u32[]{:S(2)}, u32[]{:S(2)}) collective-permute-start(f32[32,256]{1,0:T(8,128)S(1)} %get-tuple-element.75.sum_second), channel_id=1, source_target_pairs={{0,1},{1,0},{2,3},{3,2},{4,5},{5,4},{6,7},{7,6},{8,16},{9,17},{10,... | collective-permute-start | bytes 98312 | tf_op jit(solution)/shard_map/ppermute | solution.py:348
  24.5 2.2 %copy-start = (bf16[216,343]{1,0:T(8,128)(2,1)S(1)}, bf16[216,343]{1,0:T(8,128)(2,1)}, u32[]{:S(2)}) copy-start(bf16[216,343]{1,0:T(8,128)(2,1)} %basis_ref.3) | copy-start | bytes 444532
  24.5 2.2 %copy-start.3 = (f32[32]{0:T(128)S(1)}, f32[32]{0:T(128)}, u32[]{:S(2)}) copy-start(f32[32]{0:T(128)} %param.16) | copy-start | bytes 388
  26.7 8.6 %copy-start.1 = (f32[9,343]{1,0:T(8,128)S(1)}, f32[9,343]{1,0:T(8,128)}, u32[]{:S(2)}) copy-start(f32[9,343]{1,0:T(8,128)} %rest_3_.1) | copy-start | bytes 37048
  26.7 8.6 %copy-start.2 = (f32[9,343]{1,0:T(8,128)S(1)}, f32[9,343]{1,0:T(8,128)}, u32[]{:S(2)}) copy-start(f32[9,343]{1,0:T(8,128)} %rest_4_.1) | copy-start | bytes 37048
  27.9 1.4 %collective-permute-start.8 = (f32[9,343]{1,0:T(8,128)S(1)}, f32[9,343]{1,0:T(8,128)S(1)}, u32[]{:S(2)}, u32[]{:S(2)}) collective-permute-start(f32[9,343]{1,0:T(8,128)S(1)} %get-tuple-element.81), channel_id=1, source_target_pairs={{0,1},{1,0},{2,3},{3,2},{4,5},{5,4},{6,7},{7,6},{8,9},{9,8},{10,11... | collective-permute-start | bytes 37052 | tf_op jit(solution)/shard_map/ppermute | solution.py:356
  29.4 3.5 %collective-permute-start.10 = (f32[9,343]{1,0:T(8,128)S(1)}, f32[9,343]{1,0:T(8,128)S(1)}, u32[]{:S(2)}, u32[]{:S(2)}) collective-permute-start(f32[9,343]{1,0:T(8,128)S(1)} %add.8.total_ref), channel_id=1, source_target_pairs={{0,5},{1,4},{2,7},{3,6},{4,1},{5,0},{6,3},{7,2},{8,13},{9,12},{10,... | collective-permute-start | bytes 37052 | tf_op jit(solution)/shard_map/ppermute | solution.py:356
  30.8 4.2 %collective-permute-start.11 = (f32[9,343]{1,0:T(8,128)S(1)}, f32[9,343]{1,0:T(8,128)S(1)}, u32[]{:S(2)}, u32[]{:S(2)}) collective-permute-start(f32[9,343]{1,0:T(8,128)S(1)} %add.8.total_ref), channel_id=1, source_target_pairs={{0,7},{1,6},{2,5},{3,4},{4,3},{5,2},{6,1},{7,0},{8,15},{9,14},{10,... | collective-permute-start | bytes 37052 | tf_op jit(solution)/shard_map/ppermute | solution.py:356
  32.0 3.3 %collective-permute-start.9 = (f32[9,343]{1,0:T(8,128)S(1)}, f32[9,343]{1,0:T(8,128)S(1)}, u32[]{:S(2)}, u32[]{:S(2)}) collective-permute-start(f32[9,343]{1,0:T(8,128)S(1)} %add.8.total_ref), channel_id=1, source_target_pairs={{0,3},{1,2},{2,1},{3,0},{4,7},{5,6},{6,5},{7,4},{8,11},{9,10},{10,... | collective-permute-start | bytes 37052 | tf_op jit(solution)/shard_map/ppermute | solution.py:356
  32.5 5.1 %copy-start.4 = (f32[32]{0:T(128)S(1)}, f32[32]{0:T(128)}, u32[]{:S(2)}) copy-start(f32[32]{0:T(128)} %param.17) | copy-start | bytes 388
  35.9 3.9 %collective-permute-start.12 = (f32[32,256]{1,0:T(8,128)S(1)}, f32[32,256]{1,0:T(8,128)S(1)}, u32[]{:S(2)}, u32[]{:S(2)}) collective-permute-start(f32[32,256]{1,0:T(8,128)S(1)} %get-tuple-element.86), channel_id=1, source_target_pairs={{0,8},{1,9},{2,10},{3,11},{4,12},{5,13},{6,14},{7,15},{8,0},{9,1},... | collective-permute-start | bytes 98312 | tf_op jit(solution)/shard_map/ppermute | solution.py:348
  37.6 2.3 %collective-permute-start.13 = (f32[32,256]{1,0:T(8,128)S(1)}, f32[32,256]{1,0:T(8,128)S(1)}, u32[]{:S(2)}, u32[]{:S(2)}) collective-permute-start(f32[32,256]{1,0:T(8,128)S(1)} %get-tuple-element.86), channel_id=1, source_target_pairs={{0,1},{1,0},{2,3},{3,2},{4,5},{5,4},{6,7},{7,6},{8,16},{9,17},{10,... | collective-permute-start | bytes 98312 | tf_op jit(solution)/shard_map/ppermute | solution.py:348

commit v4 on v3

--- a/solution.py
+++ b/solution.py
@@ -62,22 +62,62 @@
     )(*args)
 
 
-def pick_kernel(w_in, face_in, links_in, matrix_in, w_ref, face_ref, links_ref, matrix_ref, table_ref, out_ref, sems):
-    pairs = ((w_in, w_ref), (face_in, face_ref), (links_in, links_ref), (matrix_in, matrix_ref))
+LANES = 128
+ROWS = 16
+ALONG = lax.GatherDimensionNumbers(
+    offset_dims=(),
+    collapsed_slice_dims=(1,),
+    start_index_map=(1,),
+    operand_batching_dims=(0,),
+    start_indices_batching_dims=(0,),
+)
+
+
+def along(block, lane):
+    return lax.gather(
+        block, lane[..., None], ALONG, slice_sizes=(1, 1),
+        mode=lax.GatherScatterMode.PROMISE_IN_BOUNDS,
+    )
+
+
+def gathered(source, lane, block, start=None):
+    out = jnp.zeros(lane.shape, source.dtype) if start is None else start
+    for number in range(source.shape[1] // LANES):
+        part = along(source[:, number * LANES : (number + 1) * LANES], lane)
+        out = jnp.where(block == number, part, out)
+    return out
+
+
+def gather_columns(source, lane_ref, block_ref, start, put):
+    rows = lane_ref.shape[0]
+    for column_start in range(0, lane_ref.shape[1], LANES):
+        columns = slice(column_start, column_start + LANES)
+        lane, block = lane_ref[:, columns], block_ref[:, columns]
+        for row in range(0, source.shape[0], rows):
+            begin = None if start is None else start[row : row + rows, columns]
+            put(slice(row, row + rows), columns, gathered(source[row : row + rows], lane, block, begin))
+
+
+def split_index(index, dtype):
+    return (index & (LANES - 1)).astype(dtype), (index >> 7).astype(dtype)
+
+
+def pick_kernel(w_in, face_in, links_in, w_ref, face_ref, links_ref, out_ref, sems):
+    pairs = ((w_in, w_ref), (face_in, face_ref), (links_in, links_ref))
     copies = [
         pltpu.make_async_copy(source, target, sems.at[i]) for i, (source, target) in enumerate(pairs)
     ]
     for copy in copies:
         copy.start()
-    owned = w_ref.shape[1]
+    for copy in copies:
+        copy.wait()
     count = face_ref.shape[1]
-    copies[1].wait()
-    table = one_hot(lax.broadcasted_iota(jnp.int32, (owned, count), 0) == face_ref[...])
-    table_ref[...] = table
-    copies[0].wait()
-    out_ref[...] = dot(w_ref[...], table).astype(bf16)
-    copies[2].wait()
-    copies[3].wait()
+    w = w_ref[...]
+    for start in range(0, count, LANES):
+        index = jnp.broadcast_to(face_ref[:, start : start + LANES], (ROWS, LANES))
+        lane, block = split_index(index, jnp.int16)
+        for row in range(0, w.shape[0], ROWS):
+            out_ref[row : row + ROWS, start : start + LANES] = gathered(w[row : row + ROWS], lane, block)
 
 
 def short_one_hot(left, right):
@@ -89,70 +129,78 @@
 
 
 def tables_kernel(
-    w_ref, face_ref, links_ref, matrix_ref, face_table_ref,
-    own_ref, edge_ref, from_own_ref, from_edge_ref, padded_ref, inner_ref, values_ref, state_ref,
-    row_ref, turn_ref, wide_ref,
-):
-    owned, slots = own_ref.shape
+    matrix_in, w_ref, face_ref, links_ref,
+    from_own_ref, from_edge_ref, padded_ref, own_lane, own_block, edge_lane, edge_block,
+    node_lane, node_block, inner_ref, values_ref, state_ref,
+    row_ref, turn_ref, wide_ref, table_ref, matrix_ref, sem,
+):
+    copy = pltpu.make_async_copy(matrix_in, matrix_ref, sem)
+    copy.start()
+    slots, owned = from_own_ref.shape
     count = face_ref.shape[1]
     cells, nodes = links_ref.shape
     pitch = slots // cells
-    strip, lanes = 16, 128
     short = jnp.int16
+    half = ROWS // 2
 
     row_ref[...] = jnp.full(row_ref.shape, -1, jnp.int32)
     turn_ref[...] = jnp.full(turn_ref.shape, -1.0, f32)
     for cell in range(cells):
         line = links_ref[cell : cell + 1, :]
-        row_ref[:, cell * pitch : cell * pitch + nodes] = jnp.broadcast_to(line, (strip, nodes))
+        row_ref[:, cell * pitch : cell * pitch + nodes] = jnp.broadcast_to(line, (half, nodes))
         turn_ref[cell : cell + 1, :nodes] = line.astype(f32)
-    links = row_ref[...].astype(short)
-
-    def own_rows(i, carry):
-        start = pl.multiple_of(i * strip, strip)
-        index = lax.broadcasted_iota(jnp.int32, (strip, lanes), 0) + (start + count)
-        own_ref[pl.ds(start, strip), :] = short_one_hot(across(index.astype(short), slots), links)
-        return carry
-
-    lax.fori_loop(0, owned // strip, own_rows, 0, unroll=4)
+
+    table_ref[...] = one_hot(lax.broadcasted_iota(jnp.int32, (owned, count), 0) == face_ref[...])
+    order = lax.broadcasted_iota(jnp.int32, (half, count), 1)
+    digits = jnp.concatenate([order >> 7, (order & (LANES - 1)) + 1], axis=0)
+    sums = dot_rows(digits.astype(f32).astype(bf16), table_ref[...])
+    place = sums[:half] * float(LANES) + sums[half:]
+    node_lane[...], node_block[...] = split_index(place.astype(jnp.int32) - 1, jnp.int32)
+    inner = jnp.where(place > 0.5, 0.0, 1.0)
+    inner_ref[...] = inner
+
+    for start in range(0, slots, LANES):
+        columns = slice(start, start + LANES)
+        index = row_ref[:, columns]
+        lane, block = split_index(index - count, jnp.int32)
+        own_lane[:, columns] = jnp.concatenate([lane, lane], axis=0).astype(short)
+        own_block[:, columns] = jnp.concatenate([block, block], axis=0).astype(short)
+        at_face = gathered(place, lane, block).astype(jnp.int32)
+        index = jnp.where(index < count, index, jnp.where(at_face > 0, at_face + (count - 1), -1))
+        lane, block = split_index(index, jnp.int32)
+        edge_lane[:, columns] = jnp.concatenate([lane, lane], axis=0).astype(short)
+        edge_block[:, columns] = jnp.concatenate([block, block], axis=0).astype(short)
+
     w = w_ref[...]
-    values_ref[...] = dot(w, own_ref[...]).astype(bf16)
-
-    ghost_index = lax.broadcasted_iota(jnp.int32, (count, 1), 0)
-    face_index = column(face_ref[...].astype(f32)).astype(jnp.int32) + count
-    for part, index in enumerate((ghost_index, face_index)):
-        for start in range(0, count, strip):
-            block = jnp.broadcast_to(index[start : start + strip], (strip, lanes)).astype(short)
-            edge_ref[part * count + start : part * count + start + strip, :] = short_one_hot(
-                across(block, slots), links
-            )
+    gather_columns(w, own_lane, own_block, None, functools.partial(store, values_ref))
+    state_ref[...] = w.astype(f32) * inner[:1]
 
     edge_row = jnp.concatenate(
         [
-            lax.broadcasted_iota(jnp.int32, (strip, count), 1),
-            jnp.broadcast_to(face_ref[...], (strip, count)) + count,
+            lax.broadcasted_iota(jnp.int32, (ROWS, count), 1),
+            jnp.broadcast_to(face_ref[...], (ROWS, count)) + count,
         ],
         axis=1,
     ).astype(short)
-    own_row = (lax.broadcasted_iota(jnp.int32, (strip, owned), 1) + count).astype(short)
+    own_row = (lax.broadcasted_iota(jnp.int32, (ROWS, owned), 1) + count).astype(short)
     turned = jnp.transpose(turn_ref[...])
     for cell in range(cells):
-        for start in range(0, pitch, strip):
-            block = jnp.broadcast_to(turned[start : start + strip, cell : cell + 1], (strip, lanes))
+        for start in range(0, pitch, ROWS):
+            block = jnp.broadcast_to(turned[start : start + ROWS, cell : cell + 1], (ROWS, LANES))
             block = block.astype(jnp.int32).astype(short)
-            rows = slice(cell * pitch + start, cell * pitch + start + strip)
+            rows = slice(cell * pitch + start, cell * pitch + start + ROWS)
             from_edge_ref[rows, :] = short_one_hot(across(block, 2 * count), edge_row)
             from_own_ref[rows, :] = short_one_hot(across(block, owned), own_row)
 
     wide_ref[...] = jnp.zeros_like(wide_ref)
+    copy.wait()
     for cell in range(cells):
         wide_ref[cell % 2, :nodes, :nodes] = matrix_ref[cell].astype(f32)
         padded_ref[cell] = wide_ref[cell % 2].astype(bf16)
 
-    named = dot_rows(jnp.ones((8, count), bf16), face_table_ref[...])
-    inner = 1.0 - named
-    inner_ref[...] = inner
-    state_ref[...] = w.astype(f32) * inner[:1]
+
+def store(ref, rows, columns, values):
+    ref[rows, columns] = values
 
 
 def cell_block(values, matrix_ref, cell):
@@ -179,17 +227,16 @@
 
 
 def first_kernel(
-    flags_ref, values_ref, got_first, got_second, matrix_ref, edge_ref, from_edge_ref,
-    parts_ref, first_ref, second_ref, state_ref,
+    flags_ref, inner_values_ref, got_first, got_second, edge_lane, edge_block, matrix_ref, from_edge_ref,
+    parts_ref, first_ref, second_ref, state_ref, values_ref,
 ):
     got, _ = chosen(flags_ref, got_first[...].astype(f32), got_second[...].astype(f32))
     got = jnp.where(flags_ref[0] > 0, got, jnp.zeros_like(got))
     state_ref[...] = got
-    count = got.shape[1]
-    values = values_ref[...].astype(f32) + dot(got.astype(bf16), edge_ref[:count, :])
-    send_sums(
-        flags_ref, values.astype(bf16), matrix_ref, from_edge_ref, parts_ref, first_ref, second_ref
-    )
+    gather_columns(
+        got.astype(bf16), edge_lane, edge_block, inner_values_ref, functools.partial(store, values_ref)
+    )
+    send_sums(flags_ref, values_ref[...], matrix_ref, from_edge_ref, parts_ref, first_ref, second_ref)
 
 
 def advance(scale, applied, state, before):
@@ -208,35 +255,42 @@
     return new_ghost, new_face
 
 
-def next_values(new_ghost, new_face, values_ref, edge_ref):
+def next_values(new_ghost, new_face, inner_values_ref, edge_lane, edge_block, values_ref):
     edge = jnp.concatenate([new_ghost.astype(bf16), new_face.astype(bf16)], axis=1)
-    return (values_ref[...].astype(f32) + dot(edge, edge_ref[...])).astype(bf16)
+    gather_columns(
+        edge, edge_lane, edge_block, inner_values_ref, functools.partial(store, values_ref)
+    )
 
 
 def edge_kernel(scale, with_before, flags_ref, got_first, got_second, sum_first, sum_second, ghost, face, *rest):
     before, rest = (rest[:2], rest[2:]) if with_before else (None, rest)
-    values_ref, matrix_ref, edge_ref, from_edge_ref, parts_ref, out_first, out_second, new_ghost, new_face = rest
+    inner_values_ref, edge_lane, edge_block, matrix_ref, from_edge_ref, *outs = rest
+    parts_ref, out_first, out_second, new_ghost, new_face, values_ref = outs
     ghost_value, face_value = edge_step(
         scale, flags_ref, got_first, got_second, sum_first, sum_second, ghost, face, before
     )
     new_ghost[...] = ghost_value
     new_face[...] = face_value
-    values = next_values(ghost_value, face_value, values_ref, edge_ref)
-    send_sums(flags_ref, values, matrix_ref, from_edge_ref, parts_ref, out_first, out_second)
+    next_values(ghost_value, face_value, inner_values_ref, edge_lane, edge_block, values_ref)
+    send_sums(flags_ref, values_ref[...], matrix_ref, from_edge_ref, parts_ref, out_first, out_second)
 
 
 def inner_kernel(scale, with_before, parts_ref, state_ref, *rest):
     before = rest[0][...] if with_before else None
-    own_ref, from_own_ref, inner_ref, new_ref, values_ref = rest[1:] if with_before else rest
+    own_lane, own_block, from_own_ref, inner_ref, new_ref, values_ref = (
+        rest[1:] if with_before else rest
+    )
     applied = joined(dot(parts_ref[...], from_own_ref[...]))
     new = advance(scale, applied, state_ref[...], before) * inner_ref[:1]
     new_ref[...] = new
-    values_ref[...] = dot(new.astype(bf16), own_ref[...]).astype(bf16)
+    gather_columns(
+        new.astype(bf16), own_lane, own_block, None, functools.partial(store, values_ref)
+    )
 
 
 def density_kernel(
     flags_ref, got_first, got_second, sum_first, sum_second, ghost, face, before_ghost, before_face,
-    values_ref, edge_ref, basis_ref, occupancy_ref,
+    inner_values_ref, edge_lane, edge_block, basis_ref, occupancy_ref,
     new_face, final_ref, at_ref, band_ref, *, scale, cells,
 ):
     ghost_value, face_value = edge_step(
@@ -244,8 +298,8 @@
         (before_ghost, before_face),
     )
     new_face[...] = face_value
-    values = next_values(ghost_value, face_value, values_ref, edge_ref)
-    final_ref[...] = values
+    next_values(ghost_value, face_value, inner_values_ref, edge_lane, edge_block, final_ref)
+    values = final_ref[...]
     nodes = basis_ref.shape[0]
     waves, slots = values.shape
     pitch = slots // cells
@@ -261,7 +315,7 @@
 
 
 def products_kernel(
-    values_ref, matrix_ref, basis_ref, face_ref, product_ref, wide_basis_ref, to_face_ref, wide_ref
+    values_ref, matrix_ref, basis_ref, product_ref, wide_basis_ref, wide_ref
 ):
     cells, pitch, _ = matrix_ref.shape
     values = values_ref[...]
@@ -271,8 +325,6 @@
     wide_ref[...] = jnp.zeros_like(wide_ref)
     wide_ref[:nodes, :] = basis_ref[...].astype(f32)
     wide_basis_ref[...] = wide_ref[...].astype(bf16)
-    index = column(face_ref[...].astype(f32)).astype(jnp.int32)
-    to_face_ref[...] = one_hot(lax.broadcasted_iota(jnp.int32, to_face_ref.shape, 1) == index)
 
 
 def cube_root(x):
@@ -317,21 +369,28 @@
 
 
 def residual_kernel(
-    parts_ref, state_ref, face_ref, ritz_ref, from_own_ref, to_face_ref, potential_ref,
-    out_ref, potential_out, sem,
+    parts_ref, state_ref, face_ref, ritz_ref, from_own_ref, potential_ref,
+    out_ref, shift_ref, potential_out, sem,
 ):
     copy = pltpu.make_async_copy(potential_ref, potential_out, sem)
     copy.start()
     ritz = column(ritz_ref[...])
-    faces = joined(dot(halves(ritz * face_ref[...]), to_face_ref[...]))
-    out_ref[...] = joined(dot(parts_ref[...], from_own_ref[...])) - ritz * state_ref[...] - faces
+    shift_ref[...] = ritz * face_ref[...]
+    out_ref[...] = joined(dot(parts_ref[...], from_own_ref[...])) - ritz * state_ref[...]
     copy.wait()
 
 
-def finish_kernel(flags_ref, got_first, got_second, partial_ref, to_face_ref, out_ref, hold_ref, sem):
+def finish_kernel(
+    flags_ref, got_first, got_second, partial_ref, shift_ref, node_lane, node_block,
+    out_ref, hold_ref, sem,
+):
     _, got = chosen(flags_ref, got_first[...], got_second[...])
-    got = jnp.where(flags_ref[1] > 0, got, jnp.zeros_like(got))
-    hold_ref[...] = partial_ref[...] + joined(dot(halves(got), to_face_ref[...]))
+    got = jnp.where(flags_ref[1] > 0, got, jnp.zeros_like(got)) - shift_ref[...]
+
+    def add(rows, columns, values):
+        hold_ref[rows, columns] = partial_ref[rows, columns] + values
+
+    gather_columns(got, node_lane, node_block, None, add)
     copy = pltpu.make_async_copy(hold_ref, out_ref, sem)
     copy.start()
     copy.wait()
@@ -403,43 +462,51 @@
     values_out = ((waves, slots), bf16)
     state_out = ((waves, owned), f32)
 
-    w, faces, links, matrix, face_table, start_face = call(
+    index_out = ((ROWS, slots), jnp.int16)
+    w, faces, links, start_face = call(
         pick_kernel,
         [
             (wavefunctions.shape, bf16),
             ((1, count), jnp.int32),
             (connectivity.shape, jnp.int32),
-            (cell_hamiltonian.shape, bf16),
-            ((owned, count), bf16),
             ((waves, count), bf16),
         ],
-        wavefunctions, face_nodes.reshape(1, count), connectivity, cell_hamiltonian,
-        held=4, scratch=[pltpu.SemaphoreType.DMA((4,))], room=56,
+        wavefunctions, face_nodes.reshape(1, count), connectivity,
+        held=3, scratch=[pltpu.SemaphoreType.DMA((3,))], room=56,
     )
     start_pair = exchanged(start_face, start_face)
-    own, edge, from_own, from_edge, padded, inner, values, state = call(
+    (
+        from_own, from_edge, padded, own_lane, own_block, edge_lane, edge_block,
+        node_lane, node_block, inner, values, state,
+    ) = call(
         tables_kernel,
         [
-            ((owned, slots), bf16),
-            ((2 * count, slots), bf16),
             ((slots, owned), bf16),
             ((slots, 2 * count), bf16),
             ((cells, pitch, pitch), bf16),
-            ((8, owned), f32),
+            *[index_out] * 4,
+            ((ROWS // 2, owned), jnp.int32),
+            ((ROWS // 2, owned), jnp.int32),
+            ((ROWS // 2, owned), f32),
             values_out,
             state_out,
         ],
-        w, faces, links, matrix, face_table,
+        cell_hamiltonian, w, faces, links,
+        held=1,
         scratch=[
-            pltpu.VMEM((16, slots), jnp.int32),
-            pltpu.VMEM((-(-cells // 128) * 128, pitch), f32),
+            pltpu.VMEM((ROWS // 2, slots), jnp.int32),
+            pltpu.VMEM((-(-cells // LANES) * LANES, pitch), f32),
             pltpu.VMEM((2, pitch, pitch), f32),
+            pltpu.VMEM((owned, count), bf16),
+            pltpu.VMEM(cell_hamiltonian.shape, bf16),
+            pltpu.SemaphoreType.DMA,
         ],
-    )
-    parts, *sums, ghost = call(
+        room=44,
+    )
+    parts, *sums, ghost, _ = call(
         first_kernel,
-        [parts_out, *edge_out, edge_out[0]],
-        flags, values, *start_pair, padded, edge, from_edge, smem=1,
+        [parts_out, *edge_out, edge_out[0], values_out],
+        flags, values, *start_pair, edge_lane, edge_block, padded, from_edge, smem=1,
     )
     face = start_face.astype(f32)
     before_edge, before_state = (), ()
@@ -449,28 +516,28 @@
         new_state, values = call(
             functools.partial(inner_kernel, scale, step > 0),
             [state_out, values_out],
-            parts, state, *before_state, own, from_own, inner,
+            parts, state, *before_state, own_lane, own_block, from_own, inner,
         )
         received = (flags, *got, *sums, ghost, face, *before_edge)
         if step < 2:
-            parts, *sums, new_ghost, new_face = call(
+            parts, *sums, new_ghost, new_face, _ = call(
                 functools.partial(edge_kernel, scale, step > 0),
-                [parts_out, *edge_out, *edge_out],
-                *received, values, padded, edge, from_edge, smem=1,
+                [parts_out, *edge_out, *edge_out, values_out],
+                *received, values, edge_lane, edge_block, padded, from_edge, smem=1,
             )
             before_edge, ghost, face = (ghost, face), new_ghost, new_face
         else:
             face, final, at, band = call(
                 functools.partial(density_kernel, scale=scale, cells=cells),
                 [edge_out[0], values_out, ((cells * waves, points), f32), ((cells, points), f32)],
-                *received, values, edge, basis_values, occupancy.reshape(1, waves), smem=1,
+                *received, values, edge_lane, edge_block, basis_values, occupancy.reshape(1, waves), smem=1,
             )
         before_state, state = (state,), new_state
         scale = 2.0 / spectrum_half
-    products, wide_basis, to_face = call(
+    products, wide_basis = call(
         products_kernel,
-        [((waves, slots), f32), ((pitch, points), bf16), ((count, owned), bf16)],
-        final, padded, basis_values, faces, scratch=[pltpu.VMEM((pitch, points), f32)],
+        [((waves, slots), f32), ((pitch, points), bf16)],
+        final, padded, basis_values, scratch=[pltpu.VMEM((pitch, points), f32)],
     )
     totals = band_parts(band, "band")
     potential, parts, sum_ghost = call(
@@ -479,14 +546,14 @@
         *totals, core_density, quad_weights, at, wide_basis, products, from_edge,
     )
     returned = exchanged(sum_ghost, sum_ghost)
-    partial, potential = call(
+    partial, shift, potential = call(
         residual_kernel,
-        [state_out, ((cells, points), f32)],
-        parts, state, face, ritz_values.reshape(1, waves), from_own, to_face, potential,
+        [state_out, edge_out[0], ((cells, points), f32)],
+        parts, state, face, ritz_values.reshape(1, waves), from_own, potential,
         sent=1, scratch=[pltpu.SemaphoreType.DMA],
     )
     (residual,) = call(
-        finish_kernel, [state_out], flags, *returned, partial, to_face,
+        finish_kernel, [state_out], flags, *returned, partial, shift, node_lane, node_block,
         smem=1, sent=1, scratch=[pltpu.VMEM(*state_out), pltpu.SemaphoreType.DMA],
     )
     return (residual, potential)

time: 41.5 us -> 41.8 us (level)
  Pallas kernels: 20.8 us -> 19 us
  waiting for transfers between devices: 3.99 us -> 5.32 us
  starting transfers between devices: 15.6 us -> 16.5 us
    pallas_call x13, Pallas kernels: 20.8 us -> 19 us  [call(): pl.pallas_call(kernel, out_shape=[pltpu.VMEM(*out) for out in outs[:kept]...]
    ppermute x10, starting transfers between devices: 11.9 us -> 13.1 us  [paired(): return lax.ppermute(x, ('space', 'band'), route)]
    ppermute x10, waiting for transfers between devices: 0.76 us -> 1.83 us  [paired(): return lax.ppermute(x, ('space', 'band'), route)]
  transfers between devices with their start and end apart: 14 -> 14, of which waited for: 4 -> 8; matrix products, arithmetic and copies ran while one was open for 0% -> 0% of each run, Pallas kernels for 28% -> 21%
where the time goes in v4:
time: 41.8 us; the launch traced here: 41.7 us
  Pallas kernels  19 us (45%)
  starting transfers between devices  16.5 us (39%)
  waiting for transfers between devices  5.32 us (13%)
  between operations  0.72 us (2%)
    pallas_call x13, Pallas kernels, call(): pl.pallas_call(kernel, out_shape=[pltpu.VMEM(*out) for out in outs[:kept]...  19 us
    ppermute x10, starting transfers between devices, paired(): return lax.ppermute(x, ('space', 'band'), route)  13.1 us
    ppermute x4, waiting for transfers between devices, swapped(): lax.ppermute(x, axis, [(i, i ^ mask) for i in range(lax.axis_size(axis))])  3.48 us
    ppermute x4, starting transfers between devices, swapped(): lax.ppermute(x, axis, [(i, i ^ mask) for i in range(lax.axis_size(axis))])  3.37 us
    ppermute x10, waiting for transfers between devices, paired(): return lax.ppermute(x, ('space', 'band'), route)  1.83 us
  transfers between devices with their start and end apart: 14, of which 8 were waited for; matrix products, arithmetic and copies ran while one was open for 0% of the time, Pallas kernels for 21%

profile of v4, /device:TPU:0, one launch (start us, length us, event | category | flops | bytes accessed | tf_op | source)
XLA Modules:
  0.0 41.7 jit_solution(1986318526358704369)
XLA Ops:
  0.6 1.0 %shard_map.104 = (bf16[32,1280]{1,0:T(8,128)(2,1)S(1)}, s32[1,256]{1,0:T(1,128)S(1)}, s32[9,216]{1,0:T(8,128)S(1)}, bf16[32,256]{1,0:T(8,128)(2,1)S(1)}) custom-call(bf16[32,1280]{1,0:T(8,128)(2,1)} %w_in.1, s32[1,256]{1,0:T(1,128)} %bitcast.8, s32[9,216]{1,0:T(8,128)} %links_in.1), custom_call_target="tpu_custom_call" | custom-call | flops 268435456 | bytes 1048576 | tf_op jit(solution)/shard_map/pallas_call | solution.py:53
  1.7 0.5 %collective-permute-start.1 = (bf16[32,256]{1,0:T(8,128)(2,1)S(1)}, bf16[32,256]{1,0:T(8,128)(2,1)S(1)}, u32[]{:S(2)}, u32[]{:S(2)}) collective-permute-start(bf16[32,256]{1,0:T(8,128)(2,1)S(1)} %get-tuple-element.54), channel_id=1, source_target_pairs={{0,1},{1,0},{2,3},{3,2},{4,5},{5,4},{6,7},{7,6},{8,16},{9,17},{10,... | collective-permute-start | bytes 49160 | tf_op jit(solution)/shard_map/ppermute | solution.py:407
  2.2 4.1 %collective-permute-start = (bf16[32,256]{1,0:T(8,128)(2,1)S(1)}, bf16[32,256]{1,0:T(8,128)(2,1)S(1)}, u32[]{:S(2)}, u32[]{:S(2)}) collective-permute-start(bf16[32,256]{1,0:T(8,128)(2,1)S(1)} %get-tuple-element.54), channel_id=1, source_target_pairs={{0,8},{1,9},{2,10},{3,11},{4,12},{5,13},{6,14},{7,15},{8,0},{9,1},... | collective-permute-start | bytes 49160 | tf_op jit(solution)/shard_map/ppermute | solution.py:407
  6.3 0.1 add_convert_fusion.flags_ref
  6.4 2.3 %shard_map.105 = (bf16[2304,1280]{1,0:T(8,128)(2,1)S(1)}, bf16[2304,512]{1,0:T(8,128)(2,1)S(1)}, bf16[9,256,256]{2,1,0:T(8,128)(2,1)S(1)}, s16[16,2304]{1,0:T(8,...) custom-call(bf16[9,216,216]{2,1,0:T(8,128)(2,1)} %matrix_in.1, ...), custom_call_target="tpu_custom_call" | custom-call | flops 268435456 | bytes 1048576 | tf_op jit(solution)/shard_map/pallas_call | solution.py:53
  8.7 0.0 collective-permute-done.1.got_second
  8.7 0.0 collective-permute-done.got_first
  8.7 1.9 %shard_map.106 = (bf16[64,2304]{1,0:T(8,128)(2,1)S(1)}, f32[32,256]{1,0:T(8,128)S(1)}, f32[32,256]{1,0:T(8,128)S(1)}, f32[32,256]{1,0:T(8,128)S(1)}, bf16[32,2304]{1,0:T(8,128)(2,1)}) custom-call(s32[3]{0:T(128)S(1)} %add_convert_fusion.flags_ref, bf16[32,2304]{1,0:T(8,128)(2,1)S(1)} %get-tuple-element.53.inner_values_ref, ...), custom_call_target="tpu_custom_call" | custom-call | flops 268435456 | bytes 1048576 | tf_op jit(solution)/shard_map/pallas_call | solution.py:53
  10.6 1.4 %collective-permute-start.2 = (f32[32,256]{1,0:T(8,128)S(1)}, f32[32,256]{1,0:T(8,128)S(1)}, u32[]{:S(2)}, u32[]{:S(2)}) collective-permute-start(f32[32,256]{1,0:T(8,128)S(1)} %get-tuple-element.59.sum_first), channel_id=1, source_target_pairs={{0,8},{1,9},{2,10},{3,11},{4,12},{5,13},{6,14},{7,15},{8,0},{9,1},... | collective-permute-start | bytes 98312 | tf_op jit(solution)/shard_map/ppermute | solution.py:407
  12.0 0.0 collective-permute-start.3
  12.0 1.6 %shard_map.107 = (f32[32,1280]{1,0:T(8,128)S(1)}, bf16[32,2304]{1,0:T(8,128)(2,1)S(1)}) custom-call(bf16[64,2304]{1,0:T(8,128)(2,1)S(1)} %get-tuple-element.62.parts_ref, f32[32,1280]{1,0:T(8,128)S(1)} %get-tuple-element.63.state_ref.rest_0_, s16[16,2304]{1,0:T(8,128)(2,1)S(1)} %get-tuple-element.64.rest_0_.rest_1_, ...), custom_call_target="tpu_custom_call" | custom-call | flops 268435456 | bytes 1048576 | tf_op jit(solution)/shard_map/pallas_call | solution.py:53
  13.6 1.0 %collective-permute-done.2.got_first = f32[32,256]{1,0:T(8,128)S(1)} collective-permute-done((f32[32,256]{1,0:T(8,128)S(1)}, f32[32,256]{1,0:T(8,128)S(1)}, u32[]{:S(2)}, u32[]{:S(2)}) %collective-permute-start.2) | collective-permute-done | bytes 32800 | tf_op jit(solution)/shard_map/ppermute | solution.py:407
  14.5 0.0 collective-permute-done.3.got_second
  14.5 2.0 %shard_map.108 = (bf16[64,2304]{1,0:T(8,128)(2,1)S(1)}, f32[32,256]{1,0:T(8,128)S(1)}, f32[32,256]{1,0:T(8,128)S(1)}, f32[32,256]{1,0:T(8,128)S(1)}, f32[32,256]{1,0:T(8,128)S(1)}, /*index=5*/bf16[32,2304]{1,0:T(8,128)(2,1)}) custom-call(s32[3]{0:T(128)S(1)} %add_convert_fusion.flags_ref, f32[32,256]{1,0:T(8,128)S(1)} %collective-permute-done.2.got_first, ...), custom_call_target="tpu_custom_call" | custom-call | flops 268435456 | bytes 1048576 | tf_op jit(solution)/shard_map/pallas_call | solution.py:53
  16.5 2.0 %collective-permute-start.4 = (f32[32,256]{1,0:T(8,128)S(1)}, f32[32,256]{1,0:T(8,128)S(1)}, u32[]{:S(2)}, u32[]{:S(2)}) collective-permute-start(f32[32,256]{1,0:T(8,128)S(1)} %get-tuple-element.69.sum_first), channel_id=1, source_target_pairs={{0,8},{1,9},{2,10},{3,11},{4,12},{5,13},{6,14},{7,15},{8,0},{9,1},... | collective-permute-start | bytes 98312 | tf_op jit(solution)/shard_map/ppermute | solution.py:407
  18.6 0.0 collective-permute-start.5
  18.6 1.6 %shard_map.109 = (f32[32,1280]{1,0:T(8,128)S(1)}, bf16[32,2304]{1,0:T(8,128)(2,1)S(1)}) custom-call(bf16[64,2304]{1,0:T(8,128)(2,1)S(1)} %get-tuple-element.73.parts_ref, f32[32,1280]{1,0:T(8,128)S(1)} %get-tuple-element.74.state_ref.rest_0_, f32[32,1280]{1,0:T(8,128)S(1)} %get-tuple-element.63.state_ref.rest_0_, ...), custom_call_target="tpu_custom_call" | custom-call | flops 268435456 | bytes 1048576 | tf_op jit(solution)/shard_map/pallas_call | solution.py:53
  20.1 0.3 collective-permute-done.4.got_first
  20.5 0.0 collective-permute-done.5.got_second
  20.5 2.0 %shard_map.110 = (bf16[64,2304]{1,0:T(8,128)(2,1)S(1)}, f32[32,256]{1,0:T(8,128)S(1)}, f32[32,256]{1,0:T(8,128)S(1)}, f32[32,256]{1,0:T(8,128)S(1)}, f32[32,256]{1,0:T(8,128)S(1)}, /*index=5*/bf16[32,2304]{1,0:T(8,128)(2,1)}) custom-call(s32[3]{0:T(128)S(1)} %add_convert_fusion.flags_ref, f32[32,256]{1,0:T(8,128)S(1)} %collective-permute-done.4.got_first, ...), custom_call_target="tpu_custom_call" | custom-call | flops 268435456 | bytes 1048576 | tf_op jit(solution)/shard_map/pallas_call | solution.py:53
  22.5 2.0 %collective-permute-start.6 = (f32[32,256]{1,0:T(8,128)S(1)}, f32[32,256]{1,0:T(8,128)S(1)}, u32[]{:S(2)}, u32[]{:S(2)}) collective-permute-start(f32[32,256]{1,0:T(8,128)S(1)} %get-tuple-element.76.sum_first), channel_id=1, source_target_pairs={{0,8},{1,9},{2,10},{3,11},{4,12},{5,13},{6,14},{7,15},{8,0},{9,1},... | collective-permute-start | bytes 98312 | tf_op jit(solution)/shard_map/ppermute | solution.py:407
  24.5 0.0 collective-permute-start.7
  24.5 1.6 %shard_map.111 = (f32[32,1280]{1,0:T(8,128)S(1)}, bf16[32,2304]{1,0:T(8,128)(2,1)S(1)}) custom-call(bf16[64,2304]{1,0:T(8,128)(2,1)S(1)} %get-tuple-element.80.parts_ref, f32[32,1280]{1,0:T(8,128)S(1)} %get-tuple-element.81.state_ref, f32[32,1280]{1,0:T(8,128)S(1)} %get-tuple-element.74.state_ref.rest_0_, ...), custom_call_target="tpu_custom_call" | custom-call | flops 268435456 | bytes 1048576 | tf_op jit(solution)/shard_map/pallas_call | solution.py:53
  26.1 0.0 copy-start.2
  26.1 0.3 collective-permute-done.6.got_first
  26.4 0.0 collective-permute-done.7.got_second
  26.4 0.0 copy-done
  26.4 0.0 copy-done.4
  26.4 1.1 %shard_map.112 = (f32[32,256]{1,0:T(8,128)S(1)}, bf16[32,2304]{1,0:T(8,128)(2,1)S(1)}, f32[288,343]{1,0:T(8,128)S(1)}, f32[9,343]{1,0:T(8,128)S(1)}) custom-call(s32[3]{0:T(128)S(1)} %add_convert_fusion.flags_ref, f32[32,256]{1,0:T(8,128)S(1)} %collective-permute-done.6.got_first, f32[32,256]{1,0:T(8,128)S(1)} %collective-permute-done.7.got_second, ...), custom_call_target="tpu_custom_call" | custom-call | flops 268435456 | bytes 1048576 | tf_op jit(solution)/shard_map/pallas_call | solution.py:53
  27.5 0.3 collective-permute-start.8
  27.8 0.9 %collective-permute-done.8 = f32[9,343]{1,0:T(8,128)S(1)} collective-permute-done((f32[9,343]{1,0:T(8,128)S(1)}, f32[9,343]{1,0:T(8,128)S(1)}, u32[]{:S(2)}, u32[]{:S(2)}) %collective-permute-start.8) | collective-permute-done | bytes 12380 | tf_op jit(solution)/shard_map/ppermute | solution.py:415
  28.8 2.3 %collective-permute-start.11 = (f32[9,343]{1,0:T(8,128)S(1)}, f32[9,343]{1,0:T(8,128)S(1)}, u32[]{:S(2)}, u32[]{:S(2)}) collective-permute-start(f32[9,343]{1,0:T(8,128)S(1)} %add.8.total_ref), channel_id=1, source_target_pairs={{0,7},{1,6},{2,5},{3,4},{4,3},{5,2},{6,1},{7,0},{8,15},{9,14},{10,... | collective-permute-start | bytes 37052 | tf_op jit(solution)/shard_map/ppermute | solution.py:415
  31.1 0.4 collective-permute-start.10
  31.5 0.4 collective-permute-start.9
  31.8 0.3 shard_map.113
  32.2 0.8 %collective-permute-done.11.rest_2_ = f32[9,343]{1,0:T(8,128)S(1)} collective-permute-done((f32[9,343]{1,0:T(8,128)S(1)}, f32[9,343]{1,0:T(8,128)S(1)}, u32[]{:S(2)}, u32[]{:S(2)}) %collective-permute-start.11) | collective-permute-done | bytes 12380 | tf_op jit(solution)/shard_map/ppermute | solution.py:415
  32.9 1.4 %collective-permute-done.10.rest_1_ = f32[9,343]{1,0:T(8,128)S(1)} collective-permute-done((f32[9,343]{1,0:T(8,128)S(1)}, f32[9,343]{1,0:T(8,128)S(1)}, u32[]{:S(2)}, u32[]{:S(2)}) %collective-permute-start.10) | collective-permute-done | bytes 12380 | tf_op jit(solution)/shard_map/ppermute | solution.py:415
  34.3 0.4 collective-permute-done.9.rest_0_
  34.7 0.0 copy-done.1
  34.7 0.0 copy-done.2
  34.7 0.6 %shard_map.114 = (f32[9,343]{1,0:T(8,128)S(1)}, bf16[64,2304]{1,0:T(8,128)(2,1)S(1)}, f32[32,256]{1,0:T(8,128)S(1)}) custom-call(f32[9,343]{1,0:T(8,128)S(1)} %add.8.total_ref, f32[9,343]{1,0:T(8,128)S(1)} %collective-permute-done.9.rest_0_, f32[9,343]{1,0:T(8,128)S(1)} %collective-permute-done.10.rest_1_, f32[9,343]{1,0:T(8,128)S(1)} %collective-permute-done.11.rest_2_, ...), custom_call_target="tpu_custom_call" | custom-call | flops 268435456 | bytes 1048576 | tf_op jit(solution)/shard_map/pallas_call | solution.py:53
  35.3 0.3 collective-permute-start.13
  35.6 2.8 %collective-permute-start.12 = (f32[32,256]{1,0:T(8,128)S(1)}, f32[32,256]{1,0:T(8,128)S(1)}, u32[]{:S(2)}, u32[]{:S(2)}) collective-permute-start(f32[32,256]{1,0:T(8,128)S(1)} %get-tuple-element.88), channel_id=1, source_target_pairs={{0,8},{1,9},{2,10},{3,11},{4,12},{5,13},{6,14},{7,15},{8,0},{9,1},... | collective-permute-start | bytes 98312 | tf_op jit(solution)/shard_map/ppermute | solution.py:407
  38.4 0.0 copy-done.3
  38.4 1.6 %shard_map.115 = (f32[32,1280]{1,0:T(8,128)S(1)}, f32[32,256]{1,0:T(8,128)S(1)}, f32[9,343]{1,0:T(8,128)}) custom-call(bf16[64,2304]{1,0:T(8,128)(2,1)S(1)} %get-tuple-element.89.parts_ref, f32[32,1280]{1,0:T(8,128)S(1)} %get-tuple-element.90.state_ref, f32[32,256]{1,0:T(8,128)S(1)} %get-tuple-element.91.face_ref, f32[1,32]{1,0:T(1,128)S(1)} %bitcast.6, ...), custom_call_target="tpu_custom_call" | custom-call | flops 268435456 | bytes 1048576 | tf_op jit(solution)/shard_map/pallas_call | solution.py:53
  40.0 0.0 collective-permute-done.13.got_second
  40.0 0.2 collective-permute-done.12.got_first
  40.3 1.4 %shard_map.116 = f32[32,1280]{1,0:T(8,128)} custom-call(s32[3]{0:T(128)S(1)} %add_convert_fusion.flags_ref, f32[32,256]{1,0:T(8,128)S(1)} %collective-permute-done.12.got_first, f32[32,256]{1,0:T(8,128)S(1)} %collective-permute-done.13.got_second, f32[32,1280]{1,0:T(8,128)S(1)} %get-tuple-element.93.partial_ref, f32[32,256]{1,0:T(8,128)S(1)} %get-tuple-element.94.shift_ref, ...), custom_call_target="tpu_custom_call" | custom-call | flops 268435456 | bytes 1048576 | tf_op jit(solution)/shard_map/pallas_call | solution.py:53
  (6 shorter events, 0.0 us)
Async XLA Ops:
  1.7 7.0 %collective-permute-start.1 = (bf16[32,256]{1,0:T(8,128)(2,1)S(1)}, bf16[32,256]{1,0:T(8,128)(2,1)S(1)}, u32[]{:S(2)}, u32[]{:S(2)}) collective-permute-start(bf16[32,256]{1,0:T(8,128)(2,1)S(1)} %get-tuple-element.54), channel_id=1, source_target_pairs={{0,1},{1,0},{2,3},{3,2},{4,5},{5,4},{6,7},{7,6},{8,16},{9,17},{10,... | collective-permute-start | bytes 49160 | tf_op jit(solution)/shard_map/ppermute | solution.py:407
  2.2 6.5 %collective-permute-start = (bf16[32,256]{1,0:T(8,128)(2,1)S(1)}, bf16[32,256]{1,0:T(8,128)(2,1)S(1)}, u32[]{:S(2)}, u32[]{:S(2)}) collective-permute-start(bf16[32,256]{1,0:T(8,128)(2,1)S(1)} %get-tuple-element.54), channel_id=1, source_target_pairs={{0,8},{1,9},{2,10},{3,11},{4,12},{5,13},{6,14},{7,15},{8,0},{9,1},... | collective-permute-start | bytes 49160 | tf_op jit(solution)/shard_map/ppermute | solution.py:407
  10.6 3.9 %collective-permute-start.2 = (f32[32,256]{1,0:T(8,128)S(1)}, f32[32,256]{1,0:T(8,128)S(1)}, u32[]{:S(2)}, u32[]{:S(2)}) collective-permute-start(f32[32,256]{1,0:T(8,128)S(1)} %get-tuple-element.59.sum_first), channel_id=1, source_target_pairs={{0,8},{1,9},{2,10},{3,11},{4,12},{5,13},{6,14},{7,15},{8,0},{9,1},... | collective-permute-start | bytes 98312 | tf_op jit(solution)/shard_map/ppermute | solution.py:407
  12.0 2.6 %collective-permute-start.3 = (f32[32,256]{1,0:T(8,128)S(1)}, f32[32,256]{1,0:T(8,128)S(1)}, u32[]{:S(2)}, u32[]{:S(2)}) collective-permute-start(f32[32,256]{1,0:T(8,128)S(1)} %get-tuple-element.60.sum_second), channel_id=1, source_target_pairs={{0,1},{1,0},{2,3},{3,2},{4,5},{5,4},{6,7},{7,6},{8,16},{9,17},{10,... | collective-permute-start | bytes 98312 | tf_op jit(solution)/shard_map/ppermute | solution.py:407
  16.5 3.9 %collective-permute-start.4 = (f32[32,256]{1,0:T(8,128)S(1)}, f32[32,256]{1,0:T(8,128)S(1)}, u32[]{:S(2)}, u32[]{:S(2)}) collective-permute-start(f32[32,256]{1,0:T(8,128)S(1)} %get-tuple-element.69.sum_first), channel_id=1, source_target_pairs={{0,8},{1,9},{2,10},{3,11},{4,12},{5,13},{6,14},{7,15},{8,0},{9,1},... | collective-permute-start | bytes 98312 | tf_op jit(solution)/shard_map/ppermute | solution.py:407
  18.6 1.9 %collective-permute-start.5 = (f32[32,256]{1,0:T(8,128)S(1)}, f32[32,256]{1,0:T(8,128)S(1)}, u32[]{:S(2)}, u32[]{:S(2)}) collective-permute-start(f32[32,256]{1,0:T(8,128)S(1)} %get-tuple-element.70.sum_second), channel_id=1, source_target_pairs={{0,1},{1,0},{2,3},{3,2},{4,5},{5,4},{6,7},{7,6},{8,16},{9,17},{10,... | collective-permute-start | bytes 98312 | tf_op jit(solution)/shard_map/ppermute | solution.py:407
  22.5 3.9 %collective-permute-start.6 = (f32[32,256]{1,0:T(8,128)S(1)}, f32[32,256]{1,0:T(8,128)S(1)}, u32[]{:S(2)}, u32[]{:S(2)}) collective-permute-start(f32[32,256]{1,0:T(8,128)S(1)} %get-tuple-element.76.sum_first), channel_id=1, source_target_pairs={{0,8},{1,9},{2,10},{3,11},{4,12},{5,13},{6,14},{7,15},{8,0},{9,1},... | collective-permute-start | bytes 98312 | tf_op jit(solution)/shard_map/ppermute | solution.py:407
  24.5 1.9 %collective-permute-start.7 = (f32[32,256]{1,0:T(8,128)S(1)}, f32[32,256]{1,0:T(8,128)S(1)}, u32[]{:S(2)}, u32[]{:S(2)}) collective-permute-start(f32[32,256]{1,0:T(8,128)S(1)} %get-tuple-element.77.sum_second), channel_id=1, source_target_pairs={{0,1},{1,0},{2,3},{3,2},{4,5},{5,4},{6,7},{7,6},{8,16},{9,17},{10,... | collective-permute-start | bytes 98312 | tf_op jit(solution)/shard_map/ppermute | solution.py:407
  24.5 1.9 %copy-start = (bf16[216,343]{1,0:T(8,128)(2,1)S(1)}, bf16[216,343]{1,0:T(8,128)(2,1)}, u32[]{:S(2)}) copy-start(bf16[216,343]{1,0:T(8,128)(2,1)} %basis_ref.3) | copy-start | bytes 444532
  24.5 1.9 %copy-start.4 = (f32[32]{0:T(128)S(1)}, f32[32]{0:T(128)}, u32[]{:S(2)}) copy-start(f32[32]{0:T(128)} %param.16) | copy-start | bytes 388
  26.1 8.6 %copy-start.1 = (f32[9,343]{1,0:T(8,128)S(1)}, f32[9,343]{1,0:T(8,128)}, u32[]{:S(2)}) copy-start(f32[9,343]{1,0:T(8,128)} %rest_3_.1) | copy-start | bytes 37048
  26.1 8.6 %copy-start.2 = (f32[9,343]{1,0:T(8,128)S(1)}, f32[9,343]{1,0:T(8,128)}, u32[]{:S(2)}) copy-start(f32[9,343]{1,0:T(8,128)} %rest_4_.1) | copy-start | bytes 37048
  27.5 1.3 %collective-permute-start.8 = (f32[9,343]{1,0:T(8,128)S(1)}, f32[9,343]{1,0:T(8,128)S(1)}, u32[]{:S(2)}, u32[]{:S(2)}) collective-permute-start(f32[9,343]{1,0:T(8,128)S(1)} %get-tuple-element.83), channel_id=1, source_target_pairs={{0,1},{1,0},{2,3},{3,2},{4,5},{5,4},{6,7},{7,6},{8,9},{9,8},{10,11... | collective-permute-start | bytes 37052 | tf_op jit(solution)/shard_map/ppermute | solution.py:415
  28.8 4.2 %collective-permute-start.11 = (f32[9,343]{1,0:T(8,128)S(1)}, f32[9,343]{1,0:T(8,128)S(1)}, u32[]{:S(2)}, u32[]{:S(2)}) collective-permute-start(f32[9,343]{1,0:T(8,128)S(1)} %add.8.total_ref), channel_id=1, source_target_pairs={{0,7},{1,6},{2,5},{3,4},{4,3},{5,2},{6,1},{7,0},{8,15},{9,14},{10,... | collective-permute-start | bytes 37052 | tf_op jit(solution)/shard_map/ppermute | solution.py:415
  31.1 3.3 %collective-permute-start.10 = (f32[9,343]{1,0:T(8,128)S(1)}, f32[9,343]{1,0:T(8,128)S(1)}, u32[]{:S(2)}, u32[]{:S(2)}) collective-permute-start(f32[9,343]{1,0:T(8,128)S(1)} %add.8.total_ref), channel_id=1, source_target_pairs={{0,5},{1,4},{2,7},{3,6},{4,1},{5,0},{6,3},{7,2},{8,13},{9,12},{10,... | collective-permute-start | bytes 37052 | tf_op jit(solution)/shard_map/ppermute | solution.py:415
  31.5 3.3 %collective-permute-start.9 = (f32[9,343]{1,0:T(8,128)S(1)}, f32[9,343]{1,0:T(8,128)S(1)}, u32[]{:S(2)}, u32[]{:S(2)}) collective-permute-start(f32[9,343]{1,0:T(8,128)S(1)} %add.8.total_ref), channel_id=1, source_target_pairs={{0,3},{1,2},{2,1},{3,0},{4,7},{5,6},{6,5},{7,4},{8,11},{9,10},{10,... | collective-permute-start | bytes 37052 | tf_op jit(solution)/shard_map/ppermute | solution.py:415
  31.8 6.5 %copy-start.3 = (f32[32]{0:T(128)S(1)}, f32[32]{0:T(128)}, u32[]{:S(2)}) copy-start(f32[32]{0:T(128)} %param.17) | copy-start | bytes 388
  35.3 4.7 %collective-permute-start.13 = (f32[32,256]{1,0:T(8,128)S(1)}, f32[32,256]{1,0:T(8,128)S(1)}, u32[]{:S(2)}, u32[]{:S(2)}) collective-permute-start(f32[32,256]{1,0:T(8,128)S(1)} %get-tuple-element.88), channel_id=1, source_target_pairs={{0,1},{1,0},{2,3},{3,2},{4,5},{5,4},{6,7},{7,6},{8,16},{9,17},{10,... | collective-permute-start | bytes 98312 | tf_op jit(solution)/shard_map/ppermute | solution.py:407
  35.6 4.7 %collective-permute-start.12 = (f32[32,256]{1,0:T(8,128)S(1)}, f32[32,256]{1,0:T(8,128)S(1)}, u32[]{:S(2)}, u32[]{:S(2)}) collective-permute-start(f32[32,256]{1,0:T(8,128)S(1)} %get-tuple-element.88), channel_id=1, source_target_pairs={{0,8},{1,9},{2,10},{3,11},{4,12},{5,13},{6,14},{7,15},{8,0},{9,1},... | collective-permute-start | bytes 98312 | tf_op jit(solution)/shard_map/ppermute | solution.py:407

commit v5 on v4

--- a/solution.py
+++ b/solution.py
@@ -102,7 +102,7 @@
     return (index & (LANES - 1)).astype(dtype), (index >> 7).astype(dtype)
 
 
-def pick_kernel(w_in, face_in, links_in, w_ref, face_ref, links_ref, out_ref, sems):
+def pick_kernel(w_in, face_in, links_in, w_ref, face_ref, links_ref, out_ref, twin_ref, sems):
     pairs = ((w_in, w_ref), (face_in, face_ref), (links_in, links_ref))
     copies = [
         pltpu.make_async_copy(source, target, sems.at[i]) for i, (source, target) in enumerate(pairs)
@@ -117,7 +117,9 @@
         index = jnp.broadcast_to(face_ref[:, start : start + LANES], (ROWS, LANES))
         lane, block = split_index(index, jnp.int16)
         for row in range(0, w.shape[0], ROWS):
-            out_ref[row : row + ROWS, start : start + LANES] = gathered(w[row : row + ROWS], lane, block)
+            picked = gathered(w[row : row + ROWS], lane, block)
+            out_ref[row : row + ROWS, start : start + LANES] = picked
+            twin_ref[row : row + ROWS, start : start + LANES] = picked
 
 
 def short_one_hot(left, right):
@@ -217,10 +219,33 @@
     return jnp.where(even, second, first), jnp.where(even, first, second)
 
 
-def send_sums(flags_ref, values, matrix_ref, from_edge_ref, parts_ref, first_ref, second_ref):
+def cell_values(edge, inner_values_ref, edge_lane, edge_block, cell, pitch):
+    tiles = []
+    for start in range(cell * pitch, (cell + 1) * pitch, LANES):
+        columns = slice(start, start + LANES)
+        lane, block = edge_lane[:, columns], edge_block[:, columns]
+        tiles.append(
+            jnp.concatenate(
+                [
+                    gathered(
+                        edge[row : row + ROWS], lane, block, inner_values_ref[row : row + ROWS, columns]
+                    )
+                    for row in range(0, edge.shape[0], ROWS)
+                ],
+                axis=0,
+            )
+        )
+    return jnp.concatenate(tiles, axis=1)
+
+
+def send_sums(
+    flags_ref, edge, inner_values_ref, edge_lane, edge_block, matrix_ref, from_edge_ref,
+    parts_ref, first_ref, second_ref,
+):
     cells, pitch, _ = matrix_ref.shape
     for cell in range(cells):
-        put_parts(parts_ref, cell, pitch, cell_block(values, matrix_ref, cell))
+        values = cell_values(edge, inner_values_ref, edge_lane, edge_block, cell, pitch)
+        parts_ref[:, cell * pitch : (cell + 1) * pitch] = halves(dot(values, matrix_ref[cell]))
     sums = joined(dot(parts_ref[...], from_edge_ref[...]))
     count = first_ref.shape[1]
     first_ref[...], second_ref[...] = chosen(flags_ref, sums[:, :count], sums[:, count:])
@@ -228,15 +253,15 @@
 
 def first_kernel(
     flags_ref, inner_values_ref, got_first, got_second, edge_lane, edge_block, matrix_ref, from_edge_ref,
-    parts_ref, first_ref, second_ref, state_ref, values_ref,
+    parts_ref, first_ref, second_ref, state_ref,
 ):
     got, _ = chosen(flags_ref, got_first[...].astype(f32), got_second[...].astype(f32))
     got = jnp.where(flags_ref[0] > 0, got, jnp.zeros_like(got))
     state_ref[...] = got
-    gather_columns(
-        got.astype(bf16), edge_lane, edge_block, inner_values_ref, functools.partial(store, values_ref)
-    )
-    send_sums(flags_ref, values_ref[...], matrix_ref, from_edge_ref, parts_ref, first_ref, second_ref)
+    send_sums(
+        flags_ref, got.astype(bf16), inner_values_ref, edge_lane, edge_block, matrix_ref, from_edge_ref,
+        parts_ref, first_ref, second_ref,
+    )
 
 
 def advance(scale, applied, state, before):
@@ -255,24 +280,23 @@
     return new_ghost, new_face
 
 
-def next_values(new_ghost, new_face, inner_values_ref, edge_lane, edge_block, values_ref):
-    edge = jnp.concatenate([new_ghost.astype(bf16), new_face.astype(bf16)], axis=1)
-    gather_columns(
-        edge, edge_lane, edge_block, inner_values_ref, functools.partial(store, values_ref)
-    )
+def edge_values(new_ghost, new_face):
+    return jnp.concatenate([new_ghost.astype(bf16), new_face.astype(bf16)], axis=1)
 
 
 def edge_kernel(scale, with_before, flags_ref, got_first, got_second, sum_first, sum_second, ghost, face, *rest):
     before, rest = (rest[:2], rest[2:]) if with_before else (None, rest)
     inner_values_ref, edge_lane, edge_block, matrix_ref, from_edge_ref, *outs = rest
-    parts_ref, out_first, out_second, new_ghost, new_face, values_ref = outs
+    parts_ref, out_first, out_second, new_ghost, new_face = outs
     ghost_value, face_value = edge_step(
         scale, flags_ref, got_first, got_second, sum_first, sum_second, ghost, face, before
     )
     new_ghost[...] = ghost_value
     new_face[...] = face_value
-    next_values(ghost_value, face_value, inner_values_ref, edge_lane, edge_block, values_ref)
-    send_sums(flags_ref, values_ref[...], matrix_ref, from_edge_ref, parts_ref, out_first, out_second)
+    send_sums(
+        flags_ref, edge_values(ghost_value, face_value), inner_values_ref, edge_lane, edge_block,
+        matrix_ref, from_edge_ref, parts_ref, out_first, out_second,
+    )
 
 
 def inner_kernel(scale, with_before, parts_ref, state_ref, *rest):
@@ -298,15 +322,16 @@
         (before_ghost, before_face),
     )
     new_face[...] = face_value
-    next_values(ghost_value, face_value, inner_values_ref, edge_lane, edge_block, final_ref)
-    values = final_ref[...]
+    edge = edge_values(ghost_value, face_value)
     nodes = basis_ref.shape[0]
-    waves, slots = values.shape
+    waves, slots = final_ref.shape
     pitch = slots // cells
-    stacked = jnp.concatenate(
-        [values[:, cell * pitch : (cell + 1) * pitch] for cell in range(cells)], axis=0
-    )
-    at = dot(stacked[:, :nodes], basis_ref[...])
+    stacked = []
+    for cell in range(cells):
+        values = cell_values(edge, inner_values_ref, edge_lane, edge_block, cell, pitch)
+        final_ref[:, cell * pitch : (cell + 1) * pitch] = values
+        stacked.append(values)
+    at = dot(jnp.concatenate(stacked, axis=0)[:, :nodes], basis_ref[...])
     at_ref[...] = at
     weights = column(occupancy_ref[...])
     for cell in range(cells):
@@ -343,7 +368,7 @@
 
 def potential_kernel(total_ref, *rest, factor):
     more, (core_ref, quad_ref, at_ref, basis_ref, product_ref, from_edge_ref,
-           potential_ref, parts_ref, ghost_ref) = rest[:-9], rest[-9:]
+           potential_ref, parts_ref, ghost_ref, twin_ref) = rest[:-10], rest[-10:]
     total = total_ref[...]
     if more:
         total = (total + more[0][...]) + (more[1][...] + more[2][...])
@@ -365,7 +390,9 @@
         block = product_ref[:, cell * pitch : (cell + 1) * pitch]
         put_parts(parts_ref, cell, pitch, block + projected[cell * waves : (cell + 1) * waves])
     count = ghost_ref.shape[1]
-    ghost_ref[...] = joined(dot(parts_ref[...], from_edge_ref[:, :count]))
+    sums = joined(dot(parts_ref[...], from_edge_ref[:, :count]))
+    ghost_ref[...] = sums
+    twin_ref[...] = sums
 
 
 def residual_kernel(
@@ -463,18 +490,19 @@
     state_out = ((waves, owned), f32)
 
     index_out = ((ROWS, slots), jnp.int16)
-    w, faces, links, start_face = call(
+    w, faces, links, start_face, start_twin = call(
         pick_kernel,
         [
             (wavefunctions.shape, bf16),
             ((1, count), jnp.int32),
             (connectivity.shape, jnp.int32),
             ((waves, count), bf16),
+            ((waves, count), bf16),
         ],
         wavefunctions, face_nodes.reshape(1, count), connectivity,
         held=3, scratch=[pltpu.SemaphoreType.DMA((3,))], room=56,
     )
-    start_pair = exchanged(start_face, start_face)
+    start_pair = exchanged(start_twin, start_face)
     (
         from_own, from_edge, padded, own_lane, own_block, edge_lane, edge_block,
         node_lane, node_block, inner, values, state,
@@ -503,9 +531,9 @@
         ],
         room=44,
     )
-    parts, *sums, ghost, _ = call(
+    parts, *sums, ghost = call(
         first_kernel,
-        [parts_out, *edge_out, edge_out[0], values_out],
+        [parts_out, *edge_out, edge_out[0]],
         flags, values, *start_pair, edge_lane, edge_block, padded, from_edge, smem=1,
     )
     face = start_face.astype(f32)
@@ -520,9 +548,9 @@
         )
         received = (flags, *got, *sums, ghost, face, *before_edge)
         if step < 2:
-            parts, *sums, new_ghost, new_face, _ = call(
+            parts, *sums, new_ghost, new_face = call(
                 functools.partial(edge_kernel, scale, step > 0),
-                [parts_out, *edge_out, *edge_out, values_out],
+                [parts_out, *edge_out, *edge_out],
                 *received, values, edge_lane, edge_block, padded, from_edge, smem=1,
             )
             before_edge, ghost, face = (ghost, face), new_ghost, new_face
@@ -540,12 +568,12 @@
         final, padded, basis_values, scratch=[pltpu.VMEM((pitch, points), f32)],
     )
     totals = band_parts(band, "band")
-    potential, parts, sum_ghost = call(
+    potential, parts, *sums = call(
         functools.partial(potential_kernel, factor=2.0 / band_total),
-        [((cells, points), f32), parts_out, edge_out[0]],
+        [((cells, points), f32), parts_out, *edge_out],
         *totals, core_density, quad_weights, at, wide_basis, products, from_edge,
     )
-    returned = exchanged(sum_ghost, sum_ghost)
+    returned = exchanged(*sums)
     partial, shift, potential = call(
         residual_kernel,
         [state_out, edge_out[0], ((cells, points), f32)],

time: 41.8 us -> 39 us (0.933)
  Pallas kernels: 19 us -> 17.2 us
  waiting for transfers between devices: 5.32 us -> 4.67 us
    pallas_call x13, Pallas kernels: 19 us -> 17.2 us  [call(): pl.pallas_call(kernel, out_shape=[pltpu.VMEM(*out) for out in outs[:kept]...]
    ppermute x10, waiting for transfers between devices: 1.83 us -> 1.18 us  [paired(): return lax.ppermute(x, ('space', 'band'), route)]
  transfers between devices with their start and end apart: 14 -> 14, of which waited for: 8 -> 8; matrix products, arithmetic and copies ran while one was open for 0% -> 0% of each run, Pallas kernels for 21% -> 23%
where the time goes in v5:
time: 39 us; the launch traced here: 38.8 us
  Pallas kernels  17.2 us (44%)
  starting transfers between devices  16.1 us (41%)
  waiting for transfers between devices  4.67 us (12%)
  between operations  0.74 us (2%)
    pallas_call x13, Pallas kernels, call(): pl.pallas_call(kernel, out_shape=[pltpu.VMEM(*out) for out in outs[:kept]...  17.2 us
    ppermute x10, starting transfers between devices, paired(): return lax.ppermute(x, ('space', 'band'), route)  12.7 us
    ppermute x4, waiting for transfers between devices, swapped(): lax.ppermute(x, axis, [(i, i ^ mask) for i in range(lax.axis_size(axis))])  3.49 us
    ppermute x4, starting transfers between devices, swapped(): lax.ppermute(x, axis, [(i, i ^ mask) for i in range(lax.axis_size(axis))])  3.37 us
    ppermute x10, waiting for transfers between devices, paired(): return lax.ppermute(x, ('space', 'band'), route)  1.18 us
  transfers between devices with their start and end apart: 14, of which 8 were waited for; matrix products, arithmetic and copies ran while one was open for 0% of the time, Pallas kernels for 23%

profile of v5, /device:TPU:0, one launch (start us, length us, event | category | flops | bytes accessed | tf_op | source)
XLA Modules:
  0.0 38.8 jit_solution(16593107349383523410)
XLA Ops:
  0.6 1.0 %shard_map.104 = (bf16[32,1280]{1,0:T(8,128)(2,1)S(1)}, s32[1,256]{1,0:T(1,128)S(1)}, s32[9,216]{1,0:T(8,128)S(1)}, bf16[32,256]{1,0:T(8,128)(2,1)S(1)}, bf16[32,256]{1,0:T(8,128)(2,1)S(1)}) custom-call(bf16[32,1280]{1,0:T(8,128)(2,1)} %w_in.1, s32[1,256]{1,0:T(1,128)} %bitcast.8, s32[9,216]{1,0:T(8,128)} %links_in.1), custom_call_target="tpu_custom_call" | custom-call | flops 268435456 | bytes 1048576 | tf_op jit(solution)/shard_map/pallas_call | solution.py:53
  1.7 3.1 %collective-permute-start = (bf16[32,256]{1,0:T(8,128)(2,1)S(1)}, bf16[32,256]{1,0:T(8,128)(2,1)S(1)}, u32[]{:S(2)}, u32[]{:S(2)}) collective-permute-start(bf16[32,256]{1,0:T(8,128)(2,1)S(1)} %get-tuple-element.56), channel_id=1, source_target_pairs={{0,8},{1,9},{2,10},{3,11},{4,12},{5,13},{6,14},{7,15},{8,0},{9,1},... | collective-permute-start | bytes 49160 | tf_op jit(solution)/shard_map/ppermute | solution.py:434
  4.8 0.0 collective-permute-start.1
  4.8 0.1 add_convert_fusion.flags_ref
  4.8 2.3 %shard_map.105 = (bf16[2304,1280]{1,0:T(8,128)(2,1)S(1)}, bf16[2304,512]{1,0:T(8,128)(2,1)S(1)}, bf16[9,256,256]{2,1,0:T(8,128)(2,1)S(1)}, s16[16,2304]{1,0:T(8,...) custom-call(bf16[9,216,216]{2,1,0:T(8,128)(2,1)} %matrix_in.1, ...), custom_call_target="tpu_custom_call" | custom-call | flops 268435456 | bytes 1048576 | tf_op jit(solution)/shard_map/pallas_call | solution.py:53
  7.1 0.0 collective-permute-done.got_first
  7.1 0.0 collective-permute-done.1.got_second
  7.1 1.3 %shard_map.106 = (bf16[64,2304]{1,0:T(8,128)(2,1)S(1)}, f32[32,256]{1,0:T(8,128)S(1)}, f32[32,256]{1,0:T(8,128)S(1)}, f32[32,256]{1,0:T(8,128)S(1)}) custom-call(s32[3]{0:T(128)S(1)} %add_convert_fusion.flags_ref, bf16[32,2304]{1,0:T(8,128)(2,1)S(1)} %get-tuple-element.55.inner_values_ref, bf16[32,256]{1,0:T(8,128)(2,1)S(1)} %collective-permute-done.got_first, ...), custom_call_target="tpu_custom_call" | custom-call | flops 268435456 | bytes 1048576 | tf_op jit(solution)/shard_map/pallas_call | solution.py:53
  8.5 3.2 %collective-permute-start.2 = (f32[32,256]{1,0:T(8,128)S(1)}, f32[32,256]{1,0:T(8,128)S(1)}, u32[]{:S(2)}, u32[]{:S(2)}) collective-permute-start(f32[32,256]{1,0:T(8,128)S(1)} %get-tuple-element.62.sum_first), channel_id=1, source_target_pairs={{0,8},{1,9},{2,10},{3,11},{4,12},{5,13},{6,14},{7,15},{8,0},{9,1},... | collective-permute-start | bytes 98312 | tf_op jit(solution)/shard_map/ppermute | solution.py:434
  11.7 0.0 collective-permute-start.3
  11.7 1.6 %shard_map.107 = (f32[32,1280]{1,0:T(8,128)S(1)}, bf16[32,2304]{1,0:T(8,128)(2,1)S(1)}) custom-call(bf16[64,2304]{1,0:T(8,128)(2,1)S(1)} %get-tuple-element.65.parts_ref, f32[32,1280]{1,0:T(8,128)S(1)} %get-tuple-element.66.state_ref.rest_0_, s16[16,2304]{1,0:T(8,128)(2,1)S(1)} %get-tuple-element.67.rest_0_.rest_1_, ...), custom_call_target="tpu_custom_call" | custom-call | flops 268435456 | bytes 1048576 | tf_op jit(solution)/shard_map/pallas_call | solution.py:53
  13.3 0.3 collective-permute-done.2.got_first
  13.6 0.0 collective-permute-done.3.got_second
  13.6 1.4 %shard_map.108 = (bf16[64,2304]{1,0:T(8,128)(2,1)S(1)}, f32[32,256]{1,0:T(8,128)S(1)}, f32[32,256]{1,0:T(8,128)S(1)}, f32[32,256]{1,0:T(8,128)S(1)}, f32[32,256]{1,0:T(8,128)S(1)}) custom-call(s32[3]{0:T(128)S(1)} %add_convert_fusion.flags_ref, f32[32,256]{1,0:T(8,128)S(1)} %collective-permute-done.2.got_first, ...), custom_call_target="tpu_custom_call" | custom-call | flops 268435456 | bytes 1048576 | tf_op jit(solution)/shard_map/pallas_call | solution.py:53
  15.0 2.2 %collective-permute-start.4 = (f32[32,256]{1,0:T(8,128)S(1)}, f32[32,256]{1,0:T(8,128)S(1)}, u32[]{:S(2)}, u32[]{:S(2)}) collective-permute-start(f32[32,256]{1,0:T(8,128)S(1)} %get-tuple-element.72.sum_first), channel_id=1, source_target_pairs={{0,8},{1,9},{2,10},{3,11},{4,12},{5,13},{6,14},{7,15},{8,0},{9,1},... | collective-permute-start | bytes 98312 | tf_op jit(solution)/shard_map/ppermute | solution.py:434
  17.2 0.0 collective-permute-start.5
  17.2 1.6 %shard_map.109 = (f32[32,1280]{1,0:T(8,128)S(1)}, bf16[32,2304]{1,0:T(8,128)(2,1)S(1)}) custom-call(bf16[64,2304]{1,0:T(8,128)(2,1)S(1)} %get-tuple-element.76.parts_ref, f32[32,1280]{1,0:T(8,128)S(1)} %get-tuple-element.77.state_ref.rest_0_, f32[32,1280]{1,0:T(8,128)S(1)} %get-tuple-element.66.state_ref.rest_0_, ...), custom_call_target="tpu_custom_call" | custom-call | flops 268435456 | bytes 1048576 | tf_op jit(solution)/shard_map/pallas_call | solution.py:53
  18.7 0.3 collective-permute-done.4.got_first
  19.0 0.0 collective-permute-done.5.got_second
  19.0 1.4 %shard_map.110 = (bf16[64,2304]{1,0:T(8,128)(2,1)S(1)}, f32[32,256]{1,0:T(8,128)S(1)}, f32[32,256]{1,0:T(8,128)S(1)}, f32[32,256]{1,0:T(8,128)S(1)}, f32[32,256]{1,0:T(8,128)S(1)}) custom-call(s32[3]{0:T(128)S(1)} %add_convert_fusion.flags_ref, f32[32,256]{1,0:T(8,128)S(1)} %collective-permute-done.4.got_first, ...), custom_call_target="tpu_custom_call" | custom-call | flops 268435456 | bytes 1048576 | tf_op jit(solution)/shard_map/pallas_call | solution.py:53
  20.5 2.2 %collective-permute-start.6 = (f32[32,256]{1,0:T(8,128)S(1)}, f32[32,256]{1,0:T(8,128)S(1)}, u32[]{:S(2)}, u32[]{:S(2)}) collective-permute-start(f32[32,256]{1,0:T(8,128)S(1)} %get-tuple-element.79.sum_first), channel_id=1, source_target_pairs={{0,8},{1,9},{2,10},{3,11},{4,12},{5,13},{6,14},{7,15},{8,0},{9,1},... | collective-permute-start | bytes 98312 | tf_op jit(solution)/shard_map/ppermute | solution.py:434
  22.6 0.0 collective-permute-start.7
  22.6 1.6 %shard_map.111 = (f32[32,1280]{1,0:T(8,128)S(1)}, bf16[32,2304]{1,0:T(8,128)(2,1)S(1)}) custom-call(bf16[64,2304]{1,0:T(8,128)(2,1)S(1)} %get-tuple-element.83.parts_ref, f32[32,1280]{1,0:T(8,128)S(1)} %get-tuple-element.84.state_ref, f32[32,1280]{1,0:T(8,128)S(1)} %get-tuple-element.77.state_ref.rest_0_, ...), custom_call_target="tpu_custom_call" | custom-call | flops 268435456 | bytes 1048576 | tf_op jit(solution)/shard_map/pallas_call | solution.py:53
  24.2 0.0 copy-start.2
  24.2 0.3 collective-permute-done.6.got_first
  24.5 0.0 collective-permute-done.7.got_second
  24.5 0.0 copy-done
  24.5 0.0 copy-done.4
  24.5 1.1 %shard_map.112 = (f32[32,256]{1,0:T(8,128)S(1)}, bf16[32,2304]{1,0:T(8,128)(2,1)S(1)}, f32[288,343]{1,0:T(8,128)S(1)}, f32[9,343]{1,0:T(8,128)S(1)}) custom-call(s32[3]{0:T(128)S(1)} %add_convert_fusion.flags_ref, f32[32,256]{1,0:T(8,128)S(1)} %collective-permute-done.6.got_first, f32[32,256]{1,0:T(8,128)S(1)} %collective-permute-done.7.got_second, ...), custom_call_target="tpu_custom_call" | custom-call | flops 268435456 | bytes 1048576 | tf_op jit(solution)/shard_map/pallas_call | solution.py:53
  25.6 0.3 collective-permute-start.8
  25.9 1.0 %collective-permute-done.8 = f32[9,343]{1,0:T(8,128)S(1)} collective-permute-done((f32[9,343]{1,0:T(8,128)S(1)}, f32[9,343]{1,0:T(8,128)S(1)}, u32[]{:S(2)}, u32[]{:S(2)}) %collective-permute-start.8) | collective-permute-done | bytes 12380 | tf_op jit(solution)/shard_map/ppermute | solution.py:442
  26.9 2.3 %collective-permute-start.11 = (f32[9,343]{1,0:T(8,128)S(1)}, f32[9,343]{1,0:T(8,128)S(1)}, u32[]{:S(2)}, u32[]{:S(2)}) collective-permute-start(f32[9,343]{1,0:T(8,128)S(1)} %add.8.total_ref), channel_id=1, source_target_pairs={{0,7},{1,6},{2,5},{3,4},{4,3},{5,2},{6,1},{7,0},{8,15},{9,14},{10,... | collective-permute-start | bytes 37052 | tf_op jit(solution)/shard_map/ppermute | solution.py:442
  29.2 0.4 collective-permute-start.10
  29.6 0.4 collective-permute-start.9
  29.9 0.3 shard_map.113
  30.3 0.8 %collective-permute-done.11.rest_2_ = f32[9,343]{1,0:T(8,128)S(1)} collective-permute-done((f32[9,343]{1,0:T(8,128)S(1)}, f32[9,343]{1,0:T(8,128)S(1)}, u32[]{:S(2)}, u32[]{:S(2)}) %collective-permute-start.11) | collective-permute-done | bytes 12380 | tf_op jit(solution)/shard_map/ppermute | solution.py:442
  31.0 1.4 %collective-permute-done.10.rest_1_ = f32[9,343]{1,0:T(8,128)S(1)} collective-permute-done((f32[9,343]{1,0:T(8,128)S(1)}, f32[9,343]{1,0:T(8,128)S(1)}, u32[]{:S(2)}, u32[]{:S(2)}) %collective-permute-start.10) | collective-permute-done | bytes 12380 | tf_op jit(solution)/shard_map/ppermute | solution.py:442
  32.4 0.4 collective-permute-done.9.rest_0_
  32.8 0.0 copy-done.1
  32.8 0.0 copy-done.2
  32.8 0.6 %shard_map.114 = (f32[9,343]{1,0:T(8,128)S(1)}, bf16[64,2304]{1,0:T(8,128)(2,1)S(1)}, f32[32,256]{1,0:T(8,128)S(1)}, f32[32,256]{1,0:T(8,128)S(1)}) custom-call(f32[9,343]{1,0:T(8,128)S(1)} %add.8.total_ref, f32[9,343]{1,0:T(8,128)S(1)} %collective-permute-done.9.rest_0_, f32[9,343]{1,0:T(8,128)S(1)} %collective-permute-done.10.rest_1_, ...), custom_call_target="tpu_custom_call" | custom-call | flops 268435456 | bytes 1048576 | tf_op jit(solution)/shard_map/pallas_call | solution.py:53
  33.4 2.1 %collective-permute-start.12 = (f32[32,256]{1,0:T(8,128)S(1)}, f32[32,256]{1,0:T(8,128)S(1)}, u32[]{:S(2)}, u32[]{:S(2)}) collective-permute-start(f32[32,256]{1,0:T(8,128)S(1)} %get-tuple-element.91), channel_id=1, source_target_pairs={{0,8},{1,9},{2,10},{3,11},{4,12},{5,13},{6,14},{7,15},{8,0},{9,1},... | collective-permute-start | bytes 98312 | tf_op jit(solution)/shard_map/ppermute | solution.py:434
  35.5 0.0 collective-permute-start.13
  35.5 0.0 copy-done.3
  35.5 1.6 %shard_map.115 = (f32[32,1280]{1,0:T(8,128)S(1)}, f32[32,256]{1,0:T(8,128)S(1)}, f32[9,343]{1,0:T(8,128)}) custom-call(bf16[64,2304]{1,0:T(8,128)(2,1)S(1)} %get-tuple-element.93.parts_ref, f32[32,1280]{1,0:T(8,128)S(1)} %get-tuple-element.94.state_ref, f32[32,256]{1,0:T(8,128)S(1)} %get-tuple-element.95.face_ref, f32[1,32]{1,0:T(1,128)S(1)} %bitcast.6, ...), custom_call_target="tpu_custom_call" | custom-call | flops 268435456 | bytes 1048576 | tf_op jit(solution)/shard_map/pallas_call | solution.py:53
  37.2 0.2 collective-permute-done.12.got_first
  37.4 0.0 collective-permute-done.13.got_second
  37.4 1.4 %shard_map.116 = f32[32,1280]{1,0:T(8,128)} custom-call(s32[3]{0:T(128)S(1)} %add_convert_fusion.flags_ref, f32[32,256]{1,0:T(8,128)S(1)} %collective-permute-done.12.got_first, f32[32,256]{1,0:T(8,128)S(1)} %collective-permute-done.13.got_second, f32[32,1280]{1,0:T(8,128)S(1)} %get-tuple-element.97.partial_ref, f32[32,256]{1,0:T(8,128)S(1)} %get-tuple-element.98.shift_ref, ...), custom_call_target="tpu_custom_call" | custom-call | flops 268435456 | bytes 1048576 | tf_op jit(solution)/shard_map/pallas_call | solution.py:53
  (6 shorter events, 0.0 us)
Async XLA Ops:
  1.7 5.5 %collective-permute-start = (bf16[32,256]{1,0:T(8,128)(2,1)S(1)}, bf16[32,256]{1,0:T(8,128)(2,1)S(1)}, u32[]{:S(2)}, u32[]{:S(2)}) collective-permute-start(bf16[32,256]{1,0:T(8,128)(2,1)S(1)} %get-tuple-element.56), channel_id=1, source_target_pairs={{0,8},{1,9},{2,10},{3,11},{4,12},{5,13},{6,14},{7,15},{8,0},{9,1},... | collective-permute-start | bytes 49160 | tf_op jit(solution)/shard_map/ppermute | solution.py:434
  4.8 2.4 %collective-permute-start.1 = (bf16[32,256]{1,0:T(8,128)(2,1)S(1)}, bf16[32,256]{1,0:T(8,128)(2,1)S(1)}, u32[]{:S(2)}, u32[]{:S(2)}) collective-permute-start(bf16[32,256]{1,0:T(8,128)(2,1)S(1)} %get-tuple-element.57), channel_id=1, source_target_pairs={{0,1},{1,0},{2,3},{3,2},{4,5},{5,4},{6,7},{7,6},{8,16},{9,17},{10,... | collective-permute-start | bytes 49160 | tf_op jit(solution)/shard_map/ppermute | solution.py:434
  8.5 5.1 %collective-permute-start.2 = (f32[32,256]{1,0:T(8,128)S(1)}, f32[32,256]{1,0:T(8,128)S(1)}, u32[]{:S(2)}, u32[]{:S(2)}) collective-permute-start(f32[32,256]{1,0:T(8,128)S(1)} %get-tuple-element.62.sum_first), channel_id=1, source_target_pairs={{0,8},{1,9},{2,10},{3,11},{4,12},{5,13},{6,14},{7,15},{8,0},{9,1},... | collective-permute-start | bytes 98312 | tf_op jit(solution)/shard_map/ppermute | solution.py:434
  11.7 1.9 %collective-permute-start.3 = (f32[32,256]{1,0:T(8,128)S(1)}, f32[32,256]{1,0:T(8,128)S(1)}, u32[]{:S(2)}, u32[]{:S(2)}) collective-permute-start(f32[32,256]{1,0:T(8,128)S(1)} %get-tuple-element.63.sum_second), channel_id=1, source_target_pairs={{0,1},{1,0},{2,3},{3,2},{4,5},{5,4},{6,7},{7,6},{8,16},{9,17},{10,... | collective-permute-start | bytes 98312 | tf_op jit(solution)/shard_map/ppermute | solution.py:434
  15.0 4.1 %collective-permute-start.4 = (f32[32,256]{1,0:T(8,128)S(1)}, f32[32,256]{1,0:T(8,128)S(1)}, u32[]{:S(2)}, u32[]{:S(2)}) collective-permute-start(f32[32,256]{1,0:T(8,128)S(1)} %get-tuple-element.72.sum_first), channel_id=1, source_target_pairs={{0,8},{1,9},{2,10},{3,11},{4,12},{5,13},{6,14},{7,15},{8,0},{9,1},... | collective-permute-start | bytes 98312 | tf_op jit(solution)/shard_map/ppermute | solution.py:434
  17.2 1.9 %collective-permute-start.5 = (f32[32,256]{1,0:T(8,128)S(1)}, f32[32,256]{1,0:T(8,128)S(1)}, u32[]{:S(2)}, u32[]{:S(2)}) collective-permute-start(f32[32,256]{1,0:T(8,128)S(1)} %get-tuple-element.73.sum_second), channel_id=1, source_target_pairs={{0,1},{1,0},{2,3},{3,2},{4,5},{5,4},{6,7},{7,6},{8,16},{9,17},{10,... | collective-permute-start | bytes 98312 | tf_op jit(solution)/shard_map/ppermute | solution.py:434
  20.5 4.1 %collective-permute-start.6 = (f32[32,256]{1,0:T(8,128)S(1)}, f32[32,256]{1,0:T(8,128)S(1)}, u32[]{:S(2)}, u32[]{:S(2)}) collective-permute-start(f32[32,256]{1,0:T(8,128)S(1)} %get-tuple-element.79.sum_first), channel_id=1, source_target_pairs={{0,8},{1,9},{2,10},{3,11},{4,12},{5,13},{6,14},{7,15},{8,0},{9,1},... | collective-permute-start | bytes 98312 | tf_op jit(solution)/shard_map/ppermute | solution.py:434
  22.6 1.9 %collective-permute-start.7 = (f32[32,256]{1,0:T(8,128)S(1)}, f32[32,256]{1,0:T(8,128)S(1)}, u32[]{:S(2)}, u32[]{:S(2)}) collective-permute-start(f32[32,256]{1,0:T(8,128)S(1)} %get-tuple-element.80.sum_second), channel_id=1, source_target_pairs={{0,1},{1,0},{2,3},{3,2},{4,5},{5,4},{6,7},{7,6},{8,16},{9,17},{10,... | collective-permute-start | bytes 98312 | tf_op jit(solution)/shard_map/ppermute | solution.py:434
  22.6 1.9 %copy-start = (bf16[216,343]{1,0:T(8,128)(2,1)S(1)}, bf16[216,343]{1,0:T(8,128)(2,1)}, u32[]{:S(2)}) copy-start(bf16[216,343]{1,0:T(8,128)(2,1)} %basis_ref.3) | copy-start | bytes 444532
  22.6 1.9 %copy-start.4 = (f32[32]{0:T(128)S(1)}, f32[32]{0:T(128)}, u32[]{:S(2)}) copy-start(f32[32]{0:T(128)} %param.16) | copy-start | bytes 388
  24.2 8.6 %copy-start.1 = (f32[9,343]{1,0:T(8,128)S(1)}, f32[9,343]{1,0:T(8,128)}, u32[]{:S(2)}) copy-start(f32[9,343]{1,0:T(8,128)} %rest_3_.1) | copy-start | bytes 37048
  24.2 8.6 %copy-start.2 = (f32[9,343]{1,0:T(8,128)S(1)}, f32[9,343]{1,0:T(8,128)}, u32[]{:S(2)}) copy-start(f32[9,343]{1,0:T(8,128)} %rest_4_.1) | copy-start | bytes 37048
  25.6 1.3 %collective-permute-start.8 = (f32[9,343]{1,0:T(8,128)S(1)}, f32[9,343]{1,0:T(8,128)S(1)}, u32[]{:S(2)}, u32[]{:S(2)}) collective-permute-start(f32[9,343]{1,0:T(8,128)S(1)} %get-tuple-element.86), channel_id=1, source_target_pairs={{0,1},{1,0},{2,3},{3,2},{4,5},{5,4},{6,7},{7,6},{8,9},{9,8},{10,11... | collective-permute-start | bytes 37052 | tf_op jit(solution)/shard_map/ppermute | solution.py:442
  26.9 4.2 %collective-permute-start.11 = (f32[9,343]{1,0:T(8,128)S(1)}, f32[9,343]{1,0:T(8,128)S(1)}, u32[]{:S(2)}, u32[]{:S(2)}) collective-permute-start(f32[9,343]{1,0:T(8,128)S(1)} %add.8.total_ref), channel_id=1, source_target_pairs={{0,7},{1,6},{2,5},{3,4},{4,3},{5,2},{6,1},{7,0},{8,15},{9,14},{10,... | collective-permute-start | bytes 37052 | tf_op jit(solution)/shard_map/ppermute | solution.py:442
  29.2 3.3 %collective-permute-start.10 = (f32[9,343]{1,0:T(8,128)S(1)}, f32[9,343]{1,0:T(8,128)S(1)}, u32[]{:S(2)}, u32[]{:S(2)}) collective-permute-start(f32[9,343]{1,0:T(8,128)S(1)} %add.8.total_ref), channel_id=1, source_target_pairs={{0,5},{1,4},{2,7},{3,6},{4,1},{5,0},{6,3},{7,2},{8,13},{9,12},{10,... | collective-permute-start | bytes 37052 | tf_op jit(solution)/shard_map/ppermute | solution.py:442
  29.6 3.3 %collective-permute-start.9 = (f32[9,343]{1,0:T(8,128)S(1)}, f32[9,343]{1,0:T(8,128)S(1)}, u32[]{:S(2)}, u32[]{:S(2)}) collective-permute-start(f32[9,343]{1,0:T(8,128)S(1)} %add.8.total_ref), channel_id=1, source_target_pairs={{0,3},{1,2},{2,1},{3,0},{4,7},{5,6},{6,5},{7,4},{8,11},{9,10},{10,... | collective-permute-start | bytes 37052 | tf_op jit(solution)/shard_map/ppermute | solution.py:442
  29.9 5.6 %copy-start.3 = (f32[32]{0:T(128)S(1)}, f32[32]{0:T(128)}, u32[]{:S(2)}) copy-start(f32[32]{0:T(128)} %param.17) | copy-start | bytes 388
  33.4 4.0 %collective-permute-start.12 = (f32[32,256]{1,0:T(8,128)S(1)}, f32[32,256]{1,0:T(8,128)S(1)}, u32[]{:S(2)}, u32[]{:S(2)}) collective-permute-start(f32[32,256]{1,0:T(8,128)S(1)} %get-tuple-element.91), channel_id=1, source_target_pairs={{0,8},{1,9},{2,10},{3,11},{4,12},{5,13},{6,14},{7,15},{8,0},{9,1},... | collective-permute-start | bytes 98312 | tf_op jit(solution)/shard_map/ppermute | solution.py:434
  35.5 1.9 %collective-permute-start.13 = (f32[32,256]{1,0:T(8,128)S(1)}, f32[32,256]{1,0:T(8,128)S(1)}, u32[]{:S(2)}, u32[]{:S(2)}) collective-permute-start(f32[32,256]{1,0:T(8,128)S(1)} %get-tuple-element.92), channel_id=1, source_target_pairs={{0,1},{1,0},{2,3},{3,2},{4,5},{5,4},{6,7},{7,6},{8,16},{9,17},{10,... | collective-permute-start | bytes 98312 | tf_op jit(solution)/shard_map/ppermute | solution.py:434

commit v6 on v5

--- a/solution.py
+++ b/solution.py
@@ -80,11 +80,11 @@
     )
 
 
-def gathered(source, lane, block, start=None):
+def gathered(source, lane, block, start=None, before=0):
     out = jnp.zeros(lane.shape, source.dtype) if start is None else start
     for number in range(source.shape[1] // LANES):
         part = along(source[:, number * LANES : (number + 1) * LANES], lane)
-        out = jnp.where(block == number, part, out)
+        out = jnp.where(block == number - before, part, out)
     return out
 
 
@@ -132,9 +132,8 @@
 
 def tables_kernel(
     matrix_in, w_ref, face_ref, links_ref,
-    from_own_ref, from_edge_ref, padded_ref, own_lane, own_block, edge_lane, edge_block,
-    node_lane, node_block, inner_ref, values_ref, state_ref,
-    row_ref, turn_ref, wide_ref, table_ref, matrix_ref, sem,
+    from_own_ref, from_edge_ref, padded_ref, own_lane, own_block, values_ref,
+    row_ref, turn_ref, wide_ref, matrix_ref, sem,
 ):
     copy = pltpu.make_async_copy(matrix_in, matrix_ref, sem)
     copy.start()
@@ -143,39 +142,19 @@
     cells, nodes = links_ref.shape
     pitch = slots // cells
     short = jnp.int16
-    half = ROWS // 2
 
     row_ref[...] = jnp.full(row_ref.shape, -1, jnp.int32)
     turn_ref[...] = jnp.full(turn_ref.shape, -1.0, f32)
     for cell in range(cells):
         line = links_ref[cell : cell + 1, :]
-        row_ref[:, cell * pitch : cell * pitch + nodes] = jnp.broadcast_to(line, (half, nodes))
+        row_ref[:, cell * pitch : cell * pitch + nodes] = jnp.broadcast_to(line, (ROWS, nodes))
         turn_ref[cell : cell + 1, :nodes] = line.astype(f32)
-
-    table_ref[...] = one_hot(lax.broadcasted_iota(jnp.int32, (owned, count), 0) == face_ref[...])
-    order = lax.broadcasted_iota(jnp.int32, (half, count), 1)
-    digits = jnp.concatenate([order >> 7, (order & (LANES - 1)) + 1], axis=0)
-    sums = dot_rows(digits.astype(f32).astype(bf16), table_ref[...])
-    place = sums[:half] * float(LANES) + sums[half:]
-    node_lane[...], node_block[...] = split_index(place.astype(jnp.int32) - 1, jnp.int32)
-    inner = jnp.where(place > 0.5, 0.0, 1.0)
-    inner_ref[...] = inner
 
     for start in range(0, slots, LANES):
         columns = slice(start, start + LANES)
-        index = row_ref[:, columns]
-        lane, block = split_index(index - count, jnp.int32)
-        own_lane[:, columns] = jnp.concatenate([lane, lane], axis=0).astype(short)
-        own_block[:, columns] = jnp.concatenate([block, block], axis=0).astype(short)
-        at_face = gathered(place, lane, block).astype(jnp.int32)
-        index = jnp.where(index < count, index, jnp.where(at_face > 0, at_face + (count - 1), -1))
-        lane, block = split_index(index, jnp.int32)
-        edge_lane[:, columns] = jnp.concatenate([lane, lane], axis=0).astype(short)
-        edge_block[:, columns] = jnp.concatenate([block, block], axis=0).astype(short)
-
+        own_lane[:, columns], own_block[:, columns] = split_index(row_ref[:, columns] - count, short)
     w = w_ref[...]
     gather_columns(w, own_lane, own_block, None, functools.partial(store, values_ref))
-    state_ref[...] = w.astype(f32) * inner[:1]
 
     edge_row = jnp.concatenate(
         [
@@ -219,7 +198,7 @@
     return jnp.where(even, second, first), jnp.where(even, first, second)
 
 
-def cell_values(edge, inner_values_ref, edge_lane, edge_block, cell, pitch):
+def cell_values(edge, inner_values_ref, edge_lane, edge_block, cell, pitch, before=0):
     tiles = []
     for start in range(cell * pitch, (cell + 1) * pitch, LANES):
         columns = slice(start, start + LANES)
@@ -228,7 +207,8 @@
             jnp.concatenate(
                 [
                     gathered(
-                        edge[row : row + ROWS], lane, block, inner_values_ref[row : row + ROWS, columns]
+                        edge[row : row + ROWS], lane, block,
+                        inner_values_ref[row : row + ROWS, columns], before,
                     )
                     for row in range(0, edge.shape[0], ROWS)
                 ],
@@ -240,11 +220,11 @@
 
 def send_sums(
     flags_ref, edge, inner_values_ref, edge_lane, edge_block, matrix_ref, from_edge_ref,
-    parts_ref, first_ref, second_ref,
+    parts_ref, first_ref, second_ref, before=0,
 ):
     cells, pitch, _ = matrix_ref.shape
     for cell in range(cells):
-        values = cell_values(edge, inner_values_ref, edge_lane, edge_block, cell, pitch)
+        values = cell_values(edge, inner_values_ref, edge_lane, edge_block, cell, pitch, before)
         parts_ref[:, cell * pitch : (cell + 1) * pitch] = halves(dot(values, matrix_ref[cell]))
     sums = joined(dot(parts_ref[...], from_edge_ref[...]))
     count = first_ref.shape[1]
@@ -252,15 +232,15 @@
 
 
 def first_kernel(
-    flags_ref, inner_values_ref, got_first, got_second, edge_lane, edge_block, matrix_ref, from_edge_ref,
+    flags_ref, inner_values_ref, got_first, got_second, own_lane, own_block, matrix_ref, from_edge_ref,
     parts_ref, first_ref, second_ref, state_ref,
 ):
     got, _ = chosen(flags_ref, got_first[...].astype(f32), got_second[...].astype(f32))
     got = jnp.where(flags_ref[0] > 0, got, jnp.zeros_like(got))
     state_ref[...] = got
     send_sums(
-        flags_ref, got.astype(bf16), inner_values_ref, edge_lane, edge_block, matrix_ref, from_edge_ref,
-        parts_ref, first_ref, second_ref,
+        flags_ref, got.astype(bf16), inner_values_ref, own_lane, own_block, matrix_ref, from_edge_ref,
+        parts_ref, first_ref, second_ref, before=got.shape[1] // LANES,
     )
 
 
@@ -299,13 +279,50 @@
     )
 
 
-def inner_kernel(scale, with_before, parts_ref, state_ref, *rest):
-    before = rest[0][...] if with_before else None
-    own_lane, own_block, from_own_ref, inner_ref, new_ref, values_ref = (
-        rest[1:] if with_before else rest
-    )
+def start_kernel(
+    scale, parts_ref, w_ref, face_ref, own_lane, own_block, from_own_ref,
+    new_ref, values_ref, state_ref, inner_ref, node_lane, node_block, edge_lane, edge_block, table_ref,
+):
+    slots, owned = from_own_ref.shape
+    count = face_ref.shape[1]
+    half = ROWS // 2
+    table_ref[...] = one_hot(lax.broadcasted_iota(jnp.int32, (owned, count), 0) == face_ref[...])
+    order = lax.broadcasted_iota(jnp.int32, (half, count), 1)
+    digits = jnp.concatenate([order >> 7, (order & (LANES - 1)) + 1], axis=0)
+    sums = dot_rows(digits.astype(f32).astype(bf16), table_ref[...])
+
     applied = joined(dot(parts_ref[...], from_own_ref[...]))
-    new = advance(scale, applied, state_ref[...], before) * inner_ref[:1]
+    place = sums[:half] * float(LANES) + sums[half:]
+    node_lane[...], node_block[...] = split_index(place.astype(jnp.int32) - 1, jnp.int32)
+    inner = jnp.where(place > 0.5, 0.0, 1.0)
+    inner_ref[...] = inner
+    state = w_ref[...].astype(f32) * inner[:1]
+    state_ref[...] = state
+    new = advance(scale, applied, state, None) * inner[:1]
+    new_ref[...] = new
+    gather_columns(
+        new.astype(bf16), own_lane, own_block, None, functools.partial(store, values_ref)
+    )
+
+    short_sums = sums.astype(bf16)
+    for start in range(0, slots, LANES):
+        columns = slice(start, start + LANES)
+        at_face = gathered(short_sums, own_lane[:, columns], own_block[:, columns]).astype(f32)
+        at_face = (at_face[:half] * float(LANES) + at_face[half:]).astype(jnp.int32)
+        index = own_block[:half, columns].astype(jnp.int32) * LANES + own_lane[:half, columns].astype(jnp.int32)
+        index = index + count
+        index = jnp.where(index < count, index, jnp.where(at_face > 0, at_face + (count - 1), -1))
+        lane, block = split_index(jnp.concatenate([index, index], axis=0), jnp.int16)
+        edge_lane[:, columns] = lane
+        edge_block[:, columns] = block
+
+
+def inner_kernel(
+    scale, parts_ref, state_ref, before_ref, own_lane, own_block, from_own_ref, inner_ref,
+    new_ref, values_ref,
+):
+    applied = joined(dot(parts_ref[...], from_own_ref[...]))
+    new = advance(scale, applied, state_ref[...], before_ref[...]) * inner_ref[:1]
     new_ref[...] = new
     gather_columns(
         new.astype(bf16), own_lane, own_block, None, functools.partial(store, values_ref)
@@ -504,28 +521,22 @@
     )
     start_pair = exchanged(start_twin, start_face)
     (
-        from_own, from_edge, padded, own_lane, own_block, edge_lane, edge_block,
-        node_lane, node_block, inner, values, state,
+        from_own, from_edge, padded, own_lane, own_block, values
     ) = call(
         tables_kernel,
         [
             ((slots, owned), bf16),
             ((slots, 2 * count), bf16),
             ((cells, pitch, pitch), bf16),
-            *[index_out] * 4,
-            ((ROWS // 2, owned), jnp.int32),
-            ((ROWS // 2, owned), jnp.int32),
-            ((ROWS // 2, owned), f32),
+            *[index_out] * 2,
             values_out,
-            state_out,
         ],
         cell_hamiltonian, w, faces, links,
         held=1,
         scratch=[
-            pltpu.VMEM((ROWS // 2, slots), jnp.int32),
+            pltpu.VMEM((ROWS, slots), jnp.int32),
             pltpu.VMEM((-(-cells // LANES) * LANES, pitch), f32),
             pltpu.VMEM((2, pitch, pitch), f32),
-            pltpu.VMEM((owned, count), bf16),
             pltpu.VMEM(cell_hamiltonian.shape, bf16),
             pltpu.SemaphoreType.DMA,
         ],
@@ -534,18 +545,36 @@
     parts, *sums, ghost = call(
         first_kernel,
         [parts_out, *edge_out, edge_out[0]],
-        flags, values, *start_pair, edge_lane, edge_block, padded, from_edge, smem=1,
+        flags, values, *start_pair, own_lane, own_block, padded, from_edge, smem=1,
     )
     face = start_face.astype(f32)
-    before_edge, before_state = (), ()
+    before_edge = ()
     scale = 1.0 / spectrum_half
     for step in range(3):
         got = exchanged(*sums)
-        new_state, values = call(
-            functools.partial(inner_kernel, scale, step > 0),
-            [state_out, values_out],
-            parts, state, *before_state, own_lane, own_block, from_own, inner,
-        )
+        if step == 0:
+            (
+                new_state, values, state, inner, node_lane, node_block, edge_lane, edge_block
+            ) = call(
+                functools.partial(start_kernel, scale),
+                [
+                    state_out,
+                    values_out,
+                    state_out,
+                    ((ROWS // 2, owned), f32),
+                    ((ROWS // 2, owned), jnp.int32),
+                    ((ROWS // 2, owned), jnp.int32),
+                    *[index_out] * 2,
+                ],
+                parts, w, faces, own_lane, own_block, from_own,
+                scratch=[pltpu.VMEM((owned, count), bf16)],
+            )
+        else:
+            new_state, values = call(
+                functools.partial(inner_kernel, scale),
+                [state_out, values_out],
+                parts, state, before_state, own_lane, own_block, from_own, inner,
+            )
         received = (flags, *got, *sums, ghost, face, *before_edge)
         if step < 2:
             parts, *sums, new_ghost, new_face = call(
@@ -560,7 +589,7 @@
                 [edge_out[0], values_out, ((cells * waves, points), f32), ((cells, points), f32)],
                 *received, values, edge_lane, edge_block, basis_values, occupancy.reshape(1, waves), smem=1,
             )
-        before_state, state = (state,), new_state
+        before_state, state = state, new_state
         scale = 2.0 / spectrum_half
     products, wide_basis = call(
         products_kernel,

time: 39 us -> 38.5 us (0.987)
  transfers between devices with their start and end apart: 14 -> 14, of which waited for: 8 -> 7; matrix products, arithmetic and copies ran while one was open for 0% -> 0% of each run, Pallas kernels for 23% -> 23%
where the time goes in v6:
time: 38.5 us; the launch traced here: 38.4 us
  Pallas kernels  17 us (44%)
  starting transfers between devices  16.1 us (42%)
  waiting for transfers between devices  4.39 us (11%)
  between operations  0.74 us (2%)
    pallas_call x13, Pallas kernels, call(): pl.pallas_call(kernel, out_shape=[pltpu.VMEM(*out) for out in outs[:kept]...  17 us
    ppermute x10, starting transfers between devices, paired(): return lax.ppermute(x, ('space', 'band'), route)  12.7 us
    ppermute x4, waiting for transfers between devices, swapped(): lax.ppermute(x, axis, [(i, i ^ mask) for i in range(lax.axis_size(axis))])  3.5 us
    ppermute x4, starting transfers between devices, swapped(): lax.ppermute(x, axis, [(i, i ^ mask) for i in range(lax.axis_size(axis))])  3.35 us
    ppermute x10, waiting for transfers between devices, paired(): return lax.ppermute(x, ('space', 'band'), route)  0.89 us
  transfers between devices with their start and end apart: 14, of which 7 were waited for; matrix products, arithmetic and copies ran while one was open for 0% of the time, Pallas kernels for 23%

profile of v6, /device:TPU:0, one launch (start us, length us, event | category | flops | bytes accessed | tf_op | source)
XLA Modules:
  0.0 38.4 jit_solution(10122045628879541334)
XLA Ops:
  0.6 1.0 %shard_map.104 = (bf16[32,1280]{1,0:T(8,128)(2,1)S(1)}, s32[1,256]{1,0:T(1,128)S(1)}, s32[9,216]{1,0:T(8,128)S(1)}, bf16[32,256]{1,0:T(8,128)(2,1)S(1)}, bf16[32,256]{1,0:T(8,128)(2,1)S(1)}) custom-call(bf16[32,1280]{1,0:T(8,128)(2,1)} %w_in.1, s32[1,256]{1,0:T(1,128)} %bitcast.8, s32[9,216]{1,0:T(8,128)} %links_in.1), custom_call_target="tpu_custom_call" | custom-call | flops 268435456 | bytes 1048576 | tf_op jit(solution)/shard_map/pallas_call | solution.py:53
  1.7 3.1 %collective-permute-start = (bf16[32,256]{1,0:T(8,128)(2,1)S(1)}, bf16[32,256]{1,0:T(8,128)(2,1)S(1)}, u32[]{:S(2)}, u32[]{:S(2)}) collective-permute-start(bf16[32,256]{1,0:T(8,128)(2,1)S(1)} %get-tuple-element.56), channel_id=1, source_target_pairs={{0,8},{1,9},{2,10},{3,11},{4,12},{5,13},{6,14},{7,15},{8,0},{9,1},... | collective-permute-start | bytes 49160 | tf_op jit(solution)/shard_map/ppermute | solution.py:451
  4.8 0.0 collective-permute-start.1
  4.8 0.1 add_convert_fusion.flags_ref
  4.8 1.8 %shard_map.105 = (bf16[2304,1280]{1,0:T(8,128)(2,1)S(1)}, bf16[2304,512]{1,0:T(8,128)(2,1)S(1)}, bf16[9,256,256]{2,1,0:T(8,128)(2,1)S(1)}, s16[16,2304]{1,0:T(8,...) custom-call(bf16[9,216,216]{2,1,0:T(8,128)(2,1)} %matrix_in.1, ...), custom_call_target="tpu_custom_call" | custom-call | flops 268435456 | bytes 1048576 | tf_op jit(solution)/shard_map/pallas_call | solution.py:53
  6.6 0.0 collective-permute-done.got_first
  6.7 0.0 collective-permute-done.1.got_second
  6.7 1.3 %shard_map.106 = (bf16[64,2304]{1,0:T(8,128)(2,1)S(1)}, f32[32,256]{1,0:T(8,128)S(1)}, f32[32,256]{1,0:T(8,128)S(1)}, f32[32,256]{1,0:T(8,128)S(1)}) custom-call(s32[3]{0:T(128)S(1)} %add_convert_fusion.flags_ref, bf16[32,2304]{1,0:T(8,128)(2,1)S(1)} %get-tuple-element.55.inner_values_ref, bf16[32,256]{1,0:T(8,128)(2,1)S(1)} %collective-permute-done.got_first, ...), custom_call_target="tpu_custom_call" | custom-call | flops 268435456 | bytes 1048576 | tf_op jit(solution)/shard_map/pallas_call | solution.py:53
  8.0 3.2 %collective-permute-start.2 = (f32[32,256]{1,0:T(8,128)S(1)}, f32[32,256]{1,0:T(8,128)S(1)}, u32[]{:S(2)}, u32[]{:S(2)}) collective-permute-start(f32[32,256]{1,0:T(8,128)S(1)} %get-tuple-element.62.sum_first), channel_id=1, source_target_pairs={{0,8},{1,9},{2,10},{3,11},{4,12},{5,13},{6,14},{7,15},{8,0},{9,1},... | collective-permute-start | bytes 98312 | tf_op jit(solution)/shard_map/ppermute | solution.py:451
  11.2 0.0 collective-permute-start.3
  11.2 1.9 %shard_map.107 = (f32[32,1280]{1,0:T(8,128)S(1)}, bf16[32,2304]{1,0:T(8,128)(2,1)S(1)}, f32[32,1280]{1,0:T(8,128)S(1)}, f32[8,1280]{1,0:T(8,128)S(1)}, s32[8,128...) custom-call(bf16[64,2304]{1,0:T(8,128)(2,1)S(1)} %get-tuple-element.65.parts_re, ...), custom_call_target="tpu_custom_call" | custom-call | flops 268435456 | bytes 1048576 | tf_op jit(solution)/shard_map/pallas_call | solution.py:53
  13.1 0.0 collective-permute-done.2.got_first
  13.1 0.0 collective-permute-done.3.got_second
  13.1 1.4 %shard_map.108 = (bf16[64,2304]{1,0:T(8,128)(2,1)S(1)}, f32[32,256]{1,0:T(8,128)S(1)}, f32[32,256]{1,0:T(8,128)S(1)}, f32[32,256]{1,0:T(8,128)S(1)}, f32[32,256]{1,0:T(8,128)S(1)}) custom-call(s32[3]{0:T(128)S(1)} %add_convert_fusion.flags_ref, f32[32,256]{1,0:T(8,128)S(1)} %collective-permute-done.2.got_first, ...), custom_call_target="tpu_custom_call" | custom-call | flops 268435456 | bytes 1048576 | tf_op jit(solution)/shard_map/pallas_call | solution.py:53
  14.5 2.2 %collective-permute-start.4 = (f32[32,256]{1,0:T(8,128)S(1)}, f32[32,256]{1,0:T(8,128)S(1)}, u32[]{:S(2)}, u32[]{:S(2)}) collective-permute-start(f32[32,256]{1,0:T(8,128)S(1)} %get-tuple-element.70.sum_first), channel_id=1, source_target_pairs={{0,8},{1,9},{2,10},{3,11},{4,12},{5,13},{6,14},{7,15},{8,0},{9,1},... | collective-permute-start | bytes 98312 | tf_op jit(solution)/shard_map/ppermute | solution.py:451
  16.7 0.0 collective-permute-start.5
  16.7 1.6 %shard_map.109 = (f32[32,1280]{1,0:T(8,128)S(1)}, bf16[32,2304]{1,0:T(8,128)(2,1)S(1)}) custom-call(bf16[64,2304]{1,0:T(8,128)(2,1)S(1)} %get-tuple-element.74.parts_ref, f32[32,1280]{1,0:T(8,128)S(1)} %get-tuple-element.75.state_ref.before_ref, f32[32,1280]{1,0:T(8,128)S(1)} %get-tuple-element.76.before_ref, ...), custom_call_target="tpu_custom_call" | custom-call | flops 268435456 | bytes 1048576 | tf_op jit(solution)/shard_map/pallas_call | solution.py:53
  18.3 0.3 collective-permute-done.4.got_first
  18.6 0.0 collective-permute-done.5.got_second
  18.6 1.4 %shard_map.110 = (bf16[64,2304]{1,0:T(8,128)(2,1)S(1)}, f32[32,256]{1,0:T(8,128)S(1)}, f32[32,256]{1,0:T(8,128)S(1)}, f32[32,256]{1,0:T(8,128)S(1)}, f32[32,256]{1,0:T(8,128)S(1)}) custom-call(s32[3]{0:T(128)S(1)} %add_convert_fusion.flags_ref, f32[32,256]{1,0:T(8,128)S(1)} %collective-permute-done.4.got_first, ...), custom_call_target="tpu_custom_call" | custom-call | flops 268435456 | bytes 1048576 | tf_op jit(solution)/shard_map/pallas_call | solution.py:53
  20.0 2.2 %collective-permute-start.6 = (f32[32,256]{1,0:T(8,128)S(1)}, f32[32,256]{1,0:T(8,128)S(1)}, u32[]{:S(2)}, u32[]{:S(2)}) collective-permute-start(f32[32,256]{1,0:T(8,128)S(1)} %get-tuple-element.79.sum_first), channel_id=1, source_target_pairs={{0,8},{1,9},{2,10},{3,11},{4,12},{5,13},{6,14},{7,15},{8,0},{9,1},... | collective-permute-start | bytes 98312 | tf_op jit(solution)/shard_map/ppermute | solution.py:451
  22.2 0.0 collective-permute-start.7
  22.2 1.6 %shard_map.111 = (f32[32,1280]{1,0:T(8,128)S(1)}, bf16[32,2304]{1,0:T(8,128)(2,1)S(1)}) custom-call(bf16[64,2304]{1,0:T(8,128)(2,1)S(1)} %get-tuple-element.83.parts_ref, f32[32,1280]{1,0:T(8,128)S(1)} %get-tuple-element.84.state_ref, f32[32,1280]{1,0:T(8,128)S(1)} %get-tuple-element.75.state_ref.before_ref, s16[16,2304]{1,0:T(8,128)(2,1)S(1)} %get-tuple-element.58.own_lane, ...), custom_call_target="tpu_custom_call" | custom-call | flops 268435456 | bytes 1048576 | tf_op jit(solution)/shard_map/pallas_call | solution.py:53
  23.7 0.0 copy-start.2
  23.8 0.3 collective-permute-done.6.got_first
  24.1 0.0 collective-permute-done.7.got_second
  24.1 0.0 copy-done
  24.1 0.0 copy-done.4
  24.1 1.1 %shard_map.112 = (f32[32,256]{1,0:T(8,128)S(1)}, bf16[32,2304]{1,0:T(8,128)(2,1)S(1)}, f32[288,343]{1,0:T(8,128)S(1)}, f32[9,343]{1,0:T(8,128)S(1)}) custom-call(s32[3]{0:T(128)S(1)} %add_convert_fusion.flags_ref, f32[32,256]{1,0:T(8,128)S(1)} %collective-permute-done.6.got_first, f32[32,256]{1,0:T(8,128)S(1)} %collective-permute-done.7.got_second, ...), custom_call_target="tpu_custom_call" | custom-call | flops 268435456 | bytes 1048576 | tf_op jit(solution)/shard_map/pallas_call | solution.py:53
  25.1 0.3 collective-permute-start.8
  25.5 1.0 %collective-permute-done.8 = f32[9,343]{1,0:T(8,128)S(1)} collective-permute-done((f32[9,343]{1,0:T(8,128)S(1)}, f32[9,343]{1,0:T(8,128)S(1)}, u32[]{:S(2)}, u32[]{:S(2)}) %collective-permute-start.8) | collective-permute-done | bytes 12380 | tf_op jit(solution)/shard_map/ppermute | solution.py:459
  26.4 2.3 %collective-permute-start.11 = (f32[9,343]{1,0:T(8,128)S(1)}, f32[9,343]{1,0:T(8,128)S(1)}, u32[]{:S(2)}, u32[]{:S(2)}) collective-permute-start(f32[9,343]{1,0:T(8,128)S(1)} %add.8.total_ref), channel_id=1, source_target_pairs={{0,7},{1,6},{2,5},{3,4},{4,3},{5,2},{6,1},{7,0},{8,15},{9,14},{10,... | collective-permute-start | bytes 37052 | tf_op jit(solution)/shard_map/ppermute | solution.py:459
  28.7 0.4 collective-permute-start.10
  29.1 0.4 collective-permute-start.9
  29.5 0.3 shard_map.113
  29.8 0.8 %collective-permute-done.11.rest_2_ = f32[9,343]{1,0:T(8,128)S(1)} collective-permute-done((f32[9,343]{1,0:T(8,128)S(1)}, f32[9,343]{1,0:T(8,128)S(1)}, u32[]{:S(2)}, u32[]{:S(2)}) %collective-permute-start.11) | collective-permute-done | bytes 12380 | tf_op jit(solution)/shard_map/ppermute | solution.py:459
  30.6 1.4 %collective-permute-done.10.rest_1_ = f32[9,343]{1,0:T(8,128)S(1)} collective-permute-done((f32[9,343]{1,0:T(8,128)S(1)}, f32[9,343]{1,0:T(8,128)S(1)}, u32[]{:S(2)}, u32[]{:S(2)}) %collective-permute-start.10) | collective-permute-done | bytes 12380 | tf_op jit(solution)/shard_map/ppermute | solution.py:459
  32.0 0.4 collective-permute-done.9.rest_0_
  32.3 0.0 copy-done.1
  32.3 0.0 copy-done.2
  32.3 0.6 %shard_map.114 = (f32[9,343]{1,0:T(8,128)S(1)}, bf16[64,2304]{1,0:T(8,128)(2,1)S(1)}, f32[32,256]{1,0:T(8,128)S(1)}, f32[32,256]{1,0:T(8,128)S(1)}) custom-call(f32[9,343]{1,0:T(8,128)S(1)} %add.8.total_ref, f32[9,343]{1,0:T(8,128)S(1)} %collective-permute-done.9.rest_0_, f32[9,343]{1,0:T(8,128)S(1)} %collective-permute-done.10.rest_1_, ...), custom_call_target="tpu_custom_call" | custom-call | flops 268435456 | bytes 1048576 | tf_op jit(solution)/shard_map/pallas_call | solution.py:53
  33.0 2.1 %collective-permute-start.12 = (f32[32,256]{1,0:T(8,128)S(1)}, f32[32,256]{1,0:T(8,128)S(1)}, u32[]{:S(2)}, u32[]{:S(2)}) collective-permute-start(f32[32,256]{1,0:T(8,128)S(1)} %get-tuple-element.91), channel_id=1, source_target_pairs={{0,8},{1,9},{2,10},{3,11},{4,12},{5,13},{6,14},{7,15},{8,0},{9,1},... | collective-permute-start | bytes 98312 | tf_op jit(solution)/shard_map/ppermute | solution.py:451
  35.1 0.0 collective-permute-start.13
  35.1 0.0 copy-done.3
  35.1 1.6 %shard_map.115 = (f32[32,1280]{1,0:T(8,128)S(1)}, f32[32,256]{1,0:T(8,128)S(1)}, f32[9,343]{1,0:T(8,128)}) custom-call(bf16[64,2304]{1,0:T(8,128)(2,1)S(1)} %get-tuple-element.93.parts_ref, f32[32,1280]{1,0:T(8,128)S(1)} %get-tuple-element.94.state_ref, f32[32,256]{1,0:T(8,128)S(1)} %get-tuple-element.95.face_ref, f32[1,32]{1,0:T(1,128)S(1)} %bitcast.6, ...), custom_call_target="tpu_custom_call" | custom-call | flops 268435456 | bytes 1048576 | tf_op jit(solution)/shard_map/pallas_call | solution.py:53
  36.7 0.2 collective-permute-done.12.got_first
  37.0 0.0 collective-permute-done.13.got_second
  37.0 1.4 %shard_map.116 = f32[32,1280]{1,0:T(8,128)} custom-call(s32[3]{0:T(128)S(1)} %add_convert_fusion.flags_ref, f32[32,256]{1,0:T(8,128)S(1)} %collective-permute-done.12.got_first, f32[32,256]{1,0:T(8,128)S(1)} %collective-permute-done.13.got_second, f32[32,1280]{1,0:T(8,128)S(1)} %get-tuple-element.97.partial_ref, f32[32,256]{1,0:T(8,128)S(1)} %get-tuple-element.98.shift_ref, ...), custom_call_target="tpu_custom_call" | custom-call | flops 268435456 | bytes 1048576 | tf_op jit(solution)/shard_map/pallas_call | solution.py:53
  (6 shorter events, 0.0 us)
Async XLA Ops:
  1.7 5.0 %collective-permute-start = (bf16[32,256]{1,0:T(8,128)(2,1)S(1)}, bf16[32,256]{1,0:T(8,128)(2,1)S(1)}, u32[]{:S(2)}, u32[]{:S(2)}) collective-permute-start(bf16[32,256]{1,0:T(8,128)(2,1)S(1)} %get-tuple-element.56), channel_id=1, source_target_pairs={{0,8},{1,9},{2,10},{3,11},{4,12},{5,13},{6,14},{7,15},{8,0},{9,1},... | collective-permute-start | bytes 49160 | tf_op jit(solution)/shard_map/ppermute | solution.py:451
  4.8 1.9 %collective-permute-start.1 = (bf16[32,256]{1,0:T(8,128)(2,1)S(1)}, bf16[32,256]{1,0:T(8,128)(2,1)S(1)}, u32[]{:S(2)}, u32[]{:S(2)}) collective-permute-start(bf16[32,256]{1,0:T(8,128)(2,1)S(1)} %get-tuple-element.57), channel_id=1, source_target_pairs={{0,1},{1,0},{2,3},{3,2},{4,5},{5,4},{6,7},{7,6},{8,16},{9,17},{10,... | collective-permute-start | bytes 49160 | tf_op jit(solution)/shard_map/ppermute | solution.py:451
  8.0 5.1 %collective-permute-start.2 = (f32[32,256]{1,0:T(8,128)S(1)}, f32[32,256]{1,0:T(8,128)S(1)}, u32[]{:S(2)}, u32[]{:S(2)}) collective-permute-start(f32[32,256]{1,0:T(8,128)S(1)} %get-tuple-element.62.sum_first), channel_id=1, source_target_pairs={{0,8},{1,9},{2,10},{3,11},{4,12},{5,13},{6,14},{7,15},{8,0},{9,1},... | collective-permute-start | bytes 98312 | tf_op jit(solution)/shard_map/ppermute | solution.py:451
  11.2 1.9 %collective-permute-start.3 = (f32[32,256]{1,0:T(8,128)S(1)}, f32[32,256]{1,0:T(8,128)S(1)}, u32[]{:S(2)}, u32[]{:S(2)}) collective-permute-start(f32[32,256]{1,0:T(8,128)S(1)} %get-tuple-element.63.sum_second), channel_id=1, source_target_pairs={{0,1},{1,0},{2,3},{3,2},{4,5},{5,4},{6,7},{7,6},{8,16},{9,17},{10,... | collective-permute-start | bytes 98312 | tf_op jit(solution)/shard_map/ppermute | solution.py:451
  14.5 4.1 %collective-permute-start.4 = (f32[32,256]{1,0:T(8,128)S(1)}, f32[32,256]{1,0:T(8,128)S(1)}, u32[]{:S(2)}, u32[]{:S(2)}) collective-permute-start(f32[32,256]{1,0:T(8,128)S(1)} %get-tuple-element.70.sum_first), channel_id=1, source_target_pairs={{0,8},{1,9},{2,10},{3,11},{4,12},{5,13},{6,14},{7,15},{8,0},{9,1},... | collective-permute-start | bytes 98312 | tf_op jit(solution)/shard_map/ppermute | solution.py:451
  16.7 1.9 %collective-permute-start.5 = (f32[32,256]{1,0:T(8,128)S(1)}, f32[32,256]{1,0:T(8,128)S(1)}, u32[]{:S(2)}, u32[]{:S(2)}) collective-permute-start(f32[32,256]{1,0:T(8,128)S(1)} %get-tuple-element.71.sum_second), channel_id=1, source_target_pairs={{0,1},{1,0},{2,3},{3,2},{4,5},{5,4},{6,7},{7,6},{8,16},{9,17},{10,... | collective-permute-start | bytes 98312 | tf_op jit(solution)/shard_map/ppermute | solution.py:451
  20.0 4.1 %collective-permute-start.6 = (f32[32,256]{1,0:T(8,128)S(1)}, f32[32,256]{1,0:T(8,128)S(1)}, u32[]{:S(2)}, u32[]{:S(2)}) collective-permute-start(f32[32,256]{1,0:T(8,128)S(1)} %get-tuple-element.79.sum_first), channel_id=1, source_target_pairs={{0,8},{1,9},{2,10},{3,11},{4,12},{5,13},{6,14},{7,15},{8,0},{9,1},... | collective-permute-start | bytes 98312 | tf_op jit(solution)/shard_map/ppermute | solution.py:451
  22.2 1.9 %collective-permute-start.7 = (f32[32,256]{1,0:T(8,128)S(1)}, f32[32,256]{1,0:T(8,128)S(1)}, u32[]{:S(2)}, u32[]{:S(2)}) collective-permute-start(f32[32,256]{1,0:T(8,128)S(1)} %get-tuple-element.80.sum_second), channel_id=1, source_target_pairs={{0,1},{1,0},{2,3},{3,2},{4,5},{5,4},{6,7},{7,6},{8,16},{9,17},{10,... | collective-permute-start | bytes 98312 | tf_op jit(solution)/shard_map/ppermute | solution.py:451
  22.2 1.9 %copy-start = (bf16[216,343]{1,0:T(8,128)(2,1)S(1)}, bf16[216,343]{1,0:T(8,128)(2,1)}, u32[]{:S(2)}) copy-start(bf16[216,343]{1,0:T(8,128)(2,1)} %basis_ref.3) | copy-start | bytes 444532
  22.2 1.9 %copy-start.4 = (f32[32]{0:T(128)S(1)}, f32[32]{0:T(128)}, u32[]{:S(2)}) copy-start(f32[32]{0:T(128)} %param.16) | copy-start | bytes 388
  23.7 8.6 %copy-start.1 = (f32[9,343]{1,0:T(8,128)S(1)}, f32[9,343]{1,0:T(8,128)}, u32[]{:S(2)}) copy-start(f32[9,343]{1,0:T(8,128)} %rest_3_.1) | copy-start | bytes 37048
  23.7 8.6 %copy-start.2 = (f32[9,343]{1,0:T(8,128)S(1)}, f32[9,343]{1,0:T(8,128)}, u32[]{:S(2)}) copy-start(f32[9,343]{1,0:T(8,128)} %rest_4_.1) | copy-start | bytes 37048
  25.1 1.3 %collective-permute-start.8 = (f32[9,343]{1,0:T(8,128)S(1)}, f32[9,343]{1,0:T(8,128)S(1)}, u32[]{:S(2)}, u32[]{:S(2)}) collective-permute-start(f32[9,343]{1,0:T(8,128)S(1)} %get-tuple-element.86), channel_id=1, source_target_pairs={{0,1},{1,0},{2,3},{3,2},{4,5},{5,4},{6,7},{7,6},{8,9},{9,8},{10,11... | collective-permute-start | bytes 37052 | tf_op jit(solution)/shard_map/ppermute | solution.py:459
  26.4 4.2 %collective-permute-start.11 = (f32[9,343]{1,0:T(8,128)S(1)}, f32[9,343]{1,0:T(8,128)S(1)}, u32[]{:S(2)}, u32[]{:S(2)}) collective-permute-start(f32[9,343]{1,0:T(8,128)S(1)} %add.8.total_ref), channel_id=1, source_target_pairs={{0,7},{1,6},{2,5},{3,4},{4,3},{5,2},{6,1},{7,0},{8,15},{9,14},{10,... | collective-permute-start | bytes 37052 | tf_op jit(solution)/shard_map/ppermute | solution.py:459
  28.7 3.3 %collective-permute-start.10 = (f32[9,343]{1,0:T(8,128)S(1)}, f32[9,343]{1,0:T(8,128)S(1)}, u32[]{:S(2)}, u32[]{:S(2)}) collective-permute-start(f32[9,343]{1,0:T(8,128)S(1)} %add.8.total_ref), channel_id=1, source_target_pairs={{0,5},{1,4},{2,7},{3,6},{4,1},{5,0},{6,3},{7,2},{8,13},{9,12},{10,... | collective-permute-start | bytes 37052 | tf_op jit(solution)/shard_map/ppermute | solution.py:459
  29.1 3.3 %collective-permute-start.9 = (f32[9,343]{1,0:T(8,128)S(1)}, f32[9,343]{1,0:T(8,128)S(1)}, u32[]{:S(2)}, u32[]{:S(2)}) collective-permute-start(f32[9,343]{1,0:T(8,128)S(1)} %add.8.total_ref), channel_id=1, source_target_pairs={{0,3},{1,2},{2,1},{3,0},{4,7},{5,6},{6,5},{7,4},{8,11},{9,10},{10,... | collective-permute-start | bytes 37052 | tf_op jit(solution)/shard_map/ppermute | solution.py:459
  29.5 5.6 %copy-start.3 = (f32[32]{0:T(128)S(1)}, f32[32]{0:T(128)}, u32[]{:S(2)}) copy-start(f32[32]{0:T(128)} %param.17) | copy-start | bytes 388
  33.0 4.0 %collective-permute-start.12 = (f32[32,256]{1,0:T(8,128)S(1)}, f32[32,256]{1,0:T(8,128)S(1)}, u32[]{:S(2)}, u32[]{:S(2)}) collective-permute-start(f32[32,256]{1,0:T(8,128)S(1)} %get-tuple-element.91), channel_id=1, source_target_pairs={{0,8},{1,9},{2,10},{3,11},{4,12},{5,13},{6,14},{7,15},{8,0},{9,1},... | collective-permute-start | bytes 98312 | tf_op jit(solution)/shard_map/ppermute | solution.py:451
  35.1 1.9 %collective-permute-start.13 = (f32[32,256]{1,0:T(8,128)S(1)}, f32[32,256]{1,0:T(8,128)S(1)}, u32[]{:S(2)}, u32[]{:S(2)}) collective-permute-start(f32[32,256]{1,0:T(8,128)S(1)} %get-tuple-element.92), channel_id=1, source_target_pairs={{0,1},{1,0},{2,3},{3,2},{4,5},{5,4},{6,7},{7,6},{8,16},{9,17},{10,... | collective-permute-start | bytes 98312 | tf_op jit(solution)/shard_map/ppermute | solution.py:451

commit v7 on v6

--- a/solution.py
+++ b/solution.py
@@ -150,12 +150,6 @@
         row_ref[:, cell * pitch : cell * pitch + nodes] = jnp.broadcast_to(line, (ROWS, nodes))
         turn_ref[cell : cell + 1, :nodes] = line.astype(f32)
 
-    for start in range(0, slots, LANES):
-        columns = slice(start, start + LANES)
-        own_lane[:, columns], own_block[:, columns] = split_index(row_ref[:, columns] - count, short)
-    w = w_ref[...]
-    gather_columns(w, own_lane, own_block, None, functools.partial(store, values_ref))
-
     edge_row = jnp.concatenate(
         [
             lax.broadcasted_iota(jnp.int32, (ROWS, count), 1),
@@ -171,6 +165,18 @@
             block = block.astype(jnp.int32).astype(short)
             rows = slice(cell * pitch + start, cell * pitch + start + ROWS)
             from_edge_ref[rows, :] = short_one_hot(across(block, 2 * count), edge_row)
+
+    for start in range(0, slots, LANES):
+        columns = slice(start, start + LANES)
+        own_lane[:, columns], own_block[:, columns] = split_index(row_ref[:, columns] - count, short)
+    w = w_ref[...]
+    gather_columns(w, own_lane, own_block, None, functools.partial(store, values_ref))
+
+    for cell in range(cells):
+        for start in range(0, pitch, ROWS):
+            block = jnp.broadcast_to(turned[start : start + ROWS, cell : cell + 1], (ROWS, LANES))
+            block = block.astype(jnp.int32).astype(short)
+            rows = slice(cell * pitch + start, cell * pitch + start + ROWS)
             from_own_ref[rows, :] = short_one_hot(across(block, owned), own_row)
 
     wide_ref[...] = jnp.zeros_like(wide_ref)

time: 38.5 us -> 38.5 us (level)
  no operation moved by 1% of the time
where the time goes in v7:
time: 38.5 us; the launch traced here: 38.4 us
  Pallas kernels  17 us (44%)
  starting transfers between devices  16.1 us (42%)
  waiting for transfers between devices  4.39 us (11%)
  between operations  0.74 us (2%)
    pallas_call x13, Pallas kernels, call(): pl.pallas_call(kernel, out_shape=[pltpu.VMEM(*out) for out in outs[:kept]...  17 us
    ppermute x10, starting transfers between devices, paired(): return lax.ppermute(x, ('space', 'band'), route)  12.7 us
    ppermute x4, waiting for transfers between devices, swapped(): lax.ppermute(x, axis, [(i, i ^ mask) for i in range(lax.axis_size(axis))])  3.49 us
    ppermute x4, starting transfers between devices, swapped(): lax.ppermute(x, axis, [(i, i ^ mask) for i in range(lax.axis_size(axis))])  3.36 us
    ppermute x10, waiting for transfers between devices, paired(): return lax.ppermute(x, ('space', 'band'), route)  0.9 us
  transfers between devices with their start and end apart: 14, of which 7 were waited for; matrix products, arithmetic and copies ran while one was open for 0% of the time, Pallas kernels for 23%

profile of v7, /device:TPU:0, one launch (start us, length us, event | category | flops | bytes accessed | tf_op | source)
XLA Modules:
  0.0 38.4 jit_solution(14167268733282058315)
XLA Ops:
  0.6 1.0 %shard_map.104 = (bf16[32,1280]{1,0:T(8,128)(2,1)S(1)}, s32[1,256]{1,0:T(1,128)S(1)}, s32[9,216]{1,0:T(8,128)S(1)}, bf16[32,256]{1,0:T(8,128)(2,1)S(1)}, bf16[32,256]{1,0:T(8,128)(2,1)S(1)}) custom-call(bf16[32,1280]{1,0:T(8,128)(2,1)} %w_in.1, s32[1,256]{1,0:T(1,128)} %bitcast.8, s32[9,216]{1,0:T(8,128)} %links_in.1), custom_call_target="tpu_custom_call" | custom-call | flops 268435456 | bytes 1048576 | tf_op jit(solution)/shard_map/pallas_call | solution.py:53
  1.7 3.1 %collective-permute-start = (bf16[32,256]{1,0:T(8,128)(2,1)S(1)}, bf16[32,256]{1,0:T(8,128)(2,1)S(1)}, u32[]{:S(2)}, u32[]{:S(2)}) collective-permute-start(bf16[32,256]{1,0:T(8,128)(2,1)S(1)} %get-tuple-element.56), channel_id=1, source_target_pairs={{0,8},{1,9},{2,10},{3,11},{4,12},{5,13},{6,14},{7,15},{8,0},{9,1},... | collective-permute-start | bytes 49160 | tf_op jit(solution)/shard_map/ppermute | solution.py:457
  4.8 0.0 collective-permute-start.1
  4.8 0.1 add_convert_fusion.flags_ref
  4.8 1.8 %shard_map.105 = (bf16[2304,1280]{1,0:T(8,128)(2,1)S(1)}, bf16[2304,512]{1,0:T(8,128)(2,1)S(1)}, bf16[9,256,256]{2,1,0:T(8,128)(2,1)S(1)}, s16[16,2304]{1,0:T(8,...) custom-call(bf16[9,216,216]{2,1,0:T(8,128)(2,1)} %matrix_in.1, ...), custom_call_target="tpu_custom_call" | custom-call | flops 268435456 | bytes 1048576 | tf_op jit(solution)/shard_map/pallas_call | solution.py:53
  6.6 0.0 collective-permute-done.got_first
  6.6 0.0 collective-permute-done.1.got_second
  6.7 1.3 %shard_map.106 = (bf16[64,2304]{1,0:T(8,128)(2,1)S(1)}, f32[32,256]{1,0:T(8,128)S(1)}, f32[32,256]{1,0:T(8,128)S(1)}, f32[32,256]{1,0:T(8,128)S(1)}) custom-call(s32[3]{0:T(128)S(1)} %add_convert_fusion.flags_ref, bf16[32,2304]{1,0:T(8,128)(2,1)S(1)} %get-tuple-element.55.inner_values_ref, bf16[32,256]{1,0:T(8,128)(2,1)S(1)} %collective-permute-done.got_first, ...), custom_call_target="tpu_custom_call" | custom-call | flops 268435456 | bytes 1048576 | tf_op jit(solution)/shard_map/pallas_call | solution.py:53
  8.0 3.2 %collective-permute-start.2 = (f32[32,256]{1,0:T(8,128)S(1)}, f32[32,256]{1,0:T(8,128)S(1)}, u32[]{:S(2)}, u32[]{:S(2)}) collective-permute-start(f32[32,256]{1,0:T(8,128)S(1)} %get-tuple-element.62.sum_first), channel_id=1, source_target_pairs={{0,8},{1,9},{2,10},{3,11},{4,12},{5,13},{6,14},{7,15},{8,0},{9,1},... | collective-permute-start | bytes 98312 | tf_op jit(solution)/shard_map/ppermute | solution.py:457
  11.2 0.0 collective-permute-start.3
  11.2 1.9 %shard_map.107 = (f32[32,1280]{1,0:T(8,128)S(1)}, bf16[32,2304]{1,0:T(8,128)(2,1)S(1)}, f32[32,1280]{1,0:T(8,128)S(1)}, f32[8,1280]{1,0:T(8,128)S(1)}, s32[8,128...) custom-call(bf16[64,2304]{1,0:T(8,128)(2,1)S(1)} %get-tuple-element.65.parts_re, ...), custom_call_target="tpu_custom_call" | custom-call | flops 268435456 | bytes 1048576 | tf_op jit(solution)/shard_map/pallas_call | solution.py:53
  13.1 0.0 collective-permute-done.2.got_first
  13.1 0.0 collective-permute-done.3.got_second
  13.1 1.4 %shard_map.108 = (bf16[64,2304]{1,0:T(8,128)(2,1)S(1)}, f32[32,256]{1,0:T(8,128)S(1)}, f32[32,256]{1,0:T(8,128)S(1)}, f32[32,256]{1,0:T(8,128)S(1)}, f32[32,256]{1,0:T(8,128)S(1)}) custom-call(s32[3]{0:T(128)S(1)} %add_convert_fusion.flags_ref, f32[32,256]{1,0:T(8,128)S(1)} %collective-permute-done.2.got_first, ...), custom_call_target="tpu_custom_call" | custom-call | flops 268435456 | bytes 1048576 | tf_op jit(solution)/shard_map/pallas_call | solution.py:53
  14.5 2.2 %collective-permute-start.4 = (f32[32,256]{1,0:T(8,128)S(1)}, f32[32,256]{1,0:T(8,128)S(1)}, u32[]{:S(2)}, u32[]{:S(2)}) collective-permute-start(f32[32,256]{1,0:T(8,128)S(1)} %get-tuple-element.70.sum_first), channel_id=1, source_target_pairs={{0,8},{1,9},{2,10},{3,11},{4,12},{5,13},{6,14},{7,15},{8,0},{9,1},... | collective-permute-start | bytes 98312 | tf_op jit(solution)/shard_map/ppermute | solution.py:457
  16.7 0.0 collective-permute-start.5
  16.7 1.6 %shard_map.109 = (f32[32,1280]{1,0:T(8,128)S(1)}, bf16[32,2304]{1,0:T(8,128)(2,1)S(1)}) custom-call(bf16[64,2304]{1,0:T(8,128)(2,1)S(1)} %get-tuple-element.74.parts_ref, f32[32,1280]{1,0:T(8,128)S(1)} %get-tuple-element.75.state_ref.before_ref, f32[32,1280]{1,0:T(8,128)S(1)} %get-tuple-element.76.before_ref, ...), custom_call_target="tpu_custom_call" | custom-call | flops 268435456 | bytes 1048576 | tf_op jit(solution)/shard_map/pallas_call | solution.py:53
  18.3 0.3 collective-permute-done.4.got_first
  18.6 0.0 collective-permute-done.5.got_second
  18.6 1.4 %shard_map.110 = (bf16[64,2304]{1,0:T(8,128)(2,1)S(1)}, f32[32,256]{1,0:T(8,128)S(1)}, f32[32,256]{1,0:T(8,128)S(1)}, f32[32,256]{1,0:T(8,128)S(1)}, f32[32,256]{1,0:T(8,128)S(1)}) custom-call(s32[3]{0:T(128)S(1)} %add_convert_fusion.flags_ref, f32[32,256]{1,0:T(8,128)S(1)} %collective-permute-done.4.got_first, ...), custom_call_target="tpu_custom_call" | custom-call | flops 268435456 | bytes 1048576 | tf_op jit(solution)/shard_map/pallas_call | solution.py:53
  20.0 2.2 %collective-permute-start.6 = (f32[32,256]{1,0:T(8,128)S(1)}, f32[32,256]{1,0:T(8,128)S(1)}, u32[]{:S(2)}, u32[]{:S(2)}) collective-permute-start(f32[32,256]{1,0:T(8,128)S(1)} %get-tuple-element.79.sum_first), channel_id=1, source_target_pairs={{0,8},{1,9},{2,10},{3,11},{4,12},{5,13},{6,14},{7,15},{8,0},{9,1},... | collective-permute-start | bytes 98312 | tf_op jit(solution)/shard_map/ppermute | solution.py:457
  22.1 0.0 collective-permute-start.7
  22.2 1.6 %shard_map.111 = (f32[32,1280]{1,0:T(8,128)S(1)}, bf16[32,2304]{1,0:T(8,128)(2,1)S(1)}) custom-call(bf16[64,2304]{1,0:T(8,128)(2,1)S(1)} %get-tuple-element.83.parts_ref, f32[32,1280]{1,0:T(8,128)S(1)} %get-tuple-element.84.state_ref, f32[32,1280]{1,0:T(8,128)S(1)} %get-tuple-element.75.state_ref.before_ref, s16[16,2304]{1,0:T(8,128)(2,1)S(1)} %get-tuple-element.58.own_lane, ...), custom_call_target="tpu_custom_call" | custom-call | flops 268435456 | bytes 1048576 | tf_op jit(solution)/shard_map/pallas_call | solution.py:53
  23.7 0.0 copy-start.2
  23.7 0.3 collective-permute-done.6.got_first
  24.0 0.0 collective-permute-done.7.got_second
  24.0 0.0 copy-done
  24.0 0.0 copy-done.4
  24.1 1.1 %shard_map.112 = (f32[32,256]{1,0:T(8,128)S(1)}, bf16[32,2304]{1,0:T(8,128)(2,1)S(1)}, f32[288,343]{1,0:T(8,128)S(1)}, f32[9,343]{1,0:T(8,128)S(1)}) custom-call(s32[3]{0:T(128)S(1)} %add_convert_fusion.flags_ref, f32[32,256]{1,0:T(8,128)S(1)} %collective-permute-done.6.got_first, f32[32,256]{1,0:T(8,128)S(1)} %collective-permute-done.7.got_second, ...), custom_call_target="tpu_custom_call" | custom-call | flops 268435456 | bytes 1048576 | tf_op jit(solution)/shard_map/pallas_call | solution.py:53
  25.1 0.3 collective-permute-start.8
  25.4 1.0 %collective-permute-done.8 = f32[9,343]{1,0:T(8,128)S(1)} collective-permute-done((f32[9,343]{1,0:T(8,128)S(1)}, f32[9,343]{1,0:T(8,128)S(1)}, u32[]{:S(2)}, u32[]{:S(2)}) %collective-permute-start.8) | collective-permute-done | bytes 12380 | tf_op jit(solution)/shard_map/ppermute | solution.py:465
  26.4 2.3 %collective-permute-start.11 = (f32[9,343]{1,0:T(8,128)S(1)}, f32[9,343]{1,0:T(8,128)S(1)}, u32[]{:S(2)}, u32[]{:S(2)}) collective-permute-start(f32[9,343]{1,0:T(8,128)S(1)} %add.8.total_ref), channel_id=1, source_target_pairs={{0,7},{1,6},{2,5},{3,4},{4,3},{5,2},{6,1},{7,0},{8,15},{9,14},{10,... | collective-permute-start | bytes 37052 | tf_op jit(solution)/shard_map/ppermute | solution.py:465
  28.7 0.4 collective-permute-start.10
  29.1 0.4 collective-permute-start.9
  29.5 0.3 shard_map.113
  29.8 0.8 %collective-permute-done.11.rest_2_ = f32[9,343]{1,0:T(8,128)S(1)} collective-permute-done((f32[9,343]{1,0:T(8,128)S(1)}, f32[9,343]{1,0:T(8,128)S(1)}, u32[]{:S(2)}, u32[]{:S(2)}) %collective-permute-start.11) | collective-permute-done | bytes 12380 | tf_op jit(solution)/shard_map/ppermute | solution.py:465
  30.6 1.4 %collective-permute-done.10.rest_1_ = f32[9,343]{1,0:T(8,128)S(1)} collective-permute-done((f32[9,343]{1,0:T(8,128)S(1)}, f32[9,343]{1,0:T(8,128)S(1)}, u32[]{:S(2)}, u32[]{:S(2)}) %collective-permute-start.10) | collective-permute-done | bytes 12380 | tf_op jit(solution)/shard_map/ppermute | solution.py:465
  31.9 0.4 collective-permute-done.9.rest_0_
  32.3 0.0 copy-done.1
  32.3 0.0 copy-done.2
  32.3 0.6 %shard_map.114 = (f32[9,343]{1,0:T(8,128)S(1)}, bf16[64,2304]{1,0:T(8,128)(2,1)S(1)}, f32[32,256]{1,0:T(8,128)S(1)}, f32[32,256]{1,0:T(8,128)S(1)}) custom-call(f32[9,343]{1,0:T(8,128)S(1)} %add.8.total_ref, f32[9,343]{1,0:T(8,128)S(1)} %collective-permute-done.9.rest_0_, f32[9,343]{1,0:T(8,128)S(1)} %collective-permute-done.10.rest_1_, ...), custom_call_target="tpu_custom_call" | custom-call | flops 268435456 | bytes 1048576 | tf_op jit(solution)/shard_map/pallas_call | solution.py:53
  32.9 2.1 %collective-permute-start.12 = (f32[32,256]{1,0:T(8,128)S(1)}, f32[32,256]{1,0:T(8,128)S(1)}, u32[]{:S(2)}, u32[]{:S(2)}) collective-permute-start(f32[32,256]{1,0:T(8,128)S(1)} %get-tuple-element.91), channel_id=1, source_target_pairs={{0,8},{1,9},{2,10},{3,11},{4,12},{5,13},{6,14},{7,15},{8,0},{9,1},... | collective-permute-start | bytes 98312 | tf_op jit(solution)/shard_map/ppermute | solution.py:457
  35.1 0.0 collective-permute-start.13
  35.1 0.0 copy-done.3
  35.1 1.6 %shard_map.115 = (f32[32,1280]{1,0:T(8,128)S(1)}, f32[32,256]{1,0:T(8,128)S(1)}, f32[9,343]{1,0:T(8,128)}) custom-call(bf16[64,2304]{1,0:T(8,128)(2,1)S(1)} %get-tuple-element.93.parts_ref, f32[32,1280]{1,0:T(8,128)S(1)} %get-tuple-element.94.state_ref, f32[32,256]{1,0:T(8,128)S(1)} %get-tuple-element.95.face_ref, f32[1,32]{1,0:T(1,128)S(1)} %bitcast.6, ...), custom_call_target="tpu_custom_call" | custom-call | flops 268435456 | bytes 1048576 | tf_op jit(solution)/shard_map/pallas_call | solution.py:53
  36.7 0.3 collective-permute-done.12.got_first
  36.9 0.0 collective-permute-done.13.got_second
  37.0 1.4 %shard_map.116 = f32[32,1280]{1,0:T(8,128)} custom-call(s32[3]{0:T(128)S(1)} %add_convert_fusion.flags_ref, f32[32,256]{1,0:T(8,128)S(1)} %collective-permute-done.12.got_first, f32[32,256]{1,0:T(8,128)S(1)} %collective-permute-done.13.got_second, f32[32,1280]{1,0:T(8,128)S(1)} %get-tuple-element.97.partial_ref, f32[32,256]{1,0:T(8,128)S(1)} %get-tuple-element.98.shift_ref, ...), custom_call_target="tpu_custom_call" | custom-call | flops 268435456 | bytes 1048576 | tf_op jit(solution)/shard_map/pallas_call | solution.py:53
  (6 shorter events, 0.0 us)
Async XLA Ops:
  1.7 5.0 %collective-permute-start = (bf16[32,256]{1,0:T(8,128)(2,1)S(1)}, bf16[32,256]{1,0:T(8,128)(2,1)S(1)}, u32[]{:S(2)}, u32[]{:S(2)}) collective-permute-start(bf16[32,256]{1,0:T(8,128)(2,1)S(1)} %get-tuple-element.56), channel_id=1, source_target_pairs={{0,8},{1,9},{2,10},{3,11},{4,12},{5,13},{6,14},{7,15},{8,0},{9,1},... | collective-permute-start | bytes 49160 | tf_op jit(solution)/shard_map/ppermute | solution.py:457
  4.8 1.9 %collective-permute-start.1 = (bf16[32,256]{1,0:T(8,128)(2,1)S(1)}, bf16[32,256]{1,0:T(8,128)(2,1)S(1)}, u32[]{:S(2)}, u32[]{:S(2)}) collective-permute-start(bf16[32,256]{1,0:T(8,128)(2,1)S(1)} %get-tuple-element.57), channel_id=1, source_target_pairs={{0,1},{1,0},{2,3},{3,2},{4,5},{5,4},{6,7},{7,6},{8,16},{9,17},{10,... | collective-permute-start | bytes 49160 | tf_op jit(solution)/shard_map/ppermute | solution.py:457
  8.0 5.1 %collective-permute-start.2 = (f32[32,256]{1,0:T(8,128)S(1)}, f32[32,256]{1,0:T(8,128)S(1)}, u32[]{:S(2)}, u32[]{:S(2)}) collective-permute-start(f32[32,256]{1,0:T(8,128)S(1)} %get-tuple-element.62.sum_first), channel_id=1, source_target_pairs={{0,8},{1,9},{2,10},{3,11},{4,12},{5,13},{6,14},{7,15},{8,0},{9,1},... | collective-permute-start | bytes 98312 | tf_op jit(solution)/shard_map/ppermute | solution.py:457
  11.2 1.9 %collective-permute-start.3 = (f32[32,256]{1,0:T(8,128)S(1)}, f32[32,256]{1,0:T(8,128)S(1)}, u32[]{:S(2)}, u32[]{:S(2)}) collective-permute-start(f32[32,256]{1,0:T(8,128)S(1)} %get-tuple-element.63.sum_second), channel_id=1, source_target_pairs={{0,1},{1,0},{2,3},{3,2},{4,5},{5,4},{6,7},{7,6},{8,16},{9,17},{10,... | collective-permute-start | bytes 98312 | tf_op jit(solution)/shard_map/ppermute | solution.py:457
  14.5 4.1 %collective-permute-start.4 = (f32[32,256]{1,0:T(8,128)S(1)}, f32[32,256]{1,0:T(8,128)S(1)}, u32[]{:S(2)}, u32[]{:S(2)}) collective-permute-start(f32[32,256]{1,0:T(8,128)S(1)} %get-tuple-element.70.sum_first), channel_id=1, source_target_pairs={{0,8},{1,9},{2,10},{3,11},{4,12},{5,13},{6,14},{7,15},{8,0},{9,1},... | collective-permute-start | bytes 98312 | tf_op jit(solution)/shard_map/ppermute | solution.py:457
  16.7 1.9 %collective-permute-start.5 = (f32[32,256]{1,0:T(8,128)S(1)}, f32[32,256]{1,0:T(8,128)S(1)}, u32[]{:S(2)}, u32[]{:S(2)}) collective-permute-start(f32[32,256]{1,0:T(8,128)S(1)} %get-tuple-element.71.sum_second), channel_id=1, source_target_pairs={{0,1},{1,0},{2,3},{3,2},{4,5},{5,4},{6,7},{7,6},{8,16},{9,17},{10,... | collective-permute-start | bytes 98312 | tf_op jit(solution)/shard_map/ppermute | solution.py:457
  20.0 4.1 %collective-permute-start.6 = (f32[32,256]{1,0:T(8,128)S(1)}, f32[32,256]{1,0:T(8,128)S(1)}, u32[]{:S(2)}, u32[]{:S(2)}) collective-permute-start(f32[32,256]{1,0:T(8,128)S(1)} %get-tuple-element.79.sum_first), channel_id=1, source_target_pairs={{0,8},{1,9},{2,10},{3,11},{4,12},{5,13},{6,14},{7,15},{8,0},{9,1},... | collective-permute-start | bytes 98312 | tf_op jit(solution)/shard_map/ppermute | solution.py:457
  22.1 1.9 %collective-permute-start.7 = (f32[32,256]{1,0:T(8,128)S(1)}, f32[32,256]{1,0:T(8,128)S(1)}, u32[]{:S(2)}, u32[]{:S(2)}) collective-permute-start(f32[32,256]{1,0:T(8,128)S(1)} %get-tuple-element.80.sum_second), channel_id=1, source_target_pairs={{0,1},{1,0},{2,3},{3,2},{4,5},{5,4},{6,7},{7,6},{8,16},{9,17},{10,... | collective-permute-start | bytes 98312 | tf_op jit(solution)/shard_map/ppermute | solution.py:457
  22.1 1.9 %copy-start = (bf16[216,343]{1,0:T(8,128)(2,1)S(1)}, bf16[216,343]{1,0:T(8,128)(2,1)}, u32[]{:S(2)}) copy-start(bf16[216,343]{1,0:T(8,128)(2,1)} %basis_ref.3) | copy-start | bytes 444532
  22.1 1.9 %copy-start.4 = (f32[32]{0:T(128)S(1)}, f32[32]{0:T(128)}, u32[]{:S(2)}) copy-start(f32[32]{0:T(128)} %param.16) | copy-start | bytes 388
  23.7 8.6 %copy-start.1 = (f32[9,343]{1,0:T(8,128)S(1)}, f32[9,343]{1,0:T(8,128)}, u32[]{:S(2)}) copy-start(f32[9,343]{1,0:T(8,128)} %rest_3_.1) | copy-start | bytes 37048
  23.7 8.6 %copy-start.2 = (f32[9,343]{1,0:T(8,128)S(1)}, f32[9,343]{1,0:T(8,128)}, u32[]{:S(2)}) copy-start(f32[9,343]{1,0:T(8,128)} %rest_4_.1) | copy-start | bytes 37048
  25.1 1.3 %collective-permute-start.8 = (f32[9,343]{1,0:T(8,128)S(1)}, f32[9,343]{1,0:T(8,128)S(1)}, u32[]{:S(2)}, u32[]{:S(2)}) collective-permute-start(f32[9,343]{1,0:T(8,128)S(1)} %get-tuple-element.86), channel_id=1, source_target_pairs={{0,1},{1,0},{2,3},{3,2},{4,5},{5,4},{6,7},{7,6},{8,9},{9,8},{10,11... | collective-permute-start | bytes 37052 | tf_op jit(solution)/shard_map/ppermute | solution.py:465
  26.4 4.2 %collective-permute-start.11 = (f32[9,343]{1,0:T(8,128)S(1)}, f32[9,343]{1,0:T(8,128)S(1)}, u32[]{:S(2)}, u32[]{:S(2)}) collective-permute-start(f32[9,343]{1,0:T(8,128)S(1)} %add.8.total_ref), channel_id=1, source_target_pairs={{0,7},{1,6},{2,5},{3,4},{4,3},{5,2},{6,1},{7,0},{8,15},{9,14},{10,... | collective-permute-start | bytes 37052 | tf_op jit(solution)/shard_map/ppermute | solution.py:465
  28.7 3.3 %collective-permute-start.10 = (f32[9,343]{1,0:T(8,128)S(1)}, f32[9,343]{1,0:T(8,128)S(1)}, u32[]{:S(2)}, u32[]{:S(2)}) collective-permute-start(f32[9,343]{1,0:T(8,128)S(1)} %add.8.total_ref), channel_id=1, source_target_pairs={{0,5},{1,4},{2,7},{3,6},{4,1},{5,0},{6,3},{7,2},{8,13},{9,12},{10,... | collective-permute-start | bytes 37052 | tf_op jit(solution)/shard_map/ppermute | solution.py:465
  29.1 3.3 %collective-permute-start.9 = (f32[9,343]{1,0:T(8,128)S(1)}, f32[9,343]{1,0:T(8,128)S(1)}, u32[]{:S(2)}, u32[]{:S(2)}) collective-permute-start(f32[9,343]{1,0:T(8,128)S(1)} %add.8.total_ref), channel_id=1, source_target_pairs={{0,3},{1,2},{2,1},{3,0},{4,7},{5,6},{6,5},{7,4},{8,11},{9,10},{10,... | collective-permute-start | bytes 37052 | tf_op jit(solution)/shard_map/ppermute | solution.py:465
  29.5 5.6 %copy-start.3 = (f32[32]{0:T(128)S(1)}, f32[32]{0:T(128)}, u32[]{:S(2)}) copy-start(f32[32]{0:T(128)} %param.17) | copy-start | bytes 388
  32.9 4.0 %collective-permute-start.12 = (f32[32,256]{1,0:T(8,128)S(1)}, f32[32,256]{1,0:T(8,128)S(1)}, u32[]{:S(2)}, u32[]{:S(2)}) collective-permute-start(f32[32,256]{1,0:T(8,128)S(1)} %get-tuple-element.91), channel_id=1, source_target_pairs={{0,8},{1,9},{2,10},{3,11},{4,12},{5,13},{6,14},{7,15},{8,0},{9,1},... | collective-permute-start | bytes 98312 | tf_op jit(solution)/shard_map/ppermute | solution.py:457
  35.1 1.9 %collective-permute-start.13 = (f32[32,256]{1,0:T(8,128)S(1)}, f32[32,256]{1,0:T(8,128)S(1)}, u32[]{:S(2)}, u32[]{:S(2)}) collective-permute-start(f32[32,256]{1,0:T(8,128)S(1)} %get-tuple-element.92), channel_id=1, source_target_pairs={{0,1},{1,0},{2,3},{3,2},{4,5},{5,4},{6,7},{7,6},{8,16},{9,17},{10,... | collective-permute-start | bytes 98312 | tf_op jit(solution)/shard_map/ppermute | solution.py:457

commit v8 on v7

--- a/solution.py
+++ b/solution.py
@@ -102,14 +102,16 @@
     return (index & (LANES - 1)).astype(dtype), (index >> 7).astype(dtype)
 
 
-def pick_kernel(w_in, face_in, links_in, w_ref, face_ref, links_ref, out_ref, twin_ref, sems):
-    pairs = ((w_in, w_ref), (face_in, face_ref), (links_in, links_ref))
+def pick_kernel(
+    w_in, face_in, links_in, matrix_in, w_ref, face_ref, links_ref, out_ref, twin_ref, matrix_ref, sems
+):
+    pairs = ((w_in, w_ref), (face_in, face_ref), (links_in, links_ref), (matrix_in, matrix_ref))
     copies = [
         pltpu.make_async_copy(source, target, sems.at[i]) for i, (source, target) in enumerate(pairs)
     ]
     for copy in copies:
         copy.start()
-    for copy in copies:
+    for copy in copies[:2]:
         copy.wait()
     count = face_ref.shape[1]
     w = w_ref[...]
@@ -120,6 +122,8 @@
             picked = gathered(w[row : row + ROWS], lane, block)
             out_ref[row : row + ROWS, start : start + LANES] = picked
             twin_ref[row : row + ROWS, start : start + LANES] = picked
+    for copy in copies[2:]:
+        copy.wait()
 
 
 def short_one_hot(left, right):
@@ -131,12 +135,10 @@
 
 
 def tables_kernel(
-    matrix_in, w_ref, face_ref, links_ref,
-    from_own_ref, from_edge_ref, padded_ref, own_lane, own_block, values_ref,
-    row_ref, turn_ref, wide_ref, matrix_ref, sem,
-):
-    copy = pltpu.make_async_copy(matrix_in, matrix_ref, sem)
-    copy.start()
+    w_ref, face_ref, links_ref,
+    from_own_ref, from_edge_ref, own_lane, own_block, values_ref,
+    row_ref, turn_ref,
+):
     slots, owned = from_own_ref.shape
     count = face_ref.shape[1]
     cells, nodes = links_ref.shape
@@ -179,20 +181,9 @@
             rows = slice(cell * pitch + start, cell * pitch + start + ROWS)
             from_own_ref[rows, :] = short_one_hot(across(block, owned), own_row)
 
-    wide_ref[...] = jnp.zeros_like(wide_ref)
-    copy.wait()
-    for cell in range(cells):
-        wide_ref[cell % 2, :nodes, :nodes] = matrix_ref[cell].astype(f32)
-        padded_ref[cell] = wide_ref[cell % 2].astype(bf16)
-
 
 def store(ref, rows, columns, values):
     ref[rows, columns] = values
-
-
-def cell_block(values, matrix_ref, cell):
-    pitch = matrix_ref.shape[1]
-    return dot(values[:, cell * pitch : (cell + 1) * pitch], matrix_ref[cell])
 
 
 def put_parts(parts_ref, cell, pitch, block):
@@ -228,10 +219,14 @@
     flags_ref, edge, inner_values_ref, edge_lane, edge_block, matrix_ref, from_edge_ref,
     parts_ref, first_ref, second_ref, before=0,
 ):
-    cells, pitch, _ = matrix_ref.shape
+    cells, nodes, _ = matrix_ref.shape
+    pitch = parts_ref.shape[1] // cells
     for cell in range(cells):
         values = cell_values(edge, inner_values_ref, edge_lane, edge_block, cell, pitch, before)
-        parts_ref[:, cell * pitch : (cell + 1) * pitch] = halves(dot(values, matrix_ref[cell]))
+        tail = slice((cell + 1) * pitch - LANES, (cell + 1) * pitch)
+        parts_ref[:, tail] = jnp.zeros((parts_ref.shape[0], LANES), bf16)
+        columns = slice(cell * pitch, cell * pitch + nodes)
+        parts_ref[:, columns] = halves(dot(values[:, :nodes], matrix_ref[cell]))
     sums = joined(dot(parts_ref[...], from_edge_ref[...]))
     count = first_ref.shape[1]
     first_ref[...], second_ref[...] = chosen(flags_ref, sums[:, :count], sums[:, count:])
@@ -365,10 +360,12 @@
 def products_kernel(
     values_ref, matrix_ref, basis_ref, product_ref, wide_basis_ref, wide_ref
 ):
-    cells, pitch, _ = matrix_ref.shape
-    values = values_ref[...]
-    for cell in range(cells):
-        product_ref[:, cell * pitch : (cell + 1) * pitch] = cell_block(values, matrix_ref, cell)
+    cells, nodes, _ = matrix_ref.shape
+    pitch = product_ref.shape[1] // cells
+    product_ref[...] = jnp.zeros_like(product_ref)
+    for cell in range(cells):
+        columns = slice(cell * pitch, cell * pitch + nodes)
+        product_ref[:, columns] = dot(values_ref[:, columns], matrix_ref[cell])
     nodes = basis_ref.shape[0]
     wide_ref[...] = jnp.zeros_like(wide_ref)
     wide_ref[:nodes, :] = basis_ref[...].astype(f32)
@@ -513,7 +510,7 @@
     state_out = ((waves, owned), f32)
 
     index_out = ((ROWS, slots), jnp.int16)
-    w, faces, links, start_face, start_twin = call(
+    w, faces, links, start_face, start_twin, matrix = call(
         pick_kernel,
         [
             (wavefunctions.shape, bf16),
@@ -521,37 +518,32 @@
             (connectivity.shape, jnp.int32),
             ((waves, count), bf16),
             ((waves, count), bf16),
+            (cell_hamiltonian.shape, bf16),
         ],
-        wavefunctions, face_nodes.reshape(1, count), connectivity,
-        held=3, scratch=[pltpu.SemaphoreType.DMA((3,))], room=56,
+        wavefunctions, face_nodes.reshape(1, count), connectivity, cell_hamiltonian,
+        held=4, scratch=[pltpu.SemaphoreType.DMA((4,))], room=56,
     )
     start_pair = exchanged(start_twin, start_face)
     (
-        from_own, from_edge, padded, own_lane, own_block, values
+        from_own, from_edge, own_lane, own_block, values
     ) = call(
         tables_kernel,
         [
             ((slots, owned), bf16),
             ((slots, 2 * count), bf16),
-            ((cells, pitch, pitch), bf16),
             *[index_out] * 2,
             values_out,
         ],
-        cell_hamiltonian, w, faces, links,
-        held=1,
+        w, faces, links,
         scratch=[
             pltpu.VMEM((ROWS, slots), jnp.int32),
             pltpu.VMEM((-(-cells // LANES) * LANES, pitch), f32),
-            pltpu.VMEM((2, pitch, pitch), f32),
-            pltpu.VMEM(cell_hamiltonian.shape, bf16),
-            pltpu.SemaphoreType.DMA,
         ],
-        room=44,
     )
     parts, *sums, ghost = call(
         first_kernel,
         [parts_out, *edge_out, edge_out[0]],
-        flags, values, *start_pair, own_lane, own_block, padded, from_edge, smem=1,
+        flags, values, *start_pair, own_lane, own_block, matrix, from_edge, smem=1,
     )
     face = start_face.astype(f32)
     before_edge = ()
@@ -586,7 +578,7 @@
             parts, *sums, new_ghost, new_face = call(
                 functools.partial(edge_kernel, scale, step > 0),
                 [parts_out, *edge_out, *edge_out],
-                *received, values, edge_lane, edge_block, padded, from_edge, smem=1,
+                *received, values, edge_lane, edge_block, matrix, from_edge, smem=1,
             )
             before_edge, ghost, face = (ghost, face), new_ghost, new_face
         else:
@@ -600,7 +592,7 @@
     products, wide_basis = call(
         products_kernel,
         [((waves, slots), f32), ((pitch, points), bf16)],
-        final, padded, basis_values, scratch=[pltpu.VMEM((pitch, points), f32)],
+        final, matrix, basis_values, scratch=[pltpu.VMEM((pitch, points), f32)],
     )
     totals = band_parts(band, "band")
     potential, parts, *sums = call(

time: 38.5 us -> 38.4 us (level)
  transfers between devices with their start and end apart: 14 -> 14, of which waited for: 7 -> 8; matrix products, arithmetic and copies ran while one was open for 0% -> 0% of each run, Pallas kernels for 23% -> 22%
where the time goes in v8:
time: 38.4 us; the launch traced here: 38.3 us
  Pallas kernels  16.9 us (44%)
  starting transfers between devices  16.1 us (42%)
  waiting for transfers between devices  4.48 us (12%)
  between operations  0.73 us (2%)
    pallas_call x13, Pallas kernels, call(): pl.pallas_call(kernel, out_shape=[pltpu.VMEM(*out) for out in outs[:kept]...  16.9 us
    ppermute x10, starting transfers between devices, paired(): return lax.ppermute(x, ('space', 'band'), route)  12.7 us
    ppermute x4, waiting for transfers between devices, swapped(): lax.ppermute(x, axis, [(i, i ^ mask) for i in range(lax.axis_size(axis))])  3.51 us
    ppermute x4, starting transfers between devices, swapped(): lax.ppermute(x, axis, [(i, i ^ mask) for i in range(lax.axis_size(axis))])  3.36 us
    ppermute x10, waiting for transfers between devices, paired(): return lax.ppermute(x, ('space', 'band'), route)  0.97 us
  transfers between devices with their start and end apart: 14, of which 8 were waited for; matrix products, arithmetic and copies ran while one was open for 0% of the time, Pallas kernels for 22%

profile of v8, /device:TPU:0, one launch (start us, length us, event | category | flops | bytes accessed | tf_op | source)
XLA Modules:
  0.0 38.3 jit_solution(5455114905601411378)
XLA Ops:
  0.6 1.3 %shard_map.104 = (bf16[32,1280]{1,0:T(8,128)(2,1)S(1)}, s32[1,256]{1,0:T(1,128)S(1)}, s32[9,216]{1,0:T(8,128)S(1)}, bf16[32,256]{1,0:T(8,128)(2,1)S(1)}, bf16[32...) custom-call(bf16[32,1280]{1,0:T(8,128)(2,1)} %w_in.1, s32[1,256]{1,0:T(1,128)} %bitcast.8, s32[9,216]{1,0:T(8,128)} %links_in.1, ...), custom_call_target="tpu_custom_call" | custom-call | flops 268435456 | bytes 1048576 | tf_op jit(solution)/shard_map/pallas_call | solution.py:53
  2.0 3.1 %collective-permute-start = (bf16[32,256]{1,0:T(8,128)(2,1)S(1)}, bf16[32,256]{1,0:T(8,128)(2,1)S(1)}, u32[]{:S(2)}, u32[]{:S(2)}) collective-permute-start(bf16[32,256]{1,0:T(8,128)(2,1)S(1)} %get-tuple-element.56), channel_id=1, source_target_pairs={{0,8},{1,9},{2,10},{3,11},{4,12},{5,13},{6,14},{7,15},{8,0},{9,1},... | collective-permute-start | bytes 49160 | tf_op jit(solution)/shard_map/ppermute | solution.py:454
  5.1 0.0 collective-permute-start.1
  5.1 0.1 add_convert_fusion.flags_ref
  5.1 1.5 %shard_map.105 = (bf16[2304,1280]{1,0:T(8,128)(2,1)S(1)}, bf16[2304,512]{1,0:T(8,128)(2,1)S(1)}, s16[16,2304]{1,0:T(8,128)(2,1)S(1)}, s16[16,2304]{1,0:T(8,128)(2,1)S(1)}, bf16[32,2304]{1,0:T(8,128)(2,1)S(1)}) custom-call(bf16[32,1280]{1,0:T(8,128)(2,1)S(1)} %get-tuple-element.52.w_ref, s32[1,256]{1,0:T(1,128)S(1)} %get-tuple-element.53.face_ref, ...), custom_call_target="tpu_custom_call" | custom-call | flops 268435456 | bytes 1048576 | tf_op jit(solution)/shard_map/pallas_call | solution.py:53
  6.6 0.1 collective-permute-done.got_first
  6.8 0.0 collective-permute-done.1.got_second
  6.8 1.2 %shard_map.106 = (bf16[64,2304]{1,0:T(8,128)(2,1)S(1)}, f32[32,256]{1,0:T(8,128)S(1)}, f32[32,256]{1,0:T(8,128)S(1)}, f32[32,256]{1,0:T(8,128)S(1)}) custom-call(s32[3]{0:T(128)S(1)} %add_convert_fusion.flags_ref, bf16[32,2304]{1,0:T(8,128)(2,1)S(1)} %get-tuple-element.55.inner_values_ref, bf16[32,256]{1,0:T(8,128)(2,1)S(1)} %collective-permute-done.got_first, ...), custom_call_target="tpu_custom_call" | custom-call | flops 268435456 | bytes 1048576 | tf_op jit(solution)/shard_map/pallas_call | solution.py:53
  8.0 3.2 %collective-permute-start.2 = (f32[32,256]{1,0:T(8,128)S(1)}, f32[32,256]{1,0:T(8,128)S(1)}, u32[]{:S(2)}, u32[]{:S(2)}) collective-permute-start(f32[32,256]{1,0:T(8,128)S(1)} %get-tuple-element.62.sum_first), channel_id=1, source_target_pairs={{0,8},{1,9},{2,10},{3,11},{4,12},{5,13},{6,14},{7,15},{8,0},{9,1},... | collective-permute-start | bytes 98312 | tf_op jit(solution)/shard_map/ppermute | solution.py:454
  11.2 0.0 collective-permute-start.3
  11.2 1.9 %shard_map.107 = (f32[32,1280]{1,0:T(8,128)S(1)}, bf16[32,2304]{1,0:T(8,128)(2,1)S(1)}, f32[32,1280]{1,0:T(8,128)S(1)}, f32[8,1280]{1,0:T(8,128)S(1)}, s32[8,128...) custom-call(bf16[64,2304]{1,0:T(8,128)(2,1)S(1)} %get-tuple-element.65.parts_re, ...), custom_call_target="tpu_custom_call" | custom-call | flops 268435456 | bytes 1048576 | tf_op jit(solution)/shard_map/pallas_call | solution.py:53
  13.1 0.0 collective-permute-done.2.got_first
  13.1 0.0 collective-permute-done.3.got_second
  13.1 1.4 %shard_map.108 = (bf16[64,2304]{1,0:T(8,128)(2,1)S(1)}, f32[32,256]{1,0:T(8,128)S(1)}, f32[32,256]{1,0:T(8,128)S(1)}, f32[32,256]{1,0:T(8,128)S(1)}, f32[32,256]{1,0:T(8,128)S(1)}) custom-call(s32[3]{0:T(128)S(1)} %add_convert_fusion.flags_ref, f32[32,256]{1,0:T(8,128)S(1)} %collective-permute-done.2.got_first, ...), custom_call_target="tpu_custom_call" | custom-call | flops 268435456 | bytes 1048576 | tf_op jit(solution)/shard_map/pallas_call | solution.py:53
  14.5 2.2 %collective-permute-start.4 = (f32[32,256]{1,0:T(8,128)S(1)}, f32[32,256]{1,0:T(8,128)S(1)}, u32[]{:S(2)}, u32[]{:S(2)}) collective-permute-start(f32[32,256]{1,0:T(8,128)S(1)} %get-tuple-element.70.sum_first), channel_id=1, source_target_pairs={{0,8},{1,9},{2,10},{3,11},{4,12},{5,13},{6,14},{7,15},{8,0},{9,1},... | collective-permute-start | bytes 98312 | tf_op jit(solution)/shard_map/ppermute | solution.py:454
  16.6 0.0 collective-permute-start.5
  16.6 1.6 %shard_map.109 = (f32[32,1280]{1,0:T(8,128)S(1)}, bf16[32,2304]{1,0:T(8,128)(2,1)S(1)}) custom-call(bf16[64,2304]{1,0:T(8,128)(2,1)S(1)} %get-tuple-element.74.parts_ref, f32[32,1280]{1,0:T(8,128)S(1)} %get-tuple-element.75.state_ref.before_ref, f32[32,1280]{1,0:T(8,128)S(1)} %get-tuple-element.76.before_ref, ...), custom_call_target="tpu_custom_call" | custom-call | flops 268435456 | bytes 1048576 | tf_op jit(solution)/shard_map/pallas_call | solution.py:53
  18.2 0.0 copy-start.4
  18.2 0.3 collective-permute-done.4.got_first
  18.5 0.0 collective-permute-done.5.got_second
  18.5 1.4 %shard_map.110 = (bf16[64,2304]{1,0:T(8,128)(2,1)S(1)}, f32[32,256]{1,0:T(8,128)S(1)}, f32[32,256]{1,0:T(8,128)S(1)}, f32[32,256]{1,0:T(8,128)S(1)}, f32[32,256]{1,0:T(8,128)S(1)}) custom-call(s32[3]{0:T(128)S(1)} %add_convert_fusion.flags_ref, f32[32,256]{1,0:T(8,128)S(1)} %collective-permute-done.4.got_first, ...), custom_call_target="tpu_custom_call" | custom-call | flops 268435456 | bytes 1048576 | tf_op jit(solution)/shard_map/pallas_call | solution.py:53
  19.9 2.2 %collective-permute-start.6 = (f32[32,256]{1,0:T(8,128)S(1)}, f32[32,256]{1,0:T(8,128)S(1)}, u32[]{:S(2)}, u32[]{:S(2)}) collective-permute-start(f32[32,256]{1,0:T(8,128)S(1)} %get-tuple-element.79.sum_first), channel_id=1, source_target_pairs={{0,8},{1,9},{2,10},{3,11},{4,12},{5,13},{6,14},{7,15},{8,0},{9,1},... | collective-permute-start | bytes 98312 | tf_op jit(solution)/shard_map/ppermute | solution.py:454
  22.0 0.0 collective-permute-start.7
  22.0 1.6 %shard_map.111 = (f32[32,1280]{1,0:T(8,128)S(1)}, bf16[32,2304]{1,0:T(8,128)(2,1)S(1)}) custom-call(bf16[64,2304]{1,0:T(8,128)(2,1)S(1)} %get-tuple-element.83.parts_ref, f32[32,1280]{1,0:T(8,128)S(1)} %get-tuple-element.84.state_ref, f32[32,1280]{1,0:T(8,128)S(1)} %get-tuple-element.75.state_ref.before_ref, s16[16,2304]{1,0:T(8,128)(2,1)S(1)} %get-tuple-element.58.own_lane, ...), custom_call_target="tpu_custom_call" | custom-call | flops 268435456 | bytes 1048576 | tf_op jit(solution)/shard_map/pallas_call | solution.py:53
  23.6 0.3 collective-permute-done.6.got_first
  23.9 0.0 collective-permute-done.7.got_second
  23.9 0.0 copy-done
  23.9 0.0 copy-done.4
  23.9 1.1 %shard_map.112 = (f32[32,256]{1,0:T(8,128)S(1)}, bf16[32,2304]{1,0:T(8,128)(2,1)S(1)}, f32[288,343]{1,0:T(8,128)S(1)}, f32[9,343]{1,0:T(8,128)S(1)}) custom-call(s32[3]{0:T(128)S(1)} %add_convert_fusion.flags_ref, f32[32,256]{1,0:T(8,128)S(1)} %collective-permute-done.6.got_first, f32[32,256]{1,0:T(8,128)S(1)} %collective-permute-done.7.got_second, ...), custom_call_target="tpu_custom_call" | custom-call | flops 268435456 | bytes 1048576 | tf_op jit(solution)/shard_map/pallas_call | solution.py:53
  25.0 0.3 collective-permute-start.8
  25.3 1.0 %collective-permute-done.8 = f32[9,343]{1,0:T(8,128)S(1)} collective-permute-done((f32[9,343]{1,0:T(8,128)S(1)}, f32[9,343]{1,0:T(8,128)S(1)}, u32[]{:S(2)}, u32[]{:S(2)}) %collective-permute-start.8) | collective-permute-done | bytes 12380 | tf_op jit(solution)/shard_map/ppermute | solution.py:462
  26.3 2.3 %collective-permute-start.11 = (f32[9,343]{1,0:T(8,128)S(1)}, f32[9,343]{1,0:T(8,128)S(1)}, u32[]{:S(2)}, u32[]{:S(2)}) collective-permute-start(f32[9,343]{1,0:T(8,128)S(1)} %add.8.total_ref), channel_id=1, source_target_pairs={{0,7},{1,6},{2,5},{3,4},{4,3},{5,2},{6,1},{7,0},{8,15},{9,14},{10,... | collective-permute-start | bytes 37052 | tf_op jit(solution)/shard_map/ppermute | solution.py:462
  28.6 0.4 collective-permute-start.10
  29.0 0.4 collective-permute-start.9
  29.4 0.3 shard_map.113
  29.7 0.8 %collective-permute-done.11.rest_2_ = f32[9,343]{1,0:T(8,128)S(1)} collective-permute-done((f32[9,343]{1,0:T(8,128)S(1)}, f32[9,343]{1,0:T(8,128)S(1)}, u32[]{:S(2)}, u32[]{:S(2)}) %collective-permute-start.11) | collective-permute-done | bytes 12380 | tf_op jit(solution)/shard_map/ppermute | solution.py:462
  30.5 1.4 %collective-permute-done.10.rest_1_ = f32[9,343]{1,0:T(8,128)S(1)} collective-permute-done((f32[9,343]{1,0:T(8,128)S(1)}, f32[9,343]{1,0:T(8,128)S(1)}, u32[]{:S(2)}, u32[]{:S(2)}) %collective-permute-start.10) | collective-permute-done | bytes 12380 | tf_op jit(solution)/shard_map/ppermute | solution.py:462
  31.9 0.4 collective-permute-done.9.rest_0_
  32.2 0.0 copy-done.1
  32.2 0.0 copy-done.2
  32.2 0.6 %shard_map.114 = (f32[9,343]{1,0:T(8,128)S(1)}, bf16[64,2304]{1,0:T(8,128)(2,1)S(1)}, f32[32,256]{1,0:T(8,128)S(1)}, f32[32,256]{1,0:T(8,128)S(1)}) custom-call(f32[9,343]{1,0:T(8,128)S(1)} %add.8.total_ref, f32[9,343]{1,0:T(8,128)S(1)} %collective-permute-done.9.rest_0_, f32[9,343]{1,0:T(8,128)S(1)} %collective-permute-done.10.rest_1_, ...), custom_call_target="tpu_custom_call" | custom-call | flops 268435456 | bytes 1048576 | tf_op jit(solution)/shard_map/pallas_call | solution.py:53
  32.9 2.1 %collective-permute-start.12 = (f32[32,256]{1,0:T(8,128)S(1)}, f32[32,256]{1,0:T(8,128)S(1)}, u32[]{:S(2)}, u32[]{:S(2)}) collective-permute-start(f32[32,256]{1,0:T(8,128)S(1)} %get-tuple-element.91), channel_id=1, source_target_pairs={{0,8},{1,9},{2,10},{3,11},{4,12},{5,13},{6,14},{7,15},{8,0},{9,1},... | collective-permute-start | bytes 98312 | tf_op jit(solution)/shard_map/ppermute | solution.py:454
  35.0 0.0 collective-permute-start.13
  35.0 0.0 copy-done.3
  35.0 1.6 %shard_map.115 = (f32[32,1280]{1,0:T(8,128)S(1)}, f32[32,256]{1,0:T(8,128)S(1)}, f32[9,343]{1,0:T(8,128)}) custom-call(bf16[64,2304]{1,0:T(8,128)(2,1)S(1)} %get-tuple-element.93.parts_ref, f32[32,1280]{1,0:T(8,128)S(1)} %get-tuple-element.94.state_ref, f32[32,256]{1,0:T(8,128)S(1)} %get-tuple-element.95.face_ref, f32[1,32]{1,0:T(1,128)S(1)} %bitcast.6, ...), custom_call_target="tpu_custom_call" | custom-call | flops 268435456 | bytes 1048576 | tf_op jit(solution)/shard_map/pallas_call | solution.py:53
  36.6 0.2 collective-permute-done.12.got_first
  36.9 0.0 collective-permute-done.13.got_second
  36.9 1.4 %shard_map.116 = f32[32,1280]{1,0:T(8,128)} custom-call(s32[3]{0:T(128)S(1)} %add_convert_fusion.flags_ref, f32[32,256]{1,0:T(8,128)S(1)} %collective-permute-done.12.got_first, f32[32,256]{1,0:T(8,128)S(1)} %collective-permute-done.13.got_second, f32[32,1280]{1,0:T(8,128)S(1)} %get-tuple-element.97.partial_ref, f32[32,256]{1,0:T(8,128)S(1)} %get-tuple-element.98.shift_ref, ...), custom_call_target="tpu_custom_call" | custom-call | flops 268435456 | bytes 1048576 | tf_op jit(solution)/shard_map/pallas_call | solution.py:53
  (6 shorter events, 0.0 us)
Async XLA Ops:
  2.0 4.8 %collective-permute-start = (bf16[32,256]{1,0:T(8,128)(2,1)S(1)}, bf16[32,256]{1,0:T(8,128)(2,1)S(1)}, u32[]{:S(2)}, u32[]{:S(2)}) collective-permute-start(bf16[32,256]{1,0:T(8,128)(2,1)S(1)} %get-tuple-element.56), channel_id=1, source_target_pairs={{0,8},{1,9},{2,10},{3,11},{4,12},{5,13},{6,14},{7,15},{8,0},{9,1},... | collective-permute-start | bytes 49160 | tf_op jit(solution)/shard_map/ppermute | solution.py:454
  5.1 1.7 %collective-permute-start.1 = (bf16[32,256]{1,0:T(8,128)(2,1)S(1)}, bf16[32,256]{1,0:T(8,128)(2,1)S(1)}, u32[]{:S(2)}, u32[]{:S(2)}) collective-permute-start(bf16[32,256]{1,0:T(8,128)(2,1)S(1)} %get-tuple-element.57), channel_id=1, source_target_pairs={{0,1},{1,0},{2,3},{3,2},{4,5},{5,4},{6,7},{7,6},{8,16},{9,17},{10,... | collective-permute-start | bytes 49160 | tf_op jit(solution)/shard_map/ppermute | solution.py:454
  8.0 5.1 %collective-permute-start.2 = (f32[32,256]{1,0:T(8,128)S(1)}, f32[32,256]{1,0:T(8,128)S(1)}, u32[]{:S(2)}, u32[]{:S(2)}) collective-permute-start(f32[32,256]{1,0:T(8,128)S(1)} %get-tuple-element.62.sum_first), channel_id=1, source_target_pairs={{0,8},{1,9},{2,10},{3,11},{4,12},{5,13},{6,14},{7,15},{8,0},{9,1},... | collective-permute-start | bytes 98312 | tf_op jit(solution)/shard_map/ppermute | solution.py:454
  11.2 1.9 %collective-permute-start.3 = (f32[32,256]{1,0:T(8,128)S(1)}, f32[32,256]{1,0:T(8,128)S(1)}, u32[]{:S(2)}, u32[]{:S(2)}) collective-permute-start(f32[32,256]{1,0:T(8,128)S(1)} %get-tuple-element.63.sum_second), channel_id=1, source_target_pairs={{0,1},{1,0},{2,3},{3,2},{4,5},{5,4},{6,7},{7,6},{8,16},{9,17},{10,... | collective-permute-start | bytes 98312 | tf_op jit(solution)/shard_map/ppermute | solution.py:454
  14.5 4.1 %collective-permute-start.4 = (f32[32,256]{1,0:T(8,128)S(1)}, f32[32,256]{1,0:T(8,128)S(1)}, u32[]{:S(2)}, u32[]{:S(2)}) collective-permute-start(f32[32,256]{1,0:T(8,128)S(1)} %get-tuple-element.70.sum_first), channel_id=1, source_target_pairs={{0,8},{1,9},{2,10},{3,11},{4,12},{5,13},{6,14},{7,15},{8,0},{9,1},... | collective-permute-start | bytes 98312 | tf_op jit(solution)/shard_map/ppermute | solution.py:454
  16.6 1.9 %collective-permute-start.5 = (f32[32,256]{1,0:T(8,128)S(1)}, f32[32,256]{1,0:T(8,128)S(1)}, u32[]{:S(2)}, u32[]{:S(2)}) collective-permute-start(f32[32,256]{1,0:T(8,128)S(1)} %get-tuple-element.71.sum_second), channel_id=1, source_target_pairs={{0,1},{1,0},{2,3},{3,2},{4,5},{5,4},{6,7},{7,6},{8,16},{9,17},{10,... | collective-permute-start | bytes 98312 | tf_op jit(solution)/shard_map/ppermute | solution.py:454
  18.2 5.7 %copy-start = (bf16[216,343]{1,0:T(8,128)(2,1)S(1)}, bf16[216,343]{1,0:T(8,128)(2,1)}, u32[]{:S(2)}) copy-start(bf16[216,343]{1,0:T(8,128)(2,1)} %basis_ref.3) | copy-start | bytes 444532
  18.2 5.7 %copy-start.4 = (f32[32]{0:T(128)S(1)}, f32[32]{0:T(128)}, u32[]{:S(2)}) copy-start(f32[32]{0:T(128)} %param.16) | copy-start | bytes 388
  18.5 13.7 %copy-start.1 = (f32[9,343]{1,0:T(8,128)S(1)}, f32[9,343]{1,0:T(8,128)}, u32[]{:S(2)}) copy-start(f32[9,343]{1,0:T(8,128)} %rest_3_.1) | copy-start | bytes 37048
  18.5 13.7 %copy-start.2 = (f32[9,343]{1,0:T(8,128)S(1)}, f32[9,343]{1,0:T(8,128)}, u32[]{:S(2)}) copy-start(f32[9,343]{1,0:T(8,128)} %rest_4_.1) | copy-start | bytes 37048
  19.9 4.0 %collective-permute-start.6 = (f32[32,256]{1,0:T(8,128)S(1)}, f32[32,256]{1,0:T(8,128)S(1)}, u32[]{:S(2)}, u32[]{:S(2)}) collective-permute-start(f32[32,256]{1,0:T(8,128)S(1)} %get-tuple-element.79.sum_first), channel_id=1, source_target_pairs={{0,8},{1,9},{2,10},{3,11},{4,12},{5,13},{6,14},{7,15},{8,0},{9,1},... | collective-permute-start | bytes 98312 | tf_op jit(solution)/shard_map/ppermute | solution.py:454
  22.0 1.9 %collective-permute-start.7 = (f32[32,256]{1,0:T(8,128)S(1)}, f32[32,256]{1,0:T(8,128)S(1)}, u32[]{:S(2)}, u32[]{:S(2)}) collective-permute-start(f32[32,256]{1,0:T(8,128)S(1)} %get-tuple-element.80.sum_second), channel_id=1, source_target_pairs={{0,1},{1,0},{2,3},{3,2},{4,5},{5,4},{6,7},{7,6},{8,16},{9,17},{10,... | collective-permute-start | bytes 98312 | tf_op jit(solution)/shard_map/ppermute | solution.py:454
  22.0 12.9 %copy-start.3 = (f32[32]{0:T(128)S(1)}, f32[32]{0:T(128)}, u32[]{:S(2)}) copy-start(f32[32]{0:T(128)} %param.17) | copy-start | bytes 388
  25.0 1.3 %collective-permute-start.8 = (f32[9,343]{1,0:T(8,128)S(1)}, f32[9,343]{1,0:T(8,128)S(1)}, u32[]{:S(2)}, u32[]{:S(2)}) collective-permute-start(f32[9,343]{1,0:T(8,128)S(1)} %get-tuple-element.86), channel_id=1, source_target_pairs={{0,1},{1,0},{2,3},{3,2},{4,5},{5,4},{6,7},{7,6},{8,9},{9,8},{10,11... | collective-permute-start | bytes 37052 | tf_op jit(solution)/shard_map/ppermute | solution.py:462
  26.3 4.2 %collective-permute-start.11 = (f32[9,343]{1,0:T(8,128)S(1)}, f32[9,343]{1,0:T(8,128)S(1)}, u32[]{:S(2)}, u32[]{:S(2)}) collective-permute-start(f32[9,343]{1,0:T(8,128)S(1)} %add.8.total_ref), channel_id=1, source_target_pairs={{0,7},{1,6},{2,5},{3,4},{4,3},{5,2},{6,1},{7,0},{8,15},{9,14},{10,... | collective-permute-start | bytes 37052 | tf_op jit(solution)/shard_map/ppermute | solution.py:462
  28.6 3.3 %collective-permute-start.10 = (f32[9,343]{1,0:T(8,128)S(1)}, f32[9,343]{1,0:T(8,128)S(1)}, u32[]{:S(2)}, u32[]{:S(2)}) collective-permute-start(f32[9,343]{1,0:T(8,128)S(1)} %add.8.total_ref), channel_id=1, source_target_pairs={{0,5},{1,4},{2,7},{3,6},{4,1},{5,0},{6,3},{7,2},{8,13},{9,12},{10,... | collective-permute-start | bytes 37052 | tf_op jit(solution)/shard_map/ppermute | solution.py:462
  29.0 3.3 %collective-permute-start.9 = (f32[9,343]{1,0:T(8,128)S(1)}, f32[9,343]{1,0:T(8,128)S(1)}, u32[]{:S(2)}, u32[]{:S(2)}) collective-permute-start(f32[9,343]{1,0:T(8,128)S(1)} %add.8.total_ref), channel_id=1, source_target_pairs={{0,3},{1,2},{2,1},{3,0},{4,7},{5,6},{6,5},{7,4},{8,11},{9,10},{10,... | collective-permute-start | bytes 37052 | tf_op jit(solution)/shard_map/ppermute | solution.py:462
  32.9 4.0 %collective-permute-start.12 = (f32[32,256]{1,0:T(8,128)S(1)}, f32[32,256]{1,0:T(8,128)S(1)}, u32[]{:S(2)}, u32[]{:S(2)}) collective-permute-start(f32[32,256]{1,0:T(8,128)S(1)} %get-tuple-element.91), channel_id=1, source_target_pairs={{0,8},{1,9},{2,10},{3,11},{4,12},{5,13},{6,14},{7,15},{8,0},{9,1},... | collective-permute-start | bytes 98312 | tf_op jit(solution)/shard_map/ppermute | solution.py:454
  35.0 1.9 %collective-permute-start.13 = (f32[32,256]{1,0:T(8,128)S(1)}, f32[32,256]{1,0:T(8,128)S(1)}, u32[]{:S(2)}, u32[]{:S(2)}) collective-permute-start(f32[32,256]{1,0:T(8,128)S(1)} %get-tuple-element.92), channel_id=1, source_target_pairs={{0,1},{1,0},{2,3},{3,2},{4,5},{5,4},{6,7},{7,6},{8,16},{9,17},{10,... | collective-permute-start | bytes 98312 | tf_op jit(solution)/shard_map/ppermute | solution.py:454
